TPU v7x, 512 devices: a whole 4x4x16 slice. The times are simulated.
512 devices in a mesh: ctx: 32 (over y, x, core), dp: 16 (over z).
Axes of the slice: x: 4, y: 4, z: 16, core: 2. Of those that a mesh axis runs over, the one named last changes fastest.
Arguments:
- inputs: bfloat16 [16, 4096, 4096], P('dp', 'ctx'), may hold values from -40 to 40
- grad_output: bfloat16 [16, 4096, 4096], P('dp', 'ctx'), may hold values from -6 to 6
- query_weight: bfloat16 [4096, 512], P('ctx'), may hold values from -1 to 1
- key_weight: bfloat16 [4096, 128], P('ctx'), may hold values from -1 to 1
- value_weight: bfloat16 [4096, 128], P('ctx'), may hold values from -0.09375 to 0.09375
- out_weight: bfloat16 [512, 4096], P(None, 'ctx'), may hold values from -0.25 to 0.25
- doc_lengths: int32 [16, 8], P('dp'), may hold values from 1 to 1024, 4096 in all within a row
- block_order: int32 [16, 64], P('dp'), may hold values from 0 to 63, each once within a row
Outputs:
- grad_input: bfloat16 [16, 4096, 4096], P('dp', 'ctx')
- grad_value_weight: float32 [4096, 128], P('ctx')
Inputs may be any that keep to these rules, and one draw needn't show every extreme that they name: `doc_lengths`: each row holds the lengths of the 8 documents of one sequence in order, summing to 4096. `block_order`: each row is a permutation of the 64 blocks of 64 positions.
All inputs are finite; a program needn't handle non-finite values.
Results may differ from a plain program's by a relative error of at most 0.029.
Values may be sent and summed in bfloat16 or wider, within the bound.
No kernel may reach another device: no remote copies, remote signals or barrier semaphores. Data moves between devices by JAX's collectives and lax.ppermute only.
A program may use at most 64 MiB of HBM per device.

v0:
```python
import math

import jax
import jax.numpy as jnp
from jax import lax
from jax.sharding import PartitionSpec as P

THETA = 500000.0
NEG = -1e30


def angles(positions, head_size):
    half_width = head_size // 2
    frequency = jnp.exp(
        -jnp.log(jnp.float32(THETA)) * (2.0 * jnp.arange(half_width, dtype=jnp.float32) / head_size)
    )
    phases = positions.astype(jnp.float32)[:, None] * frequency[None, :]
    return (jnp.cos(phases), jnp.sin(phases))


def rotate(vectors, cosine_table, sine_table):
    half_width = vectors.shape[-1] // 2
    first_half = vectors[..., :half_width]
    second_half = vectors[..., half_width:]
    return jnp.concatenate(
        [
            first_half * cosine_table - second_half * sine_table,
            second_half * cosine_table + first_half * sine_table,
        ],
        axis=-1,
    )


def layout(order, lengths, total_rows):
    block_width = total_rows // order.shape[0]
    positions = jnp.repeat(
        order * block_width, block_width, total_repeat_length=total_rows
    ) + jnp.tile(jnp.arange(block_width, dtype=jnp.int32), order.shape[0])
    doc_ends = jnp.cumsum(lengths)
    documents = jnp.sum((positions[:, None] >= doc_ends[None, :]).astype(jnp.int32), axis=1)
    return (positions, documents)


def on_device(
    inputs,
    grad_output,
    query_weight,
    key_weight,
    value_weight,
    out_weight,
    doc_lengths,
    block_order,
):
    tokens = inputs[0]
    upstream = grad_output[0]
    row_count, feature_count = tokens.shape
    ctx_size = lax.axis_size("ctx")
    total_rows = row_count * ctx_size
    ctx_index = lax.axis_index("ctx")
    head_size = key_weight.shape[1]
    head_count = query_weight.shape[1] // head_size
    scaling = head_size ** (-0.5)
    positions, documents = layout(block_order[0], doc_lengths[0], total_rows)
    local_positions = lax.dynamic_slice_in_dim(positions, ctx_index * row_count, row_count)
    local_documents = lax.dynamic_slice_in_dim(documents, ctx_index * row_count, row_count)
    cosine_table, sine_table = angles(local_positions, head_size)
    head_cosine = cosine_table[:, None, :]
    head_sine = sine_table[:, None, :]

    def mask_for(block_positions, block_documents):
        return (local_documents[:, None] == block_documents[None, :]) & (
            block_positions[None, :] <= local_positions[:, None]
        )

    full_query, full_key, full_value = (
        lax.all_gather(query_weight, "ctx", axis=0, tiled=True),
        lax.all_gather(key_weight, "ctx", axis=0, tiled=True),
        lax.all_gather(value_weight, "ctx", axis=0, tiled=True),
    )
    queries = rotate(
        jnp.dot(tokens, full_query, preferred_element_type=jnp.float32).reshape(
            row_count, head_count, head_size
        ),
        head_cosine,
        head_sine,
    ).astype(jnp.bfloat16)
    rotated_keys = rotate(
        jnp.dot(tokens, full_key, preferred_element_type=jnp.float32), cosine_table, sine_table
    ).astype(jnp.bfloat16)
    local_values = jnp.dot(tokens, full_value, preferred_element_type=jnp.float32).astype(
        jnp.bfloat16
    )
    all_keys, all_values = (
        lax.all_gather(rotated_keys, "ctx", axis=0, tiled=True),
        lax.all_gather(local_values, "ctx", axis=0, tiled=True),
    )
    block_rows = math.gcd(total_rows, 512)
    block_count = total_rows // block_rows
    blocks = (
        all_keys.reshape(block_count, block_rows, head_size),
        all_values.reshape(block_count, block_rows, head_size),
        positions.reshape(block_count, block_rows),
        documents.reshape(block_count, block_rows),
    )

    def scores_for(key_block):
        return (
            jnp.einsum("thd,kd->htk", queries, key_block, preferred_element_type=jnp.float32)
            * scaling
        )

    def first_pass(carried, current):
        key_block, value_block, block_positions, block_documents = current
        allowed = mask_for(block_positions, block_documents)
        running_max, running_sum = carried
        masked = jnp.where(allowed[None], scores_for(key_block), NEG)
        new_max = jnp.maximum(running_max, jnp.max(masked, axis=2))
        kept_terms = jnp.where(allowed[None], jnp.exp(masked - new_max[:, :, None]), 0.0)
        return (
            (new_max, running_sum * jnp.exp(running_max - new_max) + jnp.sum(kept_terms, axis=2)),
            None,
        )

    start_max = jnp.full((head_count, row_count), NEG, jnp.float32)
    (running_max, running_sum), unused = lax.scan(
        first_pass, (start_max, jnp.zeros_like(start_max)), blocks
    )
    log_total = running_max + jnp.log(running_sum)

    def weights_for(key_block, allowed):
        masked = jnp.where(allowed[None], scores_for(key_block), NEG)
        return jnp.where(allowed[None], jnp.exp(masked - log_total[:, :, None]), 0.0)

    def second_pass(carried, current):
        key_block, value_block, block_positions, block_documents = current
        allowed = mask_for(block_positions, block_documents)
        probabilities = weights_for(key_block, allowed).astype(jnp.bfloat16)
        return (
            carried
            + jnp.einsum(
                "htk,kd->thd", probabilities, value_block, preferred_element_type=jnp.float32
            ),
            None,
        )

    zero_query = jnp.zeros((row_count, head_count, head_size), jnp.float32)
    attention_sum, unused = lax.scan(second_pass, zero_query, blocks)
    attention = attention_sum.astype(jnp.bfloat16)
    columns = upstream
    attention_total = lax.dot_general(
        columns,
        lax.all_gather(out_weight, "ctx", axis=1, tiled=True),
        (((1,), (1,)), ((), ())),
        preferred_element_type=jnp.float32,
    )
    grad_attention = attention_total.astype(jnp.bfloat16).reshape(row_count, head_count, head_size)
    correction = jnp.einsum(
        "thd,thd->ht", grad_attention, attention, preferred_element_type=jnp.float32
    )

    def gradient_core(key_block, value_block, allowed):
        weights = weights_for(key_block, allowed)
        grad_prob = jnp.einsum(
            "thd,kd->htk", grad_attention, value_block, preferred_element_type=jnp.float32
        )
        grad_score = (weights * (grad_prob - correction[:, :, None]) * scaling).astype(jnp.bfloat16)
        return (weights.astype(jnp.bfloat16), grad_score)

    def query_term(key_block, grad_score):
        return jnp.einsum("htk,kd->thd", grad_score, key_block, preferred_element_type=jnp.float32)

    def pair_term(probabilities, grad_score):
        key_part = jnp.einsum(
            "htk,thd->kd", grad_score, queries, preferred_element_type=jnp.float32
        )
        value_part = jnp.einsum(
            "htk,thd->kd", probabilities, grad_attention, preferred_element_type=jnp.float32
        )
        return jnp.concatenate([key_part, value_part], axis=1)

    def third_pass(carried, current):
        key_block, value_block, block_positions, block_documents = current
        allowed = mask_for(block_positions, block_documents)
        probabilities, grad_score = gradient_core(key_block, value_block, allowed)
        query_part = query_term(key_block, grad_score)
        pair_part = pair_term(probabilities, grad_score)
        return (carried + query_part, pair_part)

    grad_query_rot, pair_terms = lax.scan(third_pass, zero_query, blocks)
    pair_sum = lax.psum_scatter(
        pair_terms.reshape(total_rows, 2 * head_size).astype(jnp.bfloat16),
        "ctx",
        scatter_dimension=0,
        tiled=True,
    ).astype(jnp.float32)
    grad_query = (
        rotate(grad_query_rot, head_cosine, -head_sine)
        .astype(jnp.bfloat16)
        .reshape(row_count, head_count * head_size)
    )
    grad_key = rotate(pair_sum[:, :head_size], cosine_table, -sine_table).astype(jnp.bfloat16)
    grad_value = pair_sum[:, head_size:].astype(jnp.bfloat16)
    contract_last = (((1,), (1,)), ((), ()))
    grad_input = (
        lax.dot_general(grad_query, full_query, contract_last, preferred_element_type=jnp.float32)
        + lax.dot_general(grad_key, full_key, contract_last, preferred_element_type=jnp.float32)
        + lax.dot_general(grad_value, full_value, contract_last, preferred_element_type=jnp.float32)
    ).astype(jnp.bfloat16)
    columns = tokens
    shard_rows = lax.psum_scatter(
        lax.dot_general(
            columns, grad_value, (((0,), (0,)), ((), ())), preferred_element_type=jnp.float32
        ).astype(jnp.bfloat16),
        "ctx",
        scatter_dimension=0,
        tiled=True,
    )
    grad_weight = lax.psum(shard_rows, "dp").astype(jnp.float32)
    return (grad_input[None], grad_weight)


def solution(mesh):
    placed = (
        P("dp", "ctx", None),
        P("dp", "ctx", None),
        P("ctx", None),
        P("ctx", None),
        P("ctx", None),
        P(None, "ctx"),
        P("dp", None),
        P("dp", None),
    )
    return jax.shard_map(
        on_device,
        mesh=mesh,
        in_specs=placed,
        out_specs=(P("dp", "ctx", None), P("ctx", None)),
        check_vma=False,
    )
```

profile of v0, /device:TPU:2, one launch (start us, length us, event | category | flops | bytes accessed | tf_op | source)
XLA Modules:
  0.0 720.0 jit_solution(3899706086460372605)
XLA Ops:
  13.1 4.3 compare_select_fusion.1
  17.5 2.9 compare_reduce_fusion.56
  20.4 36.6 %select_add_fusion = (s32[4096]{0:T(1024)S(1)}, s32[4096]{0:T(1024)S(1)}) fusion(s32[4096]{0:T(1024)S(1)} %tile.16, s32[32,128]{1,0:T(8,128)} %constant.170.clone.1, s32[32]{0:T(128)S(1)} %iota_multiply_fusion, pred[4096]{0:T(1024)(128)(4,1)S(1)} %get-tuple-element.450, pred[4096]{0:T(1024)(128)(4,1)S(1)} %get-tuple-element.449, ...), kind=kLoop, calls=%fused_computation.184 | loop fusion | flops 274432 | bytes 315748 | tf_op jit(solution)/shard_map/add | solution.py:36
  57.0 16.4 %all-gather.7.cloned.1.call-done = bf16[4096,128]{1,0:T(8,128)(2,1)} async-done(((bf16[128,128]{1,0:T(8,128)(2,1)}), bf16[4096,128]{1,0:T(8,128)(2,1)}) %all-gather.7.cloned.1.call-update) | async-done | bytes 1048592 | tf_op jit(solution)/shard_map/all_gather | solution.py:77
  73.4 1.7 fusion.60
  77.7 56.4 %all-gather.13.cloned.1.call-done = bf16[4096,128]{1,0:T(8,128)(2,1)} async-done(((bf16[128,128]{1,0:T(8,128)(2,1)}), bf16[4096,128]{1,0:T(8,128)(2,1)}) %all-gather.13.cloned.1.call-update) | async-done | bytes 1048592 | tf_op jit(solution)/shard_map/all_gather | solution.py:78
  134.1 2.3 convolution_convert_fusion.2
  136.4 59.0 %all-gather.9.cloned.1.call-done = bf16[4096,128]{0,1:T(8,128)(2,1)} async-done(((bf16[128,128]{0,1:T(8,128)(2,1)}), bf16[4096,128]{0,1:T(8,128)(2,1)}) %all-gather.9.cloned.1.call-update) | async-done | bytes 1048592 | tf_op jit(solution)/shard_map/all_gather | solution.py:94
  195.5 2.3 copy.77
  197.7 61.6 %all-gather.11.cloned.1.call-done = bf16[4096,512]{1,0:T(8,128)(2,1)} async-done(((bf16[128,512]{1,0:T(8,128)(2,1)}), bf16[4096,512]{1,0:T(8,128)(2,1)}) %all-gather.11.cloned.1.call-update) | async-done | bytes 4194320 | tf_op jit(solution)/shard_map/all_gather | solution.py:76
  259.4 6.4 copy.49
  265.8 3.4 fusion.56
  269.4 13.8 %while.38 = (s32[]{:T(128)}, f32[4,128]{1,0:T(4,128)S(1)}, f32[4,128]{1,0:T(4,128)S(1)}, s32[128]{0:T(128)S(1)}, s32[8,512]{1,0:T(8,128)S(1)}, /*index=5*/s32[8,...) while((s32[]{:T(128)}, f32[4,128]{1,0:T(4,128)S(1)}, ...), condition=%wide.region_5.6_spmd.clone, body=%wide.region_2.5_spmd.clone.sunk | while | flops 68880896 | bytes 2596476 | solution.py:125
  283.2 43.1 %all-gather.17.cloned.1.call-done = bf16[512,4096]{1,0:T(8,128)(2,1)} async-done(((bf16[512,128]{1,0:T(8,128)(2,1)}), bf16[512,4096]{1,0:T(8,128)(2,1)}) %all-gather.17.cloned.1.call-update) | async-done | bytes 4194320 | tf_op jit(solution)/shard_map/all_gather | solution.py:152
  326.4 4.0 convolution_convert_fusion.1
  330.6 57.0 %all-gather.15.cloned.1.call-done = bf16[4096,128]{1,0:T(8,128)(2,1)} async-done(((bf16[128,128]{1,0:T(8,128)(2,1)}), bf16[4096,128]{1,0:T(8,128)(2,1)}) %all-gather.15.cloned.1.call-update) | async-done | bytes 1048592 | tf_op jit(solution)/shard_map/all_gather | solution.py:95
  387.7 14.5 %while.39 = (s32[]{:T(128)}, f32[128,4,128]{0,2,1:T(8,128)S(1)}, bf16[8,512,128]{2,1,0:T(8,128)(2,1)}, s32[128]{0:T(128)S(1)}, s32[8,512]{1,0:T(8,128)S(1)}, /*i...) while((s32[]{:T(128)}, f32[128,4,128]{0,2,1:T(8,128)S(1)}, ...), condition=%wide.region_7.8_spmd.clone, body=%wide.region_6.7_spmd.clone.sunk | while | flops 135856128 | bytes 1065091 | solution.py:147
  387.9 1.6 fusion.133
  389.7 1.6 fusion.133
  391.5 1.6 fusion.133
  393.3 1.6 fusion.133
  395.2 1.6 fusion.133
  397.0 1.6 fusion.133
  398.8 1.6 fusion.133
  400.6 1.6 fusion.133
  402.4 42.4 %while.40 = (s32[]{:T(128)}, f32[128,4,128]{0,2,1:T(8,128)S(1)}, bf16[8,512,256]{1,2,0:T(8,128)(2,1)}, bf16[8,512,128]{2,1,0:T(8,128)(2,1)}, s32[128]{0:T(128)S(...) while((s32[]{:T(128)}, f32[128,4,128]{0,2,1:T(8,128)S(1)}, ...), condition=%wide.region_9.10_spmd.clone, body=%wide.region_8.9_spmd.clone.sunk | while | flops 338755584 | bytes 7097499 | solution.py:189
  444.8 3.9 copy.78
  449.0 101.3 %reduce-scatter.7.cloned.1.call-done = bf16[128,256]{1,0:T(8,128)(2,1)} async-done(((bf16[4096,256]{1,0:T(8,128)(2,1)}), bf16[128,256]{1,0:T(8,128)(2,1)}) %reduce-scatter.7.cloned.1.call-update) | async-done | bytes 65552
  553.3 3.8 fusion.89
  558.3 1.4 fusion.54
  559.7 95.0 %reduce-scatter.9.cloned.1.call-done = bf16[128,128]{1,0:T(8,128)(2,1)} async-done(((bf16[4096,128]{1,0:T(8,128)(2,1)}), bf16[128,128]{1,0:T(8,128)(2,1)}) %reduce-scatter.9.cloned.1.call-update) | async-done | bytes 32784
  655.6 56.9 %psum.7 = bf16[128,128]{0,1:T(8,128)(2,1)S(1)} all-reduce(bf16[128,128]{0,1:T(8,128)(2,1)S(1)} %copy.76), channel_id=1, replica_groups=mesh['ctx'=32,'dp'=16] {'dp'}, use_global_device_ids=true, to_apply=%region_12.13 | all-reduce | flops 16384 | bytes 65536 | tf_op jit(solution)/shard_map/psum | solution.py:218
  (205 shorter events, 72.0 us)
Async XLA Ops:
  7.2 66.2 %copy-start = (bf16[1,128,4096]{2,1,0:T(8,128)(2,1)S(1)}, bf16[1,128,4096]{2,1,0:T(8,128)(2,1)}, u32[]{:S(2)}) copy-start(bf16[1,128,4096]{2,1,0:T(8,128)(2,1)} %param.16) | copy-start | bytes 3145732
  7.2 70.1 %copy-start.3 = (s32[1,8]{1,0:T(1,128)S(1)}, s32[1,8]{1,0:T(1,128)}, u32[]{:S(2)}) copy-start(s32[1,8]{1,0:T(1,128)} %param.22) | copy-start | bytes 100
  7.2 66.2 %all-gather.7.cloned.1.call-start = ((), (), s32[]{:S(2)}) async-start(), calls=%async_computation.2 | async-start | bytes 1081344 | tf_op jit(solution)/shard_map/all_gather | solution.py:77
  7.9 126.2 %all-gather.13.cloned.1.call-start = ((), (), s32[]{:S(2)}) async-start(), calls=%async_computation.5 | async-start | bytes 1081344 | tf_op jit(solution)/shard_map/all_gather | solution.py:78
  8.7 186.8 %all-gather.9.cloned.1.call-start = ((), (), s32[]{:S(2)}) async-start(), calls=%async_computation.3 | async-start | bytes 1081344 | tf_op jit(solution)/shard_map/all_gather | solution.py:94
  76.0 183.4 %all-gather.11.cloned.1.call-start = ((), (), s32[]{:S(2)}) async-start(), calls=%async_computation.4 | async-start | bytes 4325376 | tf_op jit(solution)/shard_map/all_gather | solution.py:76
  76.6 249.8 %all-gather.17.cloned.1.call-start = ((), (), s32[]{:S(2)}) async-start(), calls=%async_computation.7 | async-start | bytes 4325376 | tf_op jit(solution)/shard_map/all_gather | solution.py:152
  77.2 310.5 %all-gather.15.cloned.1.call-start = ((), (), s32[]{:S(2)}) async-start(), calls=%async_computation.6 | async-start | bytes 1081344 | tf_op jit(solution)/shard_map/all_gather | solution.py:95
  136.4 413.8 %reduce-scatter.7.cloned.1.call-start = ((), (), s32[]{:S(2)}) async-start(), calls=%async_computation.8 | async-start | bytes 2162688
  448.7 206.0 %reduce-scatter.9.cloned.1.call-start = ((), (), s32[]{:S(2)}) async-start(), calls=%async_computation.9 | async-start | bytes 1081344
  553.3 3.8 copy-start.1
  557.1 1.2 copy-start.2
Sparse Core Ops, SparseCore 0:
  11.2 62.2 all-gather.6
  76.5 57.5 all-gather.12
  137.7 57.7 all-gather.8
  198.5 60.8 all-gather.10
  262.3 64.0 all-gather.16
  329.9 57.6 all-gather.14
  448.8 101.3 reduce-scatter.6
  554.6 100.0 reduce-scatter.8
where the time goes:
time: 722 us; the launch traced here: 720 us
  waiting for transfers between devices  492 us (68%)
  matrix products  74.2 us (10%)
  other arithmetic  59.4 us (8%)
  blocking collectives  56.9 us (8%)
  local copies, waits for them, and re-layouts  21 us (3%)
  between operations  14.4 us (2%)
    unnamed x10, waiting for transfers between devices  199 us
    all_gather x1, waiting for transfers between devices, on_device(): lax.all_gather(query_weight, 'ctx', axis=0, tiled=True)  61.6 us
    all_gather x1, waiting for transfers between devices, on_device(): lax.all_gather(rotated_keys, 'ctx', axis=0, tiled=True)  59 us
    all_gather x1, waiting for transfers between devices, on_device(): lax.all_gather(local_values, 'ctx', axis=0, tiled=True)  57 us
    psum x1, blocking collectives, on_device(): grad_weight = lax.psum(shard_rows, 'dp').astype(jnp.float32)  56.9 us
    all_gather x1, waiting for transfers between devices, on_device(): lax.all_gather(value_weight, 'ctx', axis=0, tiled=True)  56.4 us
    all_gather x1, waiting for transfers between devices, on_device(): lax.all_gather(out_weight, 'ctx', axis=1, tiled=True)  43.1 us
    add x2, other arithmetic, layout(): jnp.repeat(order * block_width, block_width, total_repeat_length=total_rows)  36.6 us
  transfers between devices with their start and end apart: 8, of which 8 were waited for; matrix products, arithmetic and copies ran while one was open for 12% of the time, Pallas kernels for 0%

commit v1 on v0

v1 whole, which is shorter than its diff:
```python
import math

import jax
import jax.numpy as jnp
from jax import lax
from jax.experimental import pallas as pl
from jax.experimental.pallas import tpu as pltpu
from jax.sharding import PartitionSpec as P

THETA = 500000.0
NEG = -1e30
BLOCK = 64
LONGEST = 1024
BF16 = jnp.bfloat16
F32 = jnp.float32
NT = (((1,), (1,)), ((), ()))
TN = (((0,), (0,)), ((), ()))
NN = (((1,), (0,)), ((), ()))
VMEM = pl.BlockSpec(memory_space=pltpu.VMEM)
SMEM = pl.BlockSpec(memory_space=pltpu.SMEM)


def call(body, outs, in_specs, args, flops, scratch=(), limit=48):
    moved = sum(math.prod(a.shape) * a.dtype.itemsize for a in list(args) + list(outs))
    return pl.pallas_call(
        body,
        out_shape=outs,
        in_specs=in_specs,
        out_specs=[VMEM] * len(outs),
        scratch_shapes=list(scratch),
        compiler_params=pltpu.CompilerParams(vmem_limit_bytes=limit << 20),
        cost_estimate=pl.CostEstimate(flops=flops, bytes_accessed=moved, transcendentals=0),
    )(*args)


def shape(dims, dtype=BF16):
    return jax.ShapeDtypeStruct(dims, dtype)


def tables(block_numbers, head_size):
    half = head_size // 2
    frequency = jnp.exp(-jnp.log(jnp.float32(THETA)) * (2.0 * jnp.arange(half, dtype=F32) / head_size))
    places = (block_numbers[:, None] * BLOCK + jnp.arange(BLOCK, dtype=jnp.int32)[None, :]).reshape(-1)
    phases = places.astype(F32)[:, None] * frequency[None, :]
    cosine, sine = jnp.cos(phases), jnp.sin(phases)
    return jnp.concatenate([cosine, cosine], 1), jnp.concatenate([-sine, sine], 1)


def swap_halves(v):
    return pltpu.roll(v, v.shape[-1] // 2, axis=1)


def project_kernel(tokens, weight, cosine, sine, out):
    v = lax.dot_general(tokens[...], weight[...], NN, preferred_element_type=F32)
    v = (v * cosine[...] + swap_halves(v) * sine[...]).astype(BF16)
    for chip in range(out.shape[0]):
        out[chip] = v


def attention_kernel(place, order, lengths, tokens, upstream, weights, keys_values, cosine, sine,
                     grad_query, kept, sent, q_ref, a_ref, key_window, value_window, total, stored_at):
    rows, features = tokens.shape
    head = cosine.shape[1]
    heads = q_ref.shape[1] // head
    seq = keys_values.shape[1]
    blocks = seq // BLOCK
    span = key_window.shape[0] // BLOCK
    scaling = head ** (-0.5)
    own = place[0]
    own_core = own % 2

    def invert(i, carry):
        stored_at[order[0, i]] = i
        return carry

    lax.fori_loop(0, blocks, invert, 0)
    width = heads * head
    queries = lax.dot_general(tokens[...], weights[:, :width], NN, preferred_element_type=F32)
    c, s = cosine[...], sine[...]
    for h in range(heads):
        v = queries[:, h * head:(h + 1) * head]
        q_ref[:, h * head:(h + 1) * head] = (v * c + swap_halves(v) * s).astype(BF16)
    a_ref[...] = lax.dot_general(upstream[...], weights[:, width:], NN, preferred_element_type=F32).astype(BF16)
    total[...] = jnp.zeros_like(total)

    def destination(kb):
        spot = stored_at[jnp.maximum(kb, 0)]
        device = spot // 2
        away = jnp.where(device % 2 == own_core, 0, seq // 2)
        return pl.multiple_of(away + (device // 2) * (2 * BLOCK) + (spot % 2) * BLOCK, BLOCK)

    for j in range(rows // BLOCK):
        r0 = j * BLOCK
        block = order[0, own * (rows // BLOCK) + j]
        first = block - (span - 1)
        for w in range(span):
            source = pl.multiple_of(stored_at[jnp.maximum(first + w, 0)] * BLOCK, BLOCK)
            key_window[w * BLOCK:(w + 1) * BLOCK, :] = keys_values[0, pl.ds(source, BLOCK), :]
            value_window[w * BLOCK:(w + 1) * BLOCK, :] = keys_values[1, pl.ds(source, BLOCK), :]
        q = jnp.concatenate([q_ref[r0:r0 + BLOCK, h * head:(h + 1) * head] for h in range(heads)], 0)
        a = jnp.concatenate([a_ref[r0:r0 + BLOCK, h * head:(h + 1) * head] for h in range(heads)], 0)
        lane = lax.broadcasted_iota(jnp.int32, (1, heads * BLOCK), 1)
        query_place = block * BLOCK + lane % BLOCK
        start = jnp.zeros_like(query_place)
        end = jnp.int32(0)
        for d in range(lengths.shape[1]):
            end = end + lengths[0, d]
            start = jnp.where(query_place >= end, end, start)
        key_place = first * BLOCK + lax.broadcasted_iota(jnp.int32, (span * BLOCK, heads * BLOCK), 0)
        allowed = (key_place >= start) & (key_place <= query_place)
        k, v = key_window[...], value_window[...]
        scores = lax.dot_general(k, q, NT, preferred_element_type=F32) * scaling
        scores = jnp.where(allowed, scores, NEG)
        e = jnp.exp(scores - jnp.max(scores, axis=0, keepdims=True))
        weight = e * (1.0 / jnp.sum(e, axis=0, keepdims=True))
        probability = weight.astype(BF16)
        grad_probability = lax.dot_general(v, a, NT, preferred_element_type=F32)
        correction = jnp.sum(probability.astype(F32) * grad_probability, axis=0, keepdims=True)
        grad_score = (weight * (grad_probability - correction) * scaling).astype(BF16)
        key_part = lax.dot_general(grad_score, q, NN, preferred_element_type=F32)
        value_part = lax.dot_general(probability, a, NN, preferred_element_type=F32)
        for w in range(span):
            to = destination(first + w)
            total[pl.ds(to, BLOCK), :head] += key_part[w * BLOCK:(w + 1) * BLOCK]
            total[pl.ds(to, BLOCK), head:] += value_part[w * BLOCK:(w + 1) * BLOCK]
        g = lax.dot_general(k, grad_score, TN, preferred_element_type=F32).T
        for h in range(heads):
            u = g[h * BLOCK:(h + 1) * BLOCK]
            u = u * c[r0:r0 + BLOCK] - swap_halves(u) * s[r0:r0 + BLOCK]
            grad_query[r0:r0 + BLOCK, h * head:(h + 1) * head] = u.astype(BF16)
    half = seq // 2
    kept[...] = total[:half].astype(BF16)
    sent[...] = total[half:].astype(BF16)


def owner_kernel(place, pieces, tokens, cosine, sine, grad_key_value, kept, sent):
    head = cosine.shape[1]
    total = jnp.sum(pieces[...].astype(F32), axis=0)
    u = total[:, :head]
    grad_key_value[:, :head] = (u * cosine[...] - swap_halves(u) * sine[...]).astype(BF16)
    grad_value = total[:, head:].astype(BF16)
    grad_key_value[:, head:] = grad_value
    rows = tokens.shape[0]
    own_core = place[0] % 2
    for chip in range(tokens.shape[1] // (2 * rows)):
        for away in range(2):
            core = jnp.where(own_core == away, 0, 1)
            columns = pl.ds(pl.multiple_of((2 * chip + core) * rows, rows), rows)
            part = lax.dot_general(tokens[:, columns], grad_value, TN, preferred_element_type=F32)
            (sent if away else kept)[chip * rows:(chip + 1) * rows, :] = part.astype(BF16)


def input_kernel(grad_query, grad_key_value, query_weight, other_weight, out):
    width = grad_query.shape[1]
    out[...] = (
        lax.dot_general(grad_query[...], query_weight[:, :width], NT, preferred_element_type=F32)
        + lax.dot_general(grad_key_value[:, :width // 4], other_weight[0], NT, preferred_element_type=F32)
        + lax.dot_general(grad_key_value[:, width // 4:], other_weight[1], NT, preferred_element_type=F32)
    ).astype(BF16)


def on_device(inputs, grad_output, query_weight, key_weight, value_weight, out_weight, doc_lengths, block_order):
    tokens, upstream = inputs[0], grad_output[0]
    rows, features = tokens.shape
    ctx, dp = lax.axis_size("ctx"), lax.axis_size("dp")
    chips = ctx // 2
    seq = rows * ctx
    me = lax.axis_index("ctx")
    core = me % 2
    head = key_weight.shape[1]
    width = query_weight.shape[1]
    heads = width // head
    cores = [[2 * i, 2 * i + 1] for i in range(chips)]
    planes = [[2 * i + c for i in range(chips)] for c in range(2)]
    other = [(i, i ^ 1) for i in range(ctx)]
    place = me.astype(jnp.int32).reshape(1)

    def to_chips(pieces):
        return lax.all_to_all(pieces, "ctx", 0, 0, tiled=True, axis_index_groups=planes)

    packed = jnp.concatenate([query_weight, out_weight.T], axis=1)
    big_weights = lax.all_gather(packed, "ctx", axis=0, tiled=True)

    chip_blocks = lax.dynamic_slice_in_dim(block_order[0], (me // 2) * 4, 4)
    chip_cosine, chip_sine = tables(chip_blocks, head)
    cosine = lax.dynamic_slice_in_dim(chip_cosine, core * rows, rows)
    sine = lax.dynamic_slice_in_dim(chip_sine, core * rows, rows)
    is_key = core == 0
    own_cosine = jnp.where(is_key, chip_cosine, 1.0)
    own_sine = jnp.where(is_key, chip_sine, 0.0)

    chip_tokens = lax.all_gather(tokens, "ctx", axis=0, tiled=True, axis_index_groups=cores)
    both = lax.all_gather(jnp.stack([key_weight, value_weight]), "ctx", axis=1, tiled=True, axis_index_groups=cores)
    mine = lax.dynamic_index_in_dim(both, core, 0, keepdims=False)
    own_weight = to_chips(jnp.broadcast_to(mine[None], (chips,) + mine.shape)).reshape(features, head)
    (projected,) = call(
        project_kernel, [shape((chips, 2 * rows, head))], [VMEM] * 4,
        (chip_tokens, own_weight, own_cosine, own_sine), 4 * rows * features * head)
    own_part = to_chips(projected).reshape(1, seq, head)
    keys_values = lax.all_gather(own_part, "ctx", axis=0, tiled=True, axis_index_groups=cores)
    other_weight = lax.all_gather(own_weight[None], "ctx", axis=0, tiled=True, axis_index_groups=cores)

    window = LONGEST + 2 * BLOCK
    grad_query, kept, sent = call(
        attention_kernel,
        [shape((rows, width)), shape((seq // 2, 2 * head)), shape((seq // 2, 2 * head))],
        [SMEM] * 3 + [VMEM] * 6,
        (place, block_order, doc_lengths, tokens, upstream, big_weights, keys_values, cosine, sine),
        4 * rows * features * width + 20 * rows * heads * window * head,
        scratch=[pltpu.VMEM((rows, width), BF16), pltpu.VMEM((rows, width), BF16),
                 pltpu.VMEM((window, head), BF16), pltpu.VMEM((window, head), BF16),
                 pltpu.VMEM((seq, 2 * head), F32), pltpu.SMEM((seq // BLOCK,), jnp.int32)])
    pairs = (kept.astype(F32) + lax.ppermute(sent, "ctx", other).astype(F32)).astype(BF16)
    pieces = to_chips(pairs).reshape(chips, rows, 2 * head)
    grad_key_value, kept, sent = call(
        owner_kernel,
        [shape((rows, 2 * head)), shape((features // 2, head)), shape((features // 2, head))],
        [SMEM] + [VMEM] * 4, (place, pieces, tokens, cosine, sine), 2 * rows * features * head)
    received = lax.ppermute(sent, "ctx", other)
    (grad_input,) = call(
        input_kernel, [shape((rows, features))], [VMEM] * 4,
        (grad_query, grad_key_value, big_weights, other_weight), 2 * rows * features * (width + 2 * head))
    parts = (kept.astype(F32) + received.astype(F32)).astype(BF16)
    shard = jnp.sum(to_chips(parts).reshape(chips, rows, head).astype(F32), axis=0).astype(BF16)
    slices = lax.all_to_all(shard, "dp", 0, 0, tiled=True).reshape(dp, rows // dp, head)
    own_slice = jnp.sum(slices.astype(F32), axis=0)
    grad_weight = lax.all_to_all(
        jnp.broadcast_to(own_slice[None], (dp,) + own_slice.shape), "dp", 0, 0, tiled=True).reshape(rows, head)
    return grad_input[None], grad_weight


def solution(mesh):
    placed = (
        P("dp", "ctx", None),
        P("dp", "ctx", None),
        P("ctx", None),
        P("ctx", None),
        P("ctx", None),
        P(None, "ctx"),
        P("dp", None),
        P("dp", None),
    )
    return jax.shard_map(
        on_device,
        mesh=mesh,
        in_specs=placed,
        out_specs=(P("dp", "ctx", None), P("ctx", None)),
        check_vma=False,
    )
```

time: 722 us -> 262 us (0.36)
  the two profiles are of different devices: /device:TPU:2 before, /device:TPU:1 now
where the time goes in v1:
time: 262 us; the launch traced here: 259 us
  waiting for transfers between devices  133 us (51%)
  blocking collectives  65.4 us (25%)
  starting transfers between devices  18.2 us (7%)
  Pallas kernels  17.2 us (7%)
  between operations  14 us (5%)
  local copies, waits for them, and re-layouts  6.24 us (2%)
  other arithmetic  4.87 us (2%)
    all_gather x1, waiting for transfers between devices, on_device(): big_weights = lax.all_gather(packed, 'ctx', axis=0, tiled=True)  72.3 us
    all_to_all x2, blocking collectives, to_chips(): lax.all_to_all(pieces, 'ctx', 0, 0, tiled=True, axis_index_groups=planes)  33.8 us
    all_to_all x2, waiting for transfers between devices, to_chips(): lax.all_to_all(pieces, 'ctx', 0, 0, tiled=True, axis_index_groups=planes)  32 us
    all_to_all x1, blocking collectives, on_device(): lax.all_to_all(shard, 'dp', 0, 0, tiled=True).reshape(dp, rows // dp, head)  23.2 us
    all_gather x1, waiting for transfers between devices, on_device(): lax.all_gather(own_part, 'ctx', axis=0, tiled=True, axis_index_groups=cores)  20 us
    pallas_call x4, Pallas kernels, call(): pl.pallas_call(body, out_shape=outs, in_specs=in_specs, out_specs=[VMEM]...  17.2 us
    all_to_all x2, starting transfers between devices, to_chips(): lax.all_to_all(pieces, 'ctx', 0, 0, tiled=True, axis_index_groups=planes)  8.56 us
    all_gather x1, blocking collectives, on_device(): lax.all_gather(jnp.stack([key_weight, value_weight]), 'ctx', axis=1, tile...  8.41 us
  transfers between devices with their start and end apart: 9, of which 7 were waited for; matrix products, arithmetic and copies ran while one was open for 2% of the time, Pallas kernels for 3%

profile of v1, /device:TPU:1, one launch (start us, length us, event | category | flops | bytes accessed | tf_op | source)
XLA Modules:
  0.0 259.0 jit_solution(8395906910829569366)
XLA Ops:
  7.2 0.7 all-gather.12.cloned.1.call-update
  7.9 0.8 pad_maximum_fusion.1
  8.7 8.4 %all_gather.17 = bf16[2,256,128]{2,1,0:T(8,128)(2,1)S(1)} all-gather(bf16[2,128,128]{2,1,0:T(8,128)(2,1)S(1)} %pad_maximum_fusion.1), channel_id=1, replica_groups={{0,16},{32,48},{64,80},{96,112},{128,144},{160,176},{192,208},{224,240}..., dimensions={1}, use_global_device_ids=true | all-gather | bytes 196608 | tf_op jit(solution)/shard_map/all_gather | solution.py:193
  17.1 1.2 broadcast_in_dim.29
  18.3 3.7 %all-to-all-start = ((bf16[16,256,128]{2,1,0:T(8,128)(2,1)}), bf16[16,256,128]{2,1,0:T(8,128)(2,1)S(1)}, u32[]{:S(2)}, u32[]{:S(2)}) async-start(bf16[16,256,128]{2,1,0:T(8,128)(2,1)} %broadcast_in_dim.29), calls=%async_computation | async-start | bytes 2097152 | tf_op jit(solution)/shard_map/all_to_all | solution.py:179
  22.3 0.5 fusion.2
  23.0 16.1 %all-to-all-done = bf16[16,256,128]{2,1,0:T(8,128)(2,1)S(1)} async-done(((bf16[16,256,128]{2,1,0:T(8,128)(2,1)}), bf16[16,256,128]{2,1,0:T(8,128)(2,1)S(1)}, u32[]{:S(2)}, u32[]{:S(2)}) %all-to-all-start) | async-done | bytes 1048608 | tf_op jit(solution)/shard_map/all_to_all | solution.py:179
  39.1 2.0 copy-done.2
  41.1 0.8 shard_map.95
  41.9 20.2 %all_to_all.42 = bf16[16,256,128]{2,1,0:T(8,128)(2,1)} all-to-all(bf16[16,256,128]{2,1,0:T(8,128)(2,1)S(1)} %shard_map.95), channel_id=1, replica_groups={{0,32,64,96,128,160,192,224,256,288,320,352,384,416,448,480},{16,48,80,..., dimensions={0} | all-to-all | bytes 2097152 | tf_op jit(solution)/shard_map/all_to_all | solution.py:179
  62.3 1.6 pad_maximum_fusion
  64.1 20.0 %all-gather.8.cloned.1.call-done.keys_values = bf16[2,4096,128]{2,1,0:T(8,128)(2,1)} async-done(((bf16[1,4096,128]{2,1,0:T(8,128)(2,1)}), bf16[2,4096,128]{2,1,0:T(8,128)(2,1)}) %all-gather.8.cloned.1.call-update) | async-done | bytes 2097168 | tf_op jit(solution)/shard_map/all_gather | solution.py:200
  84.1 72.3 %all-gather.6.cloned.1.call-done.weights.query_weight = bf16[4096,1024]{1,0:T(8,128)(2,1)} async-done(((bf16[128,1024]{1,0:T(8,128)(2,1)}), bf16[4096,1024]{1,0:T(8,128)(2,1)}) %all-gather.6.cloned.1.call-update) | async-done | bytes 8388624 | tf_op jit(solution)/shard_map/all_gather | solution.py:182
  156.4 9.4 %shard_map.96 = (bf16[128,512]{1,0:T(8,128)(2,1)S(1)}, bf16[2048,256]{1,0:T(8,128)(2,1)S(1)}, bf16[2048,256]{1,0:T(8,128)(2,1)S(1)}) custom-call(s32[1]{0:T(128)} %bitcast.place, s32[1,64]{1,0:T(1,128)S(1)} %copy-done.5, s32[1,8]{1,0:T(1,128)S(1)} %copy-done.6, bf16[128,4096]{1,0:T(8,128)(2,1)S(1)} %bitcast.19, bf16[128,4096]{1,0:T(8,128)(2,1)S(1)} %bitcast.24, ...), custom_call_target="tpu_custom_call" | custom-call | flops 2583691264 | bytes 14942500 | tf_op jit(solution)/shard_map/pallas_call | solution.py:25
  165.9 2.2 collective-permute-start
  168.0 2.4 collective-permute-done
  170.4 1.3 add_convert_fusion
  171.7 4.9 %all-to-all-start.2 = ((bf16[16,128,256]{2,1,0:T(8,128)(2,1)}), bf16[16,128,256]{2,1,0:T(8,128)(2,1)S(1)}, u32[]{:S(2)}, u32[]{:S(2)}) async-start(bf16[16,128,256]{2,1,0:T(8,128)(2,1)} %bitcast.11), calls=%async_computation.2 | async-start | bytes 2097152 | tf_op jit(solution)/shard_map/all_to_all | solution.py:179
  176.6 0.5 all-gather.10.cloned.1.call-update
  177.2 15.9 %all-to-all-done.2.pieces = bf16[16,128,256]{2,1,0:T(8,128)(2,1)S(1)} async-done(((bf16[16,128,256]{2,1,0:T(8,128)(2,1)}), bf16[16,128,256]{2,1,0:T(8,128)(2,1)S(1)}, u32[]{:S(2)}, u32[]{:S(2)}) %all-to-all-start.2) | async-done | bytes 1048608 | tf_op jit(solution)/shard_map/all_to_all | solution.py:179
  193.1 0.6 shard_map.97
  193.7 3.8 %collective-permute-start.1 = (bf16[2048,128]{1,0:T(8,128)(2,1)S(1)}, bf16[2048,128]{1,0:T(8,128)(2,1)S(1)}, u32[]{:S(2)}, u32[]{:S(2)}) collective-permute-start(bf16[2048,128]{1,0:T(8,128)(2,1)S(1)} %get-tuple-element.13), channel_id=1, source_target_pairs={{0,16},{16,0},{32,48},{48,32},{64,80},{80,64},{96,112},{112,96},{1... | collective-permute-start | bytes 1572872 | tf_op jit(solution)/shard_map/ppermute | solution.py:219
  197.5 1.5 collective-permute-done.1
  199.0 0.1 add_convert_fusion.1
  199.1 13.6 %all_to_all.43 = bf16[16,128,128]{2,1,0:T(8,128)(2,1)S(1)} all-to-all(bf16[16,128,128]{2,1,0:T(8,128)(2,1)S(1)} %bitcast.26), channel_id=1, replica_groups={{0,32,64,96,128,160,192,224,256,288,320,352,384,416,448,480},{16,48,80,..., dimensions={0} | all-to-all | bytes 1048576 | tf_op jit(solution)/shard_map/all_to_all | solution.py:179
  212.8 23.2 %all_to_all.44 = bf16[16,8,128]{2,1,0:T(8,128)(2,1)S(1)} all-to-all(bf16[16,8,128]{2,1,0:T(8,128)(2,1)S(1)} %bitcast.30), channel_id=1, replica_groups=mesh['ctx'=32,'dp'=16] {'dp'}, dimensions={0} | all-to-all | bytes 65536 | tf_op jit(solution)/shard_map/all_to_all | solution.py:225
  236.1 0.6 broadcast_in_dim.33
  236.7 3.5 %all-to-all-start.5 = ((f32[16,8,128]{2,1,0:T(8,128)}), f32[16,8,128]{2,1,0:T(8,128)S(1)}, u32[]{:S(2)}, u32[]{:S(2)}) async-start(f32[16,8,128]{2,1,0:T(8,128)} %broadcast_in_dim.33), calls=%async_computation.5 | async-start | bytes 131072 | tf_op jit(solution)/shard_map/all_to_all | solution.py:227
  240.2 1.6 copy-done.3
  241.8 6.4 %shard_map.98 = bf16[128,4096]{1,0:T(8,128)(2,1)} custom-call(bf16[128,512]{1,0:T(8,128)(2,1)S(1)} %get-tuple-element.8.grad_query, bf16[128,256]{1,0:T(8,128)(2,1)S(1)} %get-tuple-element.11.grad_key_value, bf16[4096,1024]{1,0:T(8,128)(2,1)} %all-gather.6.cloned.1.call-done.weights.query_weight, bf16[2,4096,128]{2,1,0:T(8,128)(2,1)S(1)} %copy-done.3), custom_call_target="tpu_custom_call" | custom-call | flops 805306368 | bytes 11730944 | tf_op jit(solution)/shard_map/pallas_call | solution.py:25
  248.2 3.6 %all-to-all-done.5 = f32[16,8,128]{2,1,0:T(8,128)S(1)} async-done(((f32[16,8,128]{2,1,0:T(8,128)}), f32[16,8,128]{2,1,0:T(8,128)S(1)}, u32[]{:S(2)}, u32[]{:S(2)}) %all-to-all-start.5) | async-done | bytes 65568 | tf_op jit(solution)/shard_map/all_to_all | solution.py:227
  251.8 0.6 copy.14
  (36 shorter events, 1.0 us)
Async XLA Ops:
  7.2 31.9 %all-gather.12.cloned.1.call-start = ((), (), s32[]{:S(2)}) async-start(), calls=%async_computation.9 | async-start | bytes 3145728 | tf_op jit(solution)/shard_map/all_gather | solution.py:192
  7.9 14.1 %copy-start.5 = (s32[1,64]{1,0:T(1,128)S(1)}, s32[1,64]{1,0:T(1,128)}, u32[]{:S(2)}) copy-start(s32[1,64]{1,0:T(1,128)} %order.1) | copy-start | bytes 772
  18.3 20.8 %all-to-all-start = ((bf16[16,256,128]{2,1,0:T(8,128)(2,1)}), bf16[16,256,128]{2,1,0:T(8,128)(2,1)S(1)}, u32[]{:S(2)}, u32[]{:S(2)}) async-start(bf16[16,256,128]{2,1,0:T(8,128)(2,1)} %broadcast_in_dim.29), calls=%async_computation | async-start | bytes 2097152 | tf_op jit(solution)/shard_map/all_to_all | solution.py:179
  22.0 62.2 %all-gather.8.cloned.1.call-start = ((), (), s32[]{:S(2)}) async-start(), calls=%async_computation.7 | async-start | bytes 3145728 | tf_op jit(solution)/shard_map/all_gather | solution.py:200
  22.8 16.3 %copy-start.7 = (f32[256,64]{1,0:T(8,128)}, f32[256,64]{1,0:T(8,128)S(1)}, u32[]{:S(2)}) copy-start(f32[256,64]{1,0:T(8,128)S(1)} %get-tuple-element.16) | copy-start | bytes 196612
  39.1 2.8 %copy-start.1 = (bf16[16,256,128]{2,1,0:T(8,128)(2,1)}, bf16[16,256,128]{2,1,0:T(8,128)(2,1)S(1)}, u32[]{:S(2)}) copy-start(bf16[16,256,128]{2,1,0:T(8,128)(2,1)S(1)} %all-to-all-done) | copy-start | bytes 3145732
  39.1 2.0 copy-start.2
  41.9 20.3 %copy-start.9 = (bf16[512,128]{1,0:T(8,128)(2,1)S(1)}, bf16[512,128]{1,0:T(8,128)(2,1)}, u32[]{:S(2)}) copy-start(bf16[512,128]{1,0:T(8,128)(2,1)} %param.13) | copy-start | bytes 393220
  41.9 114.5 %copy-start = (bf16[1,128,4096]{2,1,0:T(8,128)(2,1)S(1)}, bf16[1,128,4096]{2,1,0:T(8,128)(2,1)}, u32[]{:S(2)}) copy-start(bf16[1,128,4096]{2,1,0:T(8,128)(2,1)} %param.8) | copy-start | bytes 3145732
  41.9 114.5 %copy-start.4 = (bf16[1,128,4096]{2,1,0:T(8,128)(2,1)S(1)}, bf16[1,128,4096]{2,1,0:T(8,128)(2,1)}, u32[]{:S(2)}) copy-start(bf16[1,128,4096]{2,1,0:T(8,128)(2,1)} %param.9) | copy-start | bytes 3145732
  41.9 114.5 %copy-start.6 = (s32[1,8]{1,0:T(1,128)S(1)}, s32[1,8]{1,0:T(1,128)}, u32[]{:S(2)}) copy-start(s32[1,8]{1,0:T(1,128)} %lengths.1) | copy-start | bytes 100
  62.1 1.9 copy-start.8
  62.2 94.2 %all-gather.6.cloned.1.call-start = ((), (), s32[]{:S(2)}) async-start(), calls=%async_computation.6 | async-start | bytes 8650752 | tf_op jit(solution)/shard_map/all_gather | solution.py:182
  165.9 4.6 %collective-permute-start = (bf16[2048,256]{1,0:T(8,128)(2,1)S(1)}, bf16[2048,256]{1,0:T(8,128)(2,1)S(1)}, u32[]{:S(2)}, u32[]{:S(2)}) collective-permute-start(bf16[2048,256]{1,0:T(8,128)(2,1)S(1)} %get-tuple-element.10), channel_id=1, source_target_pairs={{0,16},{16,0},{32,48},{48,32},{64,80},{80,64},{96,112},{112,96},{1... | collective-permute-start | bytes 3145736 | tf_op jit(solution)/shard_map/ppermute | solution.py:213
  171.7 21.4 %all-to-all-start.2 = ((bf16[16,128,256]{2,1,0:T(8,128)(2,1)}), bf16[16,128,256]{2,1,0:T(8,128)(2,1)S(1)}, u32[]{:S(2)}, u32[]{:S(2)}) async-start(bf16[16,128,256]{2,1,0:T(8,128)(2,1)} %bitcast.11), calls=%async_computation.2 | async-start | bytes 2097152 | tf_op jit(solution)/shard_map/all_to_all | solution.py:179
  176.6 63.6 %all-gather.10.cloned.1.call-start = ((), (), s32[]{:S(2)}) async-start(), calls=%async_computation.8 | async-start | bytes 3145728 | tf_op jit(solution)/shard_map/all_gather | solution.py:201
  193.7 5.3 %collective-permute-start.1 = (bf16[2048,128]{1,0:T(8,128)(2,1)S(1)}, bf16[2048,128]{1,0:T(8,128)(2,1)S(1)}, u32[]{:S(2)}, u32[]{:S(2)}) collective-permute-start(bf16[2048,128]{1,0:T(8,128)(2,1)S(1)} %get-tuple-element.13), channel_id=1, source_target_pairs={{0,16},{16,0},{32,48},{48,32},{64,80},{80,64},{96,112},{112,96},{1... | collective-permute-start | bytes 1572872 | tf_op jit(solution)/shard_map/ppermute | solution.py:219
  236.7 15.1 %all-to-all-start.5 = ((f32[16,8,128]{2,1,0:T(8,128)}), f32[16,8,128]{2,1,0:T(8,128)S(1)}, u32[]{:S(2)}, u32[]{:S(2)}) async-start(f32[16,8,128]{2,1,0:T(8,128)} %broadcast_in_dim.33), calls=%async_computation.5 | async-start | bytes 131072 | tf_op jit(solution)/shard_map/all_to_all | solution.py:227
  240.2 1.6 copy-start.3
Sparse Core Ops, SparseCore 0:
  10.1 27.7 all-gather.11
  62.3 21.8 all-gather.7
  87.8 68.4 all-gather.5
  179.2 24.0 all-gather.9

commit v2 on v1

--- a/solution.py
+++ b/solution.py
@@ -50,19 +50,23 @@
     return pltpu.roll(v, v.shape[-1] // 2, axis=1)
 
 
-def project_kernel(tokens, weight, cosine, sine, out):
-    v = lax.dot_general(tokens[...], weight[...], NN, preferred_element_type=F32)
-    v = (v * cosine[...] + swap_halves(v) * sine[...]).astype(BF16)
-    for chip in range(out.shape[0]):
-        out[chip] = v
-
-
-def attention_kernel(place, order, lengths, tokens, upstream, weights, keys_values, cosine, sine,
+def project_kernel(place, tokens, other_tokens, weight, cosine, sine, out):
+    rows = tokens.shape[0]
+    own_core = place[0] % 2
+    for source, core in ((tokens, own_core), (other_tokens, 1 - own_core)):
+        here = pl.ds(pl.multiple_of(core * rows, rows), rows)
+        v = lax.dot_general(source[...], weight[...], NN, preferred_element_type=F32)
+        v = (v * cosine[here, :] + swap_halves(v) * sine[here, :]).astype(BF16)
+        for chip in range(out.shape[0]):
+            out[chip, here, :] = v
+
+
+def attention_kernel(place, order, lengths, tokens, upstream, weights, own_part, other_part, cosine, sine,
                      grad_query, kept, sent, q_ref, a_ref, key_window, value_window, total, stored_at):
     rows, features = tokens.shape
     head = cosine.shape[1]
     heads = q_ref.shape[1] // head
-    seq = keys_values.shape[1]
+    seq = own_part.shape[0]
     blocks = seq // BLOCK
     span = key_window.shape[0] // BLOCK
     scaling = head ** (-0.5)
@@ -95,8 +99,9 @@
         first = block - (span - 1)
         for w in range(span):
             source = pl.multiple_of(stored_at[jnp.maximum(first + w, 0)] * BLOCK, BLOCK)
-            key_window[w * BLOCK:(w + 1) * BLOCK, :] = keys_values[0, pl.ds(source, BLOCK), :]
-            value_window[w * BLOCK:(w + 1) * BLOCK, :] = keys_values[1, pl.ds(source, BLOCK), :]
+            first_half, second_half = own_part[pl.ds(source, BLOCK), :], other_part[pl.ds(source, BLOCK), :]
+            key_window[w * BLOCK:(w + 1) * BLOCK, :] = jnp.where(own_core == 0, first_half, second_half)
+            value_window[w * BLOCK:(w + 1) * BLOCK, :] = jnp.where(own_core == 0, second_half, first_half)
         q = jnp.concatenate([q_ref[r0:r0 + BLOCK, h * head:(h + 1) * head] for h in range(heads)], 0)
         a = jnp.concatenate([a_ref[r0:r0 + BLOCK, h * head:(h + 1) * head] for h in range(heads)], 0)
         lane = lax.broadcasted_iota(jnp.int32, (1, heads * BLOCK), 1)
@@ -150,12 +155,17 @@
             (sent if away else kept)[chip * rows:(chip + 1) * rows, :] = part.astype(BF16)
 
 
-def input_kernel(grad_query, grad_key_value, query_weight, other_weight, out):
+def input_kernel(place, grad_query, grad_key_value, query_weight, own_weight, other_weight, out):
     width = grad_query.shape[1]
+    head = own_weight.shape[1]
+    own_core = place[0] % 2
+    grad_key, grad_value = grad_key_value[:, :head], grad_key_value[:, head:]
+    own_grad = jnp.where(own_core == 0, grad_key, grad_value)
+    other_grad = jnp.where(own_core == 0, grad_value, grad_key)
     out[...] = (
         lax.dot_general(grad_query[...], query_weight[:, :width], NT, preferred_element_type=F32)
-        + lax.dot_general(grad_key_value[:, :width // 4], other_weight[0], NT, preferred_element_type=F32)
-        + lax.dot_general(grad_key_value[:, width // 4:], other_weight[1], NT, preferred_element_type=F32)
+        + lax.dot_general(own_grad, own_weight[...], NT, preferred_element_type=F32)
+        + lax.dot_general(other_grad, other_weight[...], NT, preferred_element_type=F32)
     ).astype(BF16)
 
 
@@ -170,7 +180,6 @@
     head = key_weight.shape[1]
     width = query_weight.shape[1]
     heads = width // head
-    cores = [[2 * i, 2 * i + 1] for i in range(chips)]
     planes = [[2 * i + c for i in range(chips)] for c in range(2)]
     other = [(i, i ^ 1) for i in range(ctx)]
     place = me.astype(jnp.int32).reshape(1)
@@ -189,37 +198,41 @@
     own_cosine = jnp.where(is_key, chip_cosine, 1.0)
     own_sine = jnp.where(is_key, chip_sine, 0.0)
 
-    chip_tokens = lax.all_gather(tokens, "ctx", axis=0, tiled=True, axis_index_groups=cores)
-    both = lax.all_gather(jnp.stack([key_weight, value_weight]), "ctx", axis=1, tiled=True, axis_index_groups=cores)
-    mine = lax.dynamic_index_in_dim(both, core, 0, keepdims=False)
-    own_weight = to_chips(jnp.broadcast_to(mine[None], (chips,) + mine.shape)).reshape(features, head)
+    def swap(v):
+        return lax.ppermute(v, "ctx", other)
+
+    mine = jnp.where(is_key, key_weight, value_weight)
+    theirs = swap(jnp.where(is_key, value_weight, key_weight))
+    chip_weight = jnp.concatenate([jnp.where(is_key, mine, theirs), jnp.where(is_key, theirs, mine)], axis=0)
+    own_weight = to_chips(
+        jnp.broadcast_to(chip_weight[None], (chips,) + chip_weight.shape)).reshape(features, head)
     (projected,) = call(
-        project_kernel, [shape((chips, 2 * rows, head))], [VMEM] * 4,
-        (chip_tokens, own_weight, own_cosine, own_sine), 4 * rows * features * head)
-    own_part = to_chips(projected).reshape(1, seq, head)
-    keys_values = lax.all_gather(own_part, "ctx", axis=0, tiled=True, axis_index_groups=cores)
-    other_weight = lax.all_gather(own_weight[None], "ctx", axis=0, tiled=True, axis_index_groups=cores)
+        project_kernel, [shape((chips, 2 * rows, head))], [SMEM] + [VMEM] * 5,
+        (place, tokens, swap(tokens), own_weight, own_cosine, own_sine), 4 * rows * features * head)
+    own_part = to_chips(projected).reshape(seq, head)
+    other_part = swap(own_part)
+    other_weight = swap(own_weight)
 
     window = LONGEST + 2 * BLOCK
     grad_query, kept, sent = call(
         attention_kernel,
         [shape((rows, width)), shape((seq // 2, 2 * head)), shape((seq // 2, 2 * head))],
-        [SMEM] * 3 + [VMEM] * 6,
-        (place, block_order, doc_lengths, tokens, upstream, big_weights, keys_values, cosine, sine),
+        [SMEM] * 3 + [VMEM] * 7,
+        (place, block_order, doc_lengths, tokens, upstream, big_weights, own_part, other_part, cosine, sine),
         4 * rows * features * width + 20 * rows * heads * window * head,
         scratch=[pltpu.VMEM((rows, width), BF16), pltpu.VMEM((rows, width), BF16),
                  pltpu.VMEM((window, head), BF16), pltpu.VMEM((window, head), BF16),
                  pltpu.VMEM((seq, 2 * head), F32), pltpu.SMEM((seq // BLOCK,), jnp.int32)])
-    pairs = (kept.astype(F32) + lax.ppermute(sent, "ctx", other).astype(F32)).astype(BF16)
+    pairs = (kept.astype(F32) + swap(sent).astype(F32)).astype(BF16)
     pieces = to_chips(pairs).reshape(chips, rows, 2 * head)
     grad_key_value, kept, sent = call(
         owner_kernel,
         [shape((rows, 2 * head)), shape((features // 2, head)), shape((features // 2, head))],
         [SMEM] + [VMEM] * 4, (place, pieces, tokens, cosine, sine), 2 * rows * features * head)
-    received = lax.ppermute(sent, "ctx", other)
+    received = swap(sent)
     (grad_input,) = call(
-        input_kernel, [shape((rows, features))], [VMEM] * 4,
-        (grad_query, grad_key_value, big_weights, other_weight), 2 * rows * features * (width + 2 * head))
+        input_kernel, [shape((rows, features))], [SMEM] + [VMEM] * 5,
+        (place, grad_query, grad_key_value, big_weights, own_weight, other_weight), 2 * rows * features * (width + 2 * head))
     parts = (kept.astype(F32) + received.astype(F32)).astype(BF16)
     shard = jnp.sum(to_chips(parts).reshape(chips, rows, head).astype(F32), axis=0).astype(BF16)
     slices = lax.all_to_all(shard, "dp", 0, 0, tiled=True).reshape(dp, rows // dp, head)

time: 262 us -> 195 us (0.74)
  waiting for transfers between devices: 133 us -> 43 us
  blocking collectives: 65.4 us -> 77.6 us
  starting transfers between devices: 18.2 us -> 29.4 us
    all_gather x1, waiting for transfers between devices: 72.3 us -> 17.5 us  [on_device(): big_weights = lax.all_gather(packed, 'ctx', axis=0, tiled=True)]
    all_to_all x2 -> x3, blocking collectives: 33.8 us -> 54.4 us  [to_chips(): lax.all_to_all(pieces, 'ctx', 0, 0, tiled=True, axis_index_groups=planes)]
    all_gather x3 -> x0, waiting for transfers between devices: 20 us -> none  [the longest x1 20 us: on_device(): lax.all_gather(own_part, 'ctx', axis=0, tiled=True, axis_index_groups=cores)]
    ppermute x2 -> x6, starting transfers between devices: 5.97 us -> 22.2 us  [swap(): return lax.ppermute(v, 'ctx', other)]
    all_to_all x2 -> x1, waiting for transfers between devices: 32 us -> 16.5 us  [to_chips(): lax.all_to_all(pieces, 'ctx', 0, 0, tiled=True, axis_index_groups=planes)]
    all_gather x1 -> x0, blocking collectives: 8.41 us -> none  [on_device(): lax.all_gather(jnp.stack([key_weight, value_weight]), 'ctx', axis=1, tile...]
    all_to_all x2 -> x1, starting transfers between devices: 8.56 us -> 3.66 us  [to_chips(): lax.all_to_all(pieces, 'ctx', 0, 0, tiled=True, axis_index_groups=planes)]
  transfers between devices with their start and end apart: 9 -> 9, of which waited for: 7 -> 5; matrix products, arithmetic and copies ran while one was open for 2% -> 3% of each run, Pallas kernels for 3% -> 4%
where the time goes in v2:
time: 195 us; the launch traced here: 192 us
  blocking collectives  77.6 us (40%)
  waiting for transfers between devices  43 us (22%)
  starting transfers between devices  29.4 us (15%)
  Pallas kernels  17 us (9%)
  between operations  14.3 us (7%)
  other arithmetic  5.6 us (3%)
  local copies, waits for them, and re-layouts  5.5 us (3%)
    all_to_all x3, blocking collectives, to_chips(): lax.all_to_all(pieces, 'ctx', 0, 0, tiled=True, axis_index_groups=planes)  54.4 us
    all_to_all x1, blocking collectives, on_device(): lax.all_to_all(shard, 'dp', 0, 0, tiled=True).reshape(dp, rows // dp, head)  23.3 us
    ppermute x6, starting transfers between devices, swap(): return lax.ppermute(v, 'ctx', other)  22.2 us
    all_gather x1, waiting for transfers between devices, on_device(): big_weights = lax.all_gather(packed, 'ctx', axis=0, tiled=True)  17.5 us
    pallas_call x4, Pallas kernels, call(): pl.pallas_call(body, out_shape=outs, in_specs=in_specs, out_specs=[VMEM]...  17 us
    all_to_all x1, waiting for transfers between devices, to_chips(): lax.all_to_all(pieces, 'ctx', 0, 0, tiled=True, axis_index_groups=planes)  16.5 us
    all_to_all x1, waiting for transfers between devices, on_device(): lax.all_to_all(jnp.broadcast_to(own_slice[None], (dp,) + own_slice.shape)...  5.17 us
  transfers between devices with their start and end apart: 9, of which 5 were waited for; matrix products, arithmetic and copies ran while one was open for 3% of the time, Pallas kernels for 4%

profile of v2, /device:TPU:1, one launch (start us, length us, event | category | flops | bytes accessed | tf_op | source)
XLA Modules:
  0.0 192.4 jit_solution(14481334635129838388)
XLA Ops:
  7.2 1.0 copy.11
  8.2 1.6 pad_maximum_fusion
  9.9 0.8 broadcast_select_fusion.2
  10.7 8.8 %collective-permute-start.1 = (bf16[128,128]{1,0:T(8,128)(2,1)S(1)}, bf16[128,128]{1,0:T(8,128)(2,1)S(1)}, u32[]{:S(2)}, u32[]{:S(2)}) collective-permute-start(bf16[128,128]{1,0:T(8,128)(2,1)S(1)} %broadcast_select_fusion.2), channel_id=1, source_target_pairs={{0,16},{16,0},{32,48},{48,32},{64,80},{80,64},{96,112},{112,96},{1... | collective-permute-start | bytes 98312 | tf_op jit(solution)/shard_map/ppermute | solution.py:202
  19.4 1.9 collective-permute-start
  21.4 0.8 broadcast_select_fusion.1
  22.2 1.2 broadcast_in_dim.13
  23.4 3.7 %all-to-all-start = ((bf16[16,256,128]{2,1,0:T(8,128)(2,1)}), bf16[16,256,128]{2,1,0:T(8,128)(2,1)S(1)}, u32[]{:S(2)}, u32[]{:S(2)}) async-start(bf16[16,256,128]{2,1,0:T(8,128)(2,1)} %broadcast_in_dim.13), calls=%async_computation | async-start | bytes 2097152 | tf_op jit(solution)/shard_map/all_to_all | solution.py:188
  27.3 0.5 fusion.2
  27.9 0.6 copy-done.4
  28.7 16.5 %all-to-all-done = bf16[16,256,128]{2,1,0:T(8,128)(2,1)S(1)} async-done(((bf16[16,256,128]{2,1,0:T(8,128)(2,1)}), bf16[16,256,128]{2,1,0:T(8,128)(2,1)S(1)}, u32[]{:S(2)}, u32[]{:S(2)}) %all-to-all-start) | async-done | bytes 1048608 | tf_op jit(solution)/shard_map/all_to_all | solution.py:188
  45.2 0.8 shard_map.95
  46.0 19.9 %all_to_all.42 = bf16[16,256,128]{2,1,0:T(8,128)(2,1)S(1)} all-to-all(bf16[16,256,128]{2,1,0:T(8,128)(2,1)S(1)} %shard_map.95), channel_id=1, replica_groups={{0,32,64,96,128,160,192,224,256,288,320,352,384,416,448,480},{16,48,80,..., dimensions={0} | all-to-all | bytes 2097152 | tf_op jit(solution)/shard_map/all_to_all | solution.py:188
  66.0 3.9 %collective-permute-start.2 = (bf16[4096,128]{1,0:T(8,128)(2,1)S(1)}, bf16[4096,128]{1,0:T(8,128)(2,1)}, u32[]{:S(2)}, u32[]{:S(2)}) collective-permute-start(bf16[4096,128]{1,0:T(8,128)(2,1)S(1)} %bitcast.20), channel_id=1, source_target_pairs={{0,16},{16,0},{32,48},{48,32},{64,80},{80,64},{96,112},{112,96},{1... | collective-permute-start | bytes 3145736 | tf_op jit(solution)/shard_map/ppermute | solution.py:202
  69.9 1.0 fusion
  70.9 1.5 collective-permute-done.2.other_part
  72.4 17.5 %all-gather.2.cloned.1.call-done.weights.query_weight = bf16[4096,1024]{1,0:T(8,128)(2,1)} async-done(((bf16[128,1024]{1,0:T(8,128)(2,1)}), bf16[4096,1024]{1,0:T(8,128)(2,1)}) %all-gather.2.cloned.1.call-update) | async-done | bytes 8388624 | tf_op jit(solution)/shard_map/all_gather | solution.py:191
  89.9 1.2 copy-done.1
  91.1 9.3 %shard_map.96 = (bf16[128,512]{1,0:T(8,128)(2,1)S(1)}, bf16[2048,256]{1,0:T(8,128)(2,1)S(1)}, bf16[2048,256]{1,0:T(8,128)(2,1)S(1)}) custom-call(s32[1]{0:T(128)} %bitcast.place, s32[1,64]{1,0:T(1,128)S(1)} %copy-done.2, s32[1,8]{1,0:T(1,128)S(1)} %copy-done.3, bf16[128,4096]{1,0:T(8,128)(2,1)S(1)} %bitcast.15, bf16[128,4096]{1,0:T(8,128)(2,1)S(1)} %bitcast.22, ...), custom_call_target="tpu_custom_call" | custom-call | flops 2583691264 | bytes 14942500 | tf_op jit(solution)/shard_map/pallas_call | solution.py:25
  100.3 2.2 %collective-permute-start.3 = (bf16[2048,256]{1,0:T(8,128)(2,1)S(1)}, bf16[2048,256]{1,0:T(8,128)(2,1)S(1)}, u32[]{:S(2)}, u32[]{:S(2)}) collective-permute-start(bf16[2048,256]{1,0:T(8,128)(2,1)S(1)} %get-tuple-element.10), channel_id=1, source_target_pairs={{0,16},{16,0},{32,48},{48,32},{64,80},{80,64},{96,112},{112,96},{1... | collective-permute-start | bytes 3145736 | tf_op jit(solution)/shard_map/ppermute | solution.py:202
  102.5 2.4 %collective-permute-done.3 = bf16[2048,256]{1,0:T(8,128)(2,1)S(1)} collective-permute-done((bf16[2048,256]{1,0:T(8,128)(2,1)S(1)}, bf16[2048,256]{1,0:T(8,128)(2,1)S(1)}, u32[]{:S(2)}, u32[]{:S(2)}) %collective-permute-start.3) | collective-permute-done | bytes 1048608 | tf_op jit(solution)/shard_map/ppermute | solution.py:202
  105.2 21.2 %all_to_all.43.pieces = bf16[16,128,256]{2,1,0:T(8,128)(2,1)S(1)} all-to-all(bf16[16,128,256]{2,1,0:T(8,128)(2,1)S(1)} %bitcast.23), channel_id=1, replica_groups={{0,32,64,96,128,160,192,224,256,288,320,352,384,416,448,480},{16,48,80,..., dimensions={0} | all-to-all | bytes 2097152 | tf_op jit(solution)/shard_map/all_to_all | solution.py:188
  126.4 0.5 shard_map.97
  126.9 3.6 %collective-permute-start.5 = (bf16[2048,128]{1,0:T(8,128)(2,1)S(1)}, bf16[2048,128]{1,0:T(8,128)(2,1)S(1)}, u32[]{:S(2)}, u32[]{:S(2)}) collective-permute-start(bf16[2048,128]{1,0:T(8,128)(2,1)S(1)} %get-tuple-element.13), channel_id=1, source_target_pairs={{0,16},{16,0},{32,48},{48,32},{64,80},{80,64},{96,112},{112,96},{1... | collective-permute-start | bytes 1572872 | tf_op jit(solution)/shard_map/ppermute | solution.py:202
  130.5 1.9 collective-permute-start.4
  132.6 13.3 %all_to_all.44 = bf16[16,128,128]{2,1,0:T(8,128)(2,1)S(1)} all-to-all(bf16[16,128,128]{2,1,0:T(8,128)(2,1)S(1)} %bitcast.24), channel_id=1, replica_groups={{0,32,64,96,128,160,192,224,256,288,320,352,384,416,448,480},{16,48,80,..., dimensions={0} | all-to-all | bytes 1048576 | tf_op jit(solution)/shard_map/all_to_all | solution.py:188
  145.9 23.3 %all_to_all.45 = bf16[16,8,128]{2,1,0:T(8,128)(2,1)S(1)} all-to-all(bf16[16,8,128]{2,1,0:T(8,128)(2,1)S(1)} %bitcast.28), channel_id=1, replica_groups=mesh['ctx'=32,'dp'=16] {'dp'}, dimensions={0} | all-to-all | bytes 65536 | tf_op jit(solution)/shard_map/all_to_all | solution.py:238
  169.2 0.6 broadcast_in_dim.30
  169.9 3.5 %all-to-all-start.5 = ((f32[16,8,128]{2,1,0:T(8,128)}), f32[16,8,128]{2,1,0:T(8,128)S(1)}, u32[]{:S(2)}, u32[]{:S(2)}) async-start(f32[16,8,128]{2,1,0:T(8,128)} %broadcast_in_dim.30), calls=%async_computation.5 | async-start | bytes 131072 | tf_op jit(solution)/shard_map/all_to_all | solution.py:240
  173.4 6.4 %shard_map.98 = bf16[128,4096]{1,0:T(8,128)(2,1)} custom-call(s32[1]{0:T(128)} %bitcast.place, bf16[128,512]{1,0:T(8,128)(2,1)S(1)} %get-tuple-element.8.grad_query, bf16[128,256]{1,0:T(8,128)(2,1)S(1)} %get-tuple-element.11.grad_key_value, bf16[4096,1024]{1,0:T(8,128)(2,1)} %all-gather.2.cloned.1.call-done.weights.query_weight, ...), custom_call_target="tpu_custom_call" | custom-call | flops 805306368 | bytes 11730948 | tf_op jit(solution)/shard_map/pallas_call | solution.py:25
  179.8 5.2 %all-to-all-done.5 = f32[16,8,128]{2,1,0:T(8,128)S(1)} async-done(((f32[16,8,128]{2,1,0:T(8,128)}), f32[16,8,128]{2,1,0:T(8,128)S(1)}, u32[]{:S(2)}, u32[]{:S(2)}) %all-to-all-start.5) | async-done | bytes 65568 | tf_op jit(solution)/shard_map/all_to_all | solution.py:240
  185.0 0.6 copy.13
  (30 shorter events, 1.1 us)
Async XLA Ops:
  7.2 82.7 %all-gather.2.cloned.1.call-start = ((), (), s32[]{:S(2)}) async-start(), calls=%async_computation.6 | async-start | bytes 8650752 | tf_op jit(solution)/shard_map/all_gather | solution.py:191
  9.8 17.2 %copy-start.2 = (s32[1,64]{1,0:T(1,128)S(1)}, s32[1,64]{1,0:T(1,128)}, u32[]{:S(2)}) copy-start(s32[1,64]{1,0:T(1,128)} %order.1) | copy-start | bytes 772
  10.7 10.7 %collective-permute-start.1 = (bf16[128,128]{1,0:T(8,128)(2,1)S(1)}, bf16[128,128]{1,0:T(8,128)(2,1)S(1)}, u32[]{:S(2)}, u32[]{:S(2)}) collective-permute-start(bf16[128,128]{1,0:T(8,128)(2,1)S(1)} %broadcast_select_fusion.2), channel_id=1, source_target_pairs={{0,16},{16,0},{32,48},{48,32},{64,80},{80,64},{96,112},{112,96},{1... | collective-permute-start | bytes 98312 | tf_op jit(solution)/shard_map/ppermute | solution.py:202
  19.4 25.8 %collective-permute-start = (bf16[128,4096]{1,0:T(8,128)(2,1)}, bf16[128,4096]{1,0:T(8,128)(2,1)S(1)}, u32[]{:S(2)}, u32[]{:S(2)}) collective-permute-start(bf16[128,4096]{1,0:T(8,128)(2,1)} %bitcast.13), channel_id=1, source_target_pairs={{0,16},{16,0},{32,48},{48,32},{64,80},{80,64},{96,112},{112,96},{1... | collective-permute-start | bytes 3145736 | tf_op jit(solution)/shard_map/ppermute | solution.py:202
  22.2 23.0 %copy-start = (bf16[1,128,4096]{2,1,0:T(8,128)(2,1)S(1)}, bf16[1,128,4096]{2,1,0:T(8,128)(2,1)}, u32[]{:S(2)}) copy-start(bf16[1,128,4096]{2,1,0:T(8,128)(2,1)} %param.8) | copy-start | bytes 3145732
  23.4 21.8 %all-to-all-start = ((bf16[16,256,128]{2,1,0:T(8,128)(2,1)}), bf16[16,256,128]{2,1,0:T(8,128)(2,1)S(1)}, u32[]{:S(2)}, u32[]{:S(2)}) async-start(bf16[16,256,128]{2,1,0:T(8,128)(2,1)} %broadcast_in_dim.13), calls=%async_computation | async-start | bytes 2097152 | tf_op jit(solution)/shard_map/all_to_all | solution.py:188
  27.9 0.6 copy-start.4
  27.9 0.7 copy-start.6
  27.9 0.7 copy-start.7
  46.0 23.8 %copy-start.5 = (f32[256,64]{1,0:T(8,128)S(1)}, f32[256,64]{1,0:T(8,128)}, u32[]{:S(2)}) copy-start(f32[256,64]{1,0:T(8,128)} %copy-done.4) | copy-start | bytes 196612
  46.0 43.8 %copy-start.3 = (s32[1,8]{1,0:T(1,128)S(1)}, s32[1,8]{1,0:T(1,128)}, u32[]{:S(2)}) copy-start(s32[1,8]{1,0:T(1,128)} %lengths.1) | copy-start | bytes 100
  66.0 6.4 %collective-permute-start.2 = (bf16[4096,128]{1,0:T(8,128)(2,1)S(1)}, bf16[4096,128]{1,0:T(8,128)(2,1)}, u32[]{:S(2)}, u32[]{:S(2)}) collective-permute-start(bf16[4096,128]{1,0:T(8,128)(2,1)S(1)} %bitcast.20), channel_id=1, source_target_pairs={{0,16},{16,0},{32,48},{48,32},{64,80},{80,64},{96,112},{112,96},{1... | collective-permute-start | bytes 3145736 | tf_op jit(solution)/shard_map/ppermute | solution.py:202
  89.8 1.2 copy-start.1
  100.3 4.6 %collective-permute-start.3 = (bf16[2048,256]{1,0:T(8,128)(2,1)S(1)}, bf16[2048,256]{1,0:T(8,128)(2,1)S(1)}, u32[]{:S(2)}, u32[]{:S(2)}) collective-permute-start(bf16[2048,256]{1,0:T(8,128)(2,1)S(1)} %get-tuple-element.10), channel_id=1, source_target_pairs={{0,16},{16,0},{32,48},{48,32},{64,80},{80,64},{96,112},{112,96},{1... | collective-permute-start | bytes 3145736 | tf_op jit(solution)/shard_map/ppermute | solution.py:202
  126.9 5.5 %collective-permute-start.5 = (bf16[2048,128]{1,0:T(8,128)(2,1)S(1)}, bf16[2048,128]{1,0:T(8,128)(2,1)S(1)}, u32[]{:S(2)}, u32[]{:S(2)}) collective-permute-start(bf16[2048,128]{1,0:T(8,128)(2,1)S(1)} %get-tuple-element.13), channel_id=1, source_target_pairs={{0,16},{16,0},{32,48},{48,32},{64,80},{80,64},{96,112},{112,96},{1... | collective-permute-start | bytes 1572872 | tf_op jit(solution)/shard_map/ppermute | solution.py:202
  130.5 42.9 %collective-permute-start.4 = (bf16[4096,128]{1,0:T(8,128)(2,1)S(1)}, bf16[4096,128]{1,0:T(8,128)(2,1)S(1)}, u32[]{:S(2)}, u32[]{:S(2)}) collective-permute-start(bf16[4096,128]{1,0:T(8,128)(2,1)S(1)} %bitcast.18), channel_id=1, source_target_pairs={{0,16},{16,0},{32,48},{48,32},{64,80},{80,64},{96,112},{112,96},{1... | collective-permute-start | bytes 3145736 | tf_op jit(solution)/shard_map/ppermute | solution.py:202
  169.9 15.1 %all-to-all-start.5 = ((f32[16,8,128]{2,1,0:T(8,128)}), f32[16,8,128]{2,1,0:T(8,128)S(1)}, u32[]{:S(2)}, u32[]{:S(2)}) async-start(f32[16,8,128]{2,1,0:T(8,128)} %broadcast_in_dim.30), calls=%async_computation.5 | async-start | bytes 131072 | tf_op jit(solution)/shard_map/all_to_all | solution.py:240
Sparse Core Ops, SparseCore 0:
  11.1 78.6 all-gather.1

commit v3 on v2

--- a/solution.py
+++ b/solution.py
@@ -1,3 +1,4 @@
+import functools
 import math
 
 import jax
@@ -11,6 +12,7 @@
 NEG = -1e30
 BLOCK = 64
 LONGEST = 1024
+RING = (0, -1, 1, 2)
 BF16 = jnp.bfloat16
 F32 = jnp.float32
 NT = (((1,), (1,)), ((), ()))
@@ -18,9 +20,10 @@
 NN = (((1,), (0,)), ((), ()))
 VMEM = pl.BlockSpec(memory_space=pltpu.VMEM)
 SMEM = pl.BlockSpec(memory_space=pltpu.SMEM)
-
-
-def call(body, outs, in_specs, args, flops, scratch=(), limit=48):
+HBM = pl.BlockSpec(memory_space=pltpu.HBM)
+
+
+def call(body, outs, in_specs, args, flops, scratch=(), limit=24):
     moved = sum(math.prod(a.shape) * a.dtype.itemsize for a in list(args) + list(outs))
     return pl.pallas_call(
         body,
@@ -50,6 +53,56 @@
     return pltpu.roll(v, v.shape[-1] // 2, axis=1)
 
 
+def fetch(sources, targets, arrived):
+    copies = [pltpu.make_async_copy(a, b, arrived.at[i]) for i, (a, b) in enumerate(zip(sources, targets))]
+    for copy in copies:
+        copy.start()
+    return copies
+
+
+def pack_kernel(query_weight, out_weight, out, query, turned, arrived):
+    width = query_weight.shape[1]
+    copies = fetch((query_weight, out_weight), (query, turned), arrived)
+    copies[0].wait()
+    for copy in range(out.shape[0]):
+        out[copy, :, :width] = query[...]
+    copies[1].wait()
+    columns = turned[...].T
+    for copy in range(out.shape[0]):
+        out[copy, :, width:] = columns
+
+
+def shard_order(core, chip, side):
+    row, column = chip // side, chip % side
+    order = []
+    for offset in RING:
+        for first in range(side):
+            down = jnp.where(core == 0, (row + offset + side) % side, first)
+            along = jnp.where(core == 0, first, (column + offset + side) % side)
+            order.append((down * side + along) * 2 + core)
+    return order
+
+
+def partial_kernel(place, tokens, other_tokens, upstream, other_upstream, *rest, begin):
+    pieces, (mine, theirs) = rest[:-2], rest[-2:]
+    added = pieces[-2:] if begin else ()
+    pieces = pieces[:-2] if begin else pieces
+    rows, features = tokens.shape
+    width = mine.shape[1] // 2
+    side = math.isqrt(features // (2 * rows))
+    shards = shard_order(place[0] % 2, place[0] // 2, side)
+    for source, start, which, out in ((other_tokens, 0, 1, theirs), (other_upstream, width, 1, theirs),
+                                      (tokens, 0, 0, mine), (upstream, width, 0, mine)):
+        total = added[which][:, start:start + width] if begin else jnp.zeros((rows, width), F32)
+        for n in range(0, side * len(pieces), 2):
+            piece, at = pieces[n // side], (n % side) * rows
+            columns = [pl.ds(pl.multiple_of(shards[begin * side + n + i] * rows, rows), rows) for i in range(2)]
+            t = jnp.concatenate([source[:, here] for here in columns], axis=1)
+            total += lax.dot_general(t, piece[at:at + 2 * rows, start:start + width], NN,
+                                     preferred_element_type=F32)
+        out[:, start:start + width] = total
+
+
 def project_kernel(place, tokens, other_tokens, weight, cosine, sine, out):
     rows = tokens.shape[0]
     own_core = place[0] % 2
@@ -61,9 +114,11 @@
             out[chip, here, :] = v
 
 
-def attention_kernel(place, order, lengths, tokens, upstream, weights, own_part, other_part, cosine, sine,
-                     grad_query, kept, sent, q_ref, a_ref, key_window, value_window, total, stored_at):
-    rows, features = tokens.shape
+def attention_kernel(place, order, lengths, mine_at, theirs_at, own_at, other_at, cosine, sine,
+                     grad_query, kept, sent, q_ref, a_ref, key_window, value_window, total, stored_at,
+                     mine, theirs, own_part, other_part, arrived):
+    copies = fetch((mine_at, theirs_at, own_at, other_at), (mine, theirs, own_part, other_part), arrived)
+    rows = mine.shape[0]
     head = cosine.shape[1]
     heads = q_ref.shape[1] // head
     seq = own_part.shape[0]
@@ -79,13 +134,15 @@
 
     lax.fori_loop(0, blocks, invert, 0)
     width = heads * head
-    queries = lax.dot_general(tokens[...], weights[:, :width], NN, preferred_element_type=F32)
+    total[...] = jnp.zeros_like(total)
+    for copy in copies:
+        copy.wait()
+    queries = mine[:, :width] + theirs[:, :width]
     c, s = cosine[...], sine[...]
     for h in range(heads):
         v = queries[:, h * head:(h + 1) * head]
         q_ref[:, h * head:(h + 1) * head] = (v * c + swap_halves(v) * s).astype(BF16)
-    a_ref[...] = lax.dot_general(upstream[...], weights[:, width:], NN, preferred_element_type=F32).astype(BF16)
-    total[...] = jnp.zeros_like(total)
+    a_ref[...] = (mine[:, width:] + theirs[:, width:]).astype(BF16)
 
     def destination(kb):
         spot = stored_at[jnp.maximum(kb, 0)]
@@ -138,35 +195,55 @@
     sent[...] = total[half:].astype(BF16)
 
 
-def owner_kernel(place, pieces, tokens, cosine, sine, grad_key_value, kept, sent):
+def owner_kernel(pieces, cosine, sine, grad_key_value):
     head = cosine.shape[1]
     total = jnp.sum(pieces[...].astype(F32), axis=0)
     u = total[:, :head]
     grad_key_value[:, :head] = (u * cosine[...] - swap_halves(u) * sine[...]).astype(BF16)
-    grad_value = total[:, head:].astype(BF16)
-    grad_key_value[:, head:] = grad_value
-    rows = tokens.shape[0]
-    own_core = place[0] % 2
-    for chip in range(tokens.shape[1] // (2 * rows)):
-        for away in range(2):
-            core = jnp.where(own_core == away, 0, 1)
-            columns = pl.ds(pl.multiple_of((2 * chip + core) * rows, rows), rows)
-            part = lax.dot_general(tokens[:, columns], grad_value, TN, preferred_element_type=F32)
-            (sent if away else kept)[chip * rows:(chip + 1) * rows, :] = part.astype(BF16)
-
-
-def input_kernel(place, grad_query, grad_key_value, query_weight, own_weight, other_weight, out):
-    width = grad_query.shape[1]
+    grad_key_value[:, head:] = total[:, head:].astype(BF16)
+
+
+def weight_kernel(place, tokens, other_tokens, grads, other_grads, out):
+    rows, features = tokens.shape
+    core = place[0] % 2
+    head = out.shape[2]
+    both = jnp.concatenate([grads[:, head:], other_grads[:, head:]], axis=0)
+    for chip in range(features // (2 * rows)):
+        here = pl.ds(pl.multiple_of((2 * chip + core) * rows, rows), rows)
+        t = jnp.concatenate([tokens[:, here], other_tokens[:, here]], axis=0)
+        out[chip] = lax.dot_general(t, both, TN, preferred_element_type=F32).astype(BF16)
+
+
+def input_kernel(place, grad_query, other_grad_query, grads, other_grads, own_weight, other_weight,
+                 w0, w1, w2, w3, mine, theirs):
+    rows, width = grad_query.shape
     head = own_weight.shape[1]
-    own_core = place[0] % 2
-    grad_key, grad_value = grad_key_value[:, :head], grad_key_value[:, head:]
-    own_grad = jnp.where(own_core == 0, grad_key, grad_value)
-    other_grad = jnp.where(own_core == 0, grad_value, grad_key)
-    out[...] = (
-        lax.dot_general(grad_query[...], query_weight[:, :width], NT, preferred_element_type=F32)
-        + lax.dot_general(own_grad, own_weight[...], NT, preferred_element_type=F32)
-        + lax.dot_general(other_grad, other_weight[...], NT, preferred_element_type=F32)
-    ).astype(BF16)
+    core = place[0] % 2
+    side = math.isqrt(own_weight.shape[0] // (2 * rows))
+    queries = jnp.concatenate([grad_query[...], other_grad_query[...]], axis=0)
+    both = jnp.concatenate([grads[...], other_grads[...]], axis=0)
+    own_grad = jnp.where(core == 0, both[:, :head], both[:, head:])
+    other_grad = jnp.where(core == 0, both[:, head:], both[:, :head])
+    for n, shard in enumerate(shard_order(core, place[0] // 2, side)):
+        at = (n % side) * rows
+        here = pl.ds(pl.multiple_of(shard * rows, rows), rows)
+        to = pl.ds(pl.multiple_of((shard // 2) * rows, rows), rows)
+        part = (
+            lax.dot_general(queries, (w0, w1, w2, w3)[n // side][at:at + rows, :width], NT,
+                            preferred_element_type=F32)
+            + lax.dot_general(own_grad, own_weight[here, :], NT, preferred_element_type=F32)
+            + lax.dot_general(other_grad, other_weight[here, :], NT, preferred_element_type=F32)
+        ).astype(BF16)
+        mine[:, to] = part[:rows]
+        theirs[:, to] = part[rows:]
+
+
+def merge_kernel(place, mine, received, out):
+    rows = out.shape[0]
+    core = place[0] % 2
+    for chip in range(mine.shape[1] // rows):
+        for source, shard in ((mine, 2 * chip + core), (received, 2 * chip + 1 - core)):
+            out[:, pl.ds(pl.multiple_of(shard * rows, rows), rows)] = source[:, chip * rows:(chip + 1) * rows]
 
 
 def on_device(inputs, grad_output, query_weight, key_weight, value_weight, out_weight, doc_lengths, block_order):
@@ -187,8 +264,24 @@
     def to_chips(pieces):
         return lax.all_to_all(pieces, "ctx", 0, 0, tiled=True, axis_index_groups=planes)
 
-    packed = jnp.concatenate([query_weight, out_weight.T], axis=1)
-    big_weights = lax.all_gather(packed, "ctx", axis=0, tiled=True)
+    side = math.isqrt(chips)
+
+    def moved(v, phase, step):
+        pairs = []
+        for row in range(side):
+            for column in range(side):
+                for c in range(2):
+                    to = (row, (column + step) % side) if c == phase else ((row + step) % side, column)
+                    pairs.append(((row * side + column) * 2 + c, (to[0] * side + to[1]) * 2 + c))
+        return lax.ppermute(v, "ctx", pairs)
+
+    rings = [[(row * side + i) * 2 for i in range(side)] for row in range(side)]
+    rings += [[(i * side + column) * 2 + 1 for i in range(side)] for column in range(side)]
+    (packed,) = call(pack_kernel, [shape((side, rows, 2 * width))], [HBM] * 2, (query_weight, out_weight), 0,
+                     scratch=[pltpu.VMEM((rows, width), BF16), pltpu.VMEM((width, rows), BF16),
+                              pltpu.SemaphoreType.DMA((2,))])
+    line = lax.all_to_all(packed, "ctx", 0, 0, tiled=True, axis_index_groups=rings).reshape(side * rows, 2 * width)
+    held = [line] + [moved(line, 1, -offset) for offset in RING[1:]]
 
     chip_blocks = lax.dynamic_slice_in_dim(block_order[0], (me // 2) * 4, 4)
     chip_cosine, chip_sine = tables(chip_blocks, head)
@@ -204,41 +297,63 @@
     mine = jnp.where(is_key, key_weight, value_weight)
     theirs = swap(jnp.where(is_key, value_weight, key_weight))
     chip_weight = jnp.concatenate([jnp.where(is_key, mine, theirs), jnp.where(is_key, theirs, mine)], axis=0)
-    own_weight = to_chips(
-        jnp.broadcast_to(chip_weight[None], (chips,) + chip_weight.shape)).reshape(features, head)
+    copies, _ = lax.optimization_barrier(
+        (jnp.broadcast_to(chip_weight[None], (chips,) + chip_weight.shape), line))
+    own_weight = to_chips(copies).reshape(features, head)
+    other_tokens = swap(tokens)
     (projected,) = call(
         project_kernel, [shape((chips, 2 * rows, head))], [SMEM] + [VMEM] * 5,
-        (place, tokens, swap(tokens), own_weight, own_cosine, own_sine), 4 * rows * features * head)
+        (place, tokens, other_tokens, own_weight, own_cosine, own_sine), 4 * rows * features * head)
+    sources = (place, tokens, other_tokens, upstream, swap(upstream))
+    halves = [shape((rows, 2 * width), F32)] * 2
+    mine, theirs = call(
+        functools.partial(partial_kernel, begin=0), halves, [SMEM] + [VMEM] * 7,
+        sources + tuple(held[:3]), 3 * rows * features * width)
+    mine, theirs = call(
+        functools.partial(partial_kernel, begin=3), halves, [SMEM] + [VMEM] * 7,
+        sources + (held[3], mine, theirs), rows * features * width)
     own_part = to_chips(projected).reshape(seq, head)
+    own_part, mine, theirs = lax.optimization_barrier((own_part, mine, theirs))
+    received = swap(theirs)
     other_part = swap(own_part)
     other_weight = swap(own_weight)
-
     window = LONGEST + 2 * BLOCK
     grad_query, kept, sent = call(
         attention_kernel,
         [shape((rows, width)), shape((seq // 2, 2 * head)), shape((seq // 2, 2 * head))],
-        [SMEM] * 3 + [VMEM] * 7,
-        (place, block_order, doc_lengths, tokens, upstream, big_weights, own_part, other_part, cosine, sine),
-        4 * rows * features * width + 20 * rows * heads * window * head,
+        [SMEM] * 3 + [HBM] * 4 + [VMEM] * 2,
+        (place, block_order, doc_lengths, mine, received, own_part, other_part, cosine, sine),
+        20 * rows * heads * window * head,
         scratch=[pltpu.VMEM((rows, width), BF16), pltpu.VMEM((rows, width), BF16),
                  pltpu.VMEM((window, head), BF16), pltpu.VMEM((window, head), BF16),
-                 pltpu.VMEM((seq, 2 * head), F32), pltpu.SMEM((seq // BLOCK,), jnp.int32)])
+                 pltpu.VMEM((seq, 2 * head), F32), pltpu.SMEM((seq // BLOCK,), jnp.int32),
+                 pltpu.VMEM((rows, 2 * width), F32), pltpu.VMEM((rows, 2 * width), F32),
+                 pltpu.VMEM((seq, head), BF16), pltpu.VMEM((seq, head), BF16), pltpu.SemaphoreType.DMA((4,))],
+        limit=28)
     pairs = (kept.astype(F32) + swap(sent).astype(F32)).astype(BF16)
     pieces = to_chips(pairs).reshape(chips, rows, 2 * head)
-    grad_key_value, kept, sent = call(
-        owner_kernel,
-        [shape((rows, 2 * head)), shape((features // 2, head)), shape((features // 2, head))],
-        [SMEM] + [VMEM] * 4, (place, pieces, tokens, cosine, sine), 2 * rows * features * head)
-    received = swap(sent)
+    (grads,) = call(owner_kernel, [shape((rows, 2 * head))], [VMEM] * 3, (pieces, cosine, sine), 0)
+    other_grads = swap(grads)
+    (parts,) = call(
+        weight_kernel, [shape((chips, rows, head))], [SMEM] + [VMEM] * 4,
+        (place, tokens, other_tokens, grads, other_grads), 2 * rows * features * head)
+    input_mine, input_theirs = call(
+        input_kernel, [shape((rows, features // 2))] * 2, [SMEM] + [VMEM] * 10,
+        (place, grad_query, swap(grad_query), grads, other_grads, own_weight, other_weight, *held),
+        2 * rows * features * (width + 2 * head))
     (grad_input,) = call(
-        input_kernel, [shape((rows, features))], [SMEM] + [VMEM] * 5,
-        (place, grad_query, grad_key_value, big_weights, own_weight, other_weight), 2 * rows * features * (width + 2 * head))
-    parts = (kept.astype(F32) + received.astype(F32)).astype(BF16)
-    shard = jnp.sum(to_chips(parts).reshape(chips, rows, head).astype(F32), axis=0).astype(BF16)
-    slices = lax.all_to_all(shard, "dp", 0, 0, tiled=True).reshape(dp, rows // dp, head)
-    own_slice = jnp.sum(slices.astype(F32), axis=0)
-    grad_weight = lax.all_to_all(
-        jnp.broadcast_to(own_slice[None], (dp,) + own_slice.shape), "dp", 0, 0, tiled=True).reshape(rows, head)
+        merge_kernel, [shape((rows, features))], [SMEM] + [VMEM] * 2,
+        (place, input_mine, swap(input_theirs)), 0)
+    grad_weight = jnp.sum(to_chips(parts).reshape(chips, rows, head).astype(F32), axis=0)
+    group, step = dp, dp // 2
+    while group > 4 and group % 2 == 0:
+        sent_on = lax.ppermute(grad_weight.astype(BF16), "dp", [(i, i ^ step) for i in range(dp)])
+        grad_weight = grad_weight.astype(BF16).astype(F32) + sent_on.astype(F32)
+        group, step = group // 2, step // 2
+    near = [[first + i for i in range(group)] for first in range(0, dp, group)]
+    spread = jnp.broadcast_to(grad_weight.astype(BF16)[None], (group, rows, head))
+    gathered = lax.all_to_all(spread, "dp", 0, 0, tiled=True, axis_index_groups=near)
+    grad_weight = jnp.sum(gathered.reshape(group, rows, head).astype(F32), axis=0)
     return grad_input[None], grad_weight
 
 

time: 195 us -> 183 us (0.938)
  blocking collectives: 77.6 us -> 13.6 us
  starting transfers between devices: 29.4 us -> 91.6 us
  between operations: 14.3 us -> 1.12 us
  local copies, waits for them, and re-layouts: 5.5 us -> 11.8 us
  waiting for transfers between devices: 43 us -> 38.7 us
  Pallas kernels: 17 us -> 20.4 us
    all_to_all x3 -> x1, blocking collectives: 54.4 us -> 13.6 us  [to_chips(): lax.all_to_all(pieces, 'ctx', 0, 0, tiled=True, axis_index_groups=planes)]
    ppermute x0 -> x5, starting transfers between devices: none -> 25.7 us  [the longest x2 15.5 us: on_device(): lax.ppermute(grad_weight.astype(BF16), 'dp', [(i, i ^ step) for i in rang...]
    all_to_all x1 -> x0, blocking collectives: 23.3 us -> none  [on_device(): lax.all_to_all(shard, 'dp', 0, 0, tiled=True).reshape(dp, rows // dp, head)]
    all_gather x1 -> x0, waiting for transfers between devices: 17.5 us -> none  [on_device(): big_weights = lax.all_gather(packed, 'ctx', axis=0, tiled=True)]
    ppermute x6 -> x10, starting transfers between devices: 22.2 us -> 37.7 us  [swap(): return lax.ppermute(v, 'ctx', other)]
    all_to_all x1 -> x3, starting transfers between devices: 3.66 us -> 18.1 us  [to_chips(): lax.all_to_all(pieces, 'ctx', 0, 0, tiled=True, axis_index_groups=planes)]
    ppermute x0 -> x5, waiting for transfers between devices: none -> 13.5 us  [the longest x3 13.5 us: moved(): return lax.ppermute(v, 'ctx', pairs)]
    all_to_all x1 -> x2, starting transfers between devices: 3.5 us -> 10.1 us  [the longest x1 5.16 us: on_device(): lax.all_to_all(packed, 'ctx', 0, 0, tiled=True, axis_index_groups=rings)]
  transfers between devices with their start and end apart: 9 -> 20, of which waited for: 5 -> 9; matrix products, arithmetic and copies ran while one was open for 3% -> 2% of each run, Pallas kernels for 4% -> 7%
where the time goes in v3:
time: 183 us; the launch traced here: 181 us
  starting transfers between devices  91.6 us (50%)
  waiting for transfers between devices  38.7 us (21%)
  Pallas kernels  20.4 us (11%)
  blocking collectives  13.6 us (7%)
  local copies, waits for them, and re-layouts  11.8 us (6%)
  other arithmetic  3.92 us (2%)
    ppermute x10, starting transfers between devices, swap(): return lax.ppermute(v, 'ctx', other)  37.7 us
    pallas_call x9, Pallas kernels, call(): pl.pallas_call(body, out_shape=outs, in_specs=in_specs, out_specs=[VMEM]...  20.4 us
    all_to_all x3, waiting for transfers between devices, to_chips(): lax.all_to_all(pieces, 'ctx', 0, 0, tiled=True, axis_index_groups=planes)  18.2 us
    all_to_all x3, starting transfers between devices, to_chips(): lax.all_to_all(pieces, 'ctx', 0, 0, tiled=True, axis_index_groups=planes)  18.1 us
    ppermute x2, starting transfers between devices, on_device(): lax.ppermute(grad_weight.astype(BF16), 'dp', [(i, i ^ step) for i in rang...  15.5 us
    all_to_all x1, blocking collectives, to_chips(): lax.all_to_all(pieces, 'ctx', 0, 0, tiled=True, axis_index_groups=planes)  13.6 us
    ppermute x3, waiting for transfers between devices, moved(): return lax.ppermute(v, 'ctx', pairs)  13.5 us
    ppermute x3, starting transfers between devices, moved(): return lax.ppermute(v, 'ctx', pairs)  10.2 us
  transfers between devices with their start and end apart: 20, of which 9 were waited for; matrix products, arithmetic and copies ran while one was open for 2% of the time, Pallas kernels for 7%

profile of v3, /device:TPU:1, one launch (start us, length us, event | category | flops | bytes accessed | tf_op | source)
XLA Modules:
  0.0 181.2 jit_solution(3738378869985020659)
XLA Ops:
  2.4 1.5 shard_map.95
  3.9 5.2 %all-to-all-start = ((bf16[4,128,1024]{2,1,0:T(8,128)(2,1)}), bf16[4,128,1024]{2,1,0:T(8,128)(2,1)S(1)}, u32[]{:S(2)}, u32[]{:S(2)}) async-start(bf16[4,128,1024]{2,1,0:T(8,128)(2,1)} %shard_map.95), calls=%async_computation | async-start | bytes 2097152 | tf_op jit(solution)/shard_map/all_to_all | solution.py:283
  9.1 7.3 %collective-permute-start.1 = (bf16[128,128]{1,0:T(8,128)(2,1)S(1)}, bf16[128,128]{1,0:T(8,128)(2,1)S(1)}, u32[]{:S(2)}, u32[]{:S(2)}) collective-permute-start(bf16[128,128]{1,0:T(8,128)(2,1)S(1)} %broadcast_select_fusion.2), channel_id=1, source_target_pairs={{0,16},{16,0},{32,48},{48,32},{64,80},{80,64},{96,112},{112,96},{1... | collective-permute-start | bytes 98312 | tf_op jit(solution)/shard_map/ppermute | solution.py:295
  16.5 1.9 %collective-permute-start = (bf16[128,4096]{1,0:T(8,128)(2,1)S(1)}, bf16[128,4096]{1,0:T(8,128)(2,1)S(1)}, u32[]{:S(2)}, u32[]{:S(2)}) collective-permute-start(bf16[128,4096]{1,0:T(8,128)(2,1)S(1)} %bitcast.10), channel_id=1, source_target_pairs={{0,16},{16,0},{32,48},{48,32},{64,80},{80,64},{96,112},{112,96},{1... | collective-permute-start | bytes 3145736 | tf_op jit(solution)/shard_map/ppermute | solution.py:295
  20.2 4.9 %all-to-all-start.1 = ((bf16[16,256,128]{2,1,0:T(8,128)(2,1)}), bf16[16,256,128]{2,1,0:T(8,128)(2,1)S(1)}, u32[]{:S(2)}, u32[]{:S(2)}) async-start(bf16[16,256,128]{2,1,0:T(8,128)(2,1)} %broadcast_in_dim.13), calls=%async_computation.1 | async-start | bytes 2097152 | tf_op jit(solution)/shard_map/all_to_all | solution.py:265
  25.1 7.3 %collective-permute-start.2 = (bf16[128,4096]{1,0:T(8,128)(2,1)}, bf16[128,4096]{1,0:T(8,128)(2,1)}, u32[]{:S(2)}, u32[]{:S(2)}) collective-permute-start(bf16[128,4096]{1,0:T(8,128)(2,1)} %bitcast.23), channel_id=1, source_target_pairs={{0,16},{16,0},{32,48},{48,32},{64,80},{80,64},{96,112},{112,96},{1... | collective-permute-start | bytes 3145736 | tf_op jit(solution)/shard_map/ppermute | solution.py:295
  32.6 3.4 %collective-permute-start.4 = (bf16[512,1024]{1,0:T(8,128)(2,1)}, bf16[512,1024]{1,0:T(8,128)(2,1)}, u32[]{:S(2)}, u32[]{:S(2)}) collective-permute-start(bf16[512,1024]{1,0:T(8,128)(2,1)} %bitcast.18), channel_id=1, source_target_pairs={{0,128},{16,48},{32,160},{48,80},{64,192},{80,112},{96,224},{112,1... | collective-permute-start | bytes 3145736 | tf_op jit(solution)/shard_map/ppermute | solution.py:276
  36.1 3.1 %collective-permute-start.5 = (bf16[512,1024]{1,0:T(8,128)(2,1)}, bf16[512,1024]{1,0:T(8,128)(2,1)}, u32[]{:S(2)}, u32[]{:S(2)}) collective-permute-start(bf16[512,1024]{1,0:T(8,128)(2,1)} %bitcast.19), channel_id=1, source_target_pairs={{0,384},{16,112},{32,416},{48,16},{64,448},{80,48},{96,480},{112,8... | collective-permute-start | bytes 3145736 | tf_op jit(solution)/shard_map/ppermute | solution.py:276
  39.8 3.7 %collective-permute-start.3 = (bf16[512,1024]{1,0:T(8,128)(2,1)}, bf16[512,1024]{1,0:T(8,128)(2,1)}, u32[]{:S(2)}, u32[]{:S(2)}) collective-permute-start(bf16[512,1024]{1,0:T(8,128)(2,1)} %bitcast.20), channel_id=1, source_target_pairs={{0,256},{16,80},{32,288},{48,112},{64,320},{80,16},{96,352},{112,4... | collective-permute-start | bytes 3145736 | tf_op jit(solution)/shard_map/ppermute | solution.py:276
  45.4 5.4 %all-to-all-start.2 = ((bf16[16,256,128]{2,1,0:T(8,128)(2,1)}), bf16[16,256,128]{2,1,0:T(8,128)(2,1)}, u32[]{:S(2)}, u32[]{:S(2)}) async-start(bf16[16,256,128]{2,1,0:T(8,128)(2,1)} %copy-done.4), calls=%async_computation.2 | async-start | bytes 2097152 | tf_op jit(solution)/shard_map/all_to_all | solution.py:265
  50.8 1.7 collective-permute-done.4.rest_1_.w1
  54.9 3.0 %shard_map.97 = (f32[128,1024]{1,0:T(8,128)S(1)}, f32[128,1024]{1,0:T(8,128)S(1)}) custom-call(s32[1]{0:T(128)} %bitcast.place, bf16[128,4096]{1,0:T(8,128)(2,1)S(1)} %bitcast.12, bf16[128,4096]{1,0:T(8,128)(2,1)S(1)} %collective-permute-done.other_tokens, bf16[128,4096]{1,0:T(8,128)(2,1)S(1)} %bitcast.24, ...), custom_call_target="tpu_custom_call" | custom-call | flops 805306368 | bytes 8388612 | tf_op jit(solution)/shard_map/pallas_call | solution.py:28
  57.9 11.8 %collective-permute-done.3.rest_0_.w3 = bf16[512,1024]{1,0:T(8,128)(2,1)} collective-permute-done((bf16[512,1024]{1,0:T(8,128)(2,1)}, bf16[512,1024]{1,0:T(8,128)(2,1)}, u32[]{:S(2)}, u32[]{:S(2)}) %collective-permute-start.3) | collective-permute-done | bytes 1048608 | tf_op jit(solution)/shard_map/ppermute | solution.py:276
  69.8 2.1 %shard_map.98 = (f32[128,1024]{1,0:T(8,128)S(1)}, f32[128,1024]{1,0:T(8,128)S(1)}) custom-call(s32[1]{0:T(128)} %bitcast.place, bf16[128,4096]{1,0:T(8,128)(2,1)S(1)} %bitcast.13, bf16[128,4096]{1,0:T(8,128)(2,1)S(1)} %collective-permute-done.other_tokens, bf16[128,4096]{1,0:T(8,128)(2,1)S(1)} %bitcast.25, ...), custom_call_target="tpu_custom_call" | custom-call | flops 268435456 | bytes 7340036 | tf_op jit(solution)/shard_map/pallas_call | solution.py:28
  73.4 3.7 %all-to-all-done.2 = bf16[16,256,128]{2,1,0:T(8,128)(2,1)} async-done(((bf16[16,256,128]{2,1,0:T(8,128)(2,1)}), bf16[16,256,128]{2,1,0:T(8,128)(2,1)}, u32[]{:S(2)}, u32[]{:S(2)}) %all-to-all-start.2) | async-done | bytes 1048608 | tf_op jit(solution)/shard_map/all_to_all | solution.py:265
  77.2 1.9 %collective-permute-start.7 = (bf16[4096,128]{1,0:T(8,128)(2,1)}, bf16[4096,128]{1,0:T(8,128)(2,1)}, u32[]{:S(2)}, u32[]{:S(2)}) collective-permute-start(bf16[4096,128]{1,0:T(8,128)(2,1)} %bitcast.5.own_at), channel_id=1, source_target_pairs={{0,16},{16,0},{32,48},{48,32},{64,80},{80,64},{96,112},{112,96},{1... | collective-permute-start | bytes 3145736 | tf_op jit(solution)/shard_map/ppermute | solution.py:295
  79.1 2.4 %collective-permute-start.6 = (f32[128,1024]{1,0:T(8,128)}, f32[128,1024]{1,0:T(8,128)}, u32[]{:S(2)}, u32[]{:S(2)}) collective-permute-start(f32[128,1024]{1,0:T(8,128)} %copy-done.13), channel_id=1, source_target_pairs={{0,16},{16,0},{32,48},{48,32},{64,80},{80,64},{96,112},{112,96},{1... | collective-permute-start | bytes 1572872 | tf_op jit(solution)/shard_map/ppermute | solution.py:295
  84.4 6.0 %shard_map.99 = (bf16[128,512]{1,0:T(8,128)(2,1)S(1)}, bf16[2048,256]{1,0:T(8,128)(2,1)S(1)}, bf16[2048,256]{1,0:T(8,128)(2,1)S(1)}) custom-call(s32[1]{0:T(128)} %bitcast.place, s32[1,64]{1,0:T(1,128)S(1)} %copy-done.14, s32[1,8]{1,0:T(1,128)S(1)} %copy-done.15, f32[128,1024]{1,0:T(8,128)S(1)} %copy-done.12, f32[128,1024]{1,0:T(8,128)} %collective-permute-done.6.theirs_at, ...), custom_call_target="tpu_custom_call" | custom-call | flops 1509949440 | bytes 5505316 | tf_op jit(solution)/shard_map/pallas_call | solution.py:28
  90.4 2.3 %collective-permute-start.9 = (bf16[2048,256]{1,0:T(8,128)(2,1)S(1)}, bf16[2048,256]{1,0:T(8,128)(2,1)S(1)}, u32[]{:S(2)}, u32[]{:S(2)}) collective-permute-start(bf16[2048,256]{1,0:T(8,128)(2,1)S(1)} %get-tuple-element.25), channel_id=1, source_target_pairs={{0,16},{16,0},{32,48},{48,32},{64,80},{80,64},{96,112},{112,96},{1... | collective-permute-start | bytes 3145736 | tf_op jit(solution)/shard_map/ppermute | solution.py:295
  92.7 2.3 %collective-permute-done.9 = bf16[2048,256]{1,0:T(8,128)(2,1)S(1)} collective-permute-done((bf16[2048,256]{1,0:T(8,128)(2,1)S(1)}, bf16[2048,256]{1,0:T(8,128)(2,1)S(1)}, u32[]{:S(2)}, u32[]{:S(2)}) %collective-permute-start.9) | collective-permute-done | bytes 1048608 | tf_op jit(solution)/shard_map/ppermute | solution.py:295
  96.2 7.9 %all-to-all-start.3 = ((bf16[16,128,256]{2,1,0:T(8,128)(2,1)}), bf16[16,128,256]{2,1,0:T(8,128)(2,1)}, u32[]{:S(2)}, u32[]{:S(2)}) async-start(bf16[16,128,256]{2,1,0:T(8,128)(2,1)} %bitcast.26), calls=%async_computation.3 | async-start | bytes 2097152 | tf_op jit(solution)/shard_map/all_to_all | solution.py:265
  104.1 2.3 %collective-permute-start.11 = (bf16[4096,128]{1,0:T(8,128)(2,1)S(1)}, bf16[4096,128]{1,0:T(8,128)(2,1)}, u32[]{:S(2)}, u32[]{:S(2)}) collective-permute-start(bf16[4096,128]{1,0:T(8,128)(2,1)S(1)} %bitcast.16), channel_id=1, source_target_pairs={{0,16},{16,0},{32,48},{48,32},{64,80},{80,64},{96,112},{112,96},{1... | collective-permute-start | bytes 3145736 | tf_op jit(solution)/shard_map/ppermute | solution.py:295
  106.4 14.5 %all-to-all-done.3.pieces = bf16[16,128,256]{2,1,0:T(8,128)(2,1)} async-done(((bf16[16,128,256]{2,1,0:T(8,128)(2,1)}), bf16[16,128,256]{2,1,0:T(8,128)(2,1)}, u32[]{:S(2)}, u32[]{:S(2)}) %all-to-all-start.3) | async-done | bytes 1048608 | tf_op jit(solution)/shard_map/all_to_all | solution.py:265
  122.3 3.8 %collective-permute-start.10 = (bf16[128,256]{1,0:T(8,128)(2,1)S(1)}, bf16[128,256]{1,0:T(8,128)(2,1)S(1)}, u32[]{:S(2)}, u32[]{:S(2)}) collective-permute-start(bf16[128,256]{1,0:T(8,128)(2,1)S(1)} %shard_map.100.grads), channel_id=1, source_target_pairs={{0,16},{16,0},{32,48},{48,32},{64,80},{80,64},{96,112},{112,96},{1... | collective-permute-start | bytes 196616 | tf_op jit(solution)/shard_map/ppermute | solution.py:295
  127.5 13.6 %all_to_all.34 = bf16[16,128,128]{2,1,0:T(8,128)(2,1)S(1)} all-to-all(bf16[16,128,128]{2,1,0:T(8,128)(2,1)S(1)} %shard_map.103), channel_id=1, replica_groups={{0,32,64,96,128,160,192,224,256,288,320,352,384,416,448,480},{16,48,80,..., dimensions={0} | all-to-all | bytes 1048576 | tf_op jit(solution)/shard_map/all_to_all | solution.py:265
  141.2 11.5 %collective-permute-start.13 = (bf16[128,128]{1,0:T(8,128)(2,1)S(1)}, bf16[128,128]{1,0:T(8,128)(2,1)S(1)}, u32[]{:S(2)}, u32[]{:S(2)}) collective-permute-start(bf16[128,128]{1,0:T(8,128)(2,1)S(1)} %reduce_sum.21), channel_id=1, source_target_pairs={{0,8},{1,9},{2,10},{3,11},{4,12},{5,13},{6,14},{7,15},{8,0},{9,1},... | collective-permute-start | bytes 98312 | tf_op jit(solution)/shard_map/ppermute | solution.py:350
  152.7 3.9 %collective-permute-start.8 = (bf16[128,512]{1,0:T(8,128)(2,1)S(1)}, bf16[128,512]{1,0:T(8,128)(2,1)S(1)}, u32[]{:S(2)}, u32[]{:S(2)}) collective-permute-start(bf16[128,512]{1,0:T(8,128)(2,1)S(1)} %get-tuple-element.23.grad_query), channel_id=1, source_target_pairs={{0,16},{16,0},{32,48},{48,32},{64,80},{80,64},{96,112},{112,96},{1... | collective-permute-start | bytes 393224 | tf_op jit(solution)/shard_map/ppermute | solution.py:295
  156.7 4.0 %collective-permute-start.14 = (bf16[128,128]{1,0:T(8,128)(2,1)S(1)}, bf16[128,128]{1,0:T(8,128)(2,1)S(1)}, u32[]{:S(2)}, u32[]{:S(2)}) collective-permute-start(bf16[128,128]{1,0:T(8,128)(2,1)S(1)} %add_convert_fusion.2), channel_id=1, source_target_pairs={{0,4},{1,5},{2,6},{3,7},{4,0},{5,1},{6,2},{7,3},{8,12},{9,13},{10,... | collective-permute-start | bytes 98312 | tf_op jit(solution)/shard_map/ppermute | solution.py:350
  160.7 4.0 %shard_map.101 = (bf16[128,2048]{1,0:T(8,128)(2,1)S(1)}, bf16[128,2048]{1,0:T(8,128)(2,1)S(1)}) custom-call(s32[1]{0:T(128)} %bitcast.place, bf16[128,512]{1,0:T(8,128)(2,1)S(1)} %get-tuple-element.23.grad_query, bf16[128,512]{1,0:T(8,128)(2,1)S(1)} %collective-permute-done.8.other_grad_query, bf16[128,256]{1,0:T(8,128)(2,1)S(1)} %shard_map.100.grads, ...), custom_call_target="tpu_custom_call" | custom-call | flops 805306368 | bytes 7733252 | tf_op jit(solution)/shard_map/pallas_call | solution.py:28
  165.5 4.5 %collective-permute-start.12 = (bf16[128,2048]{1,0:T(8,128)(2,1)S(1)}, bf16[128,2048]{1,0:T(8,128)(2,1)S(1)}, u32[]{:S(2)}, u32[]{:S(2)}) collective-permute-start(bf16[128,2048]{1,0:T(8,128)(2,1)S(1)} %get-tuple-element.27), channel_id=1, source_target_pairs={{0,16},{16,0},{32,48},{48,32},{64,80},{80,64},{96,112},{112,96},{1... | collective-permute-start | bytes 1572872 | tf_op jit(solution)/shard_map/ppermute | solution.py:295
  170.7 5.0 %all-to-all-start.5 = ((bf16[4,128,128]{2,1,0:T(8,128)(2,1)}), bf16[4,128,128]{2,1,0:T(8,128)(2,1)S(1)}, u32[]{:S(2)}, u32[]{:S(2)}) async-start(bf16[4,128,128]{2,1,0:T(8,128)(2,1)} %broadcast_in_dim.30), calls=%async_computation.5 | async-start | bytes 262144 | tf_op jit(solution)/shard_map/all_to_all | solution.py:355
  178.0 2.6 %all-to-all-done.5 = bf16[4,128,128]{2,1,0:T(8,128)(2,1)S(1)} async-done(((bf16[4,128,128]{2,1,0:T(8,128)(2,1)}), bf16[4,128,128]{2,1,0:T(8,128)(2,1)S(1)}, u32[]{:S(2)}, u32[]{:S(2)}) %all-to-all-start.5) | async-done | bytes 131104 | tf_op jit(solution)/shard_map/all_to_all | solution.py:355
  (77 shorter events, 21.8 us)
Async XLA Ops:
  3.9 5.2 %copy-start.19 = (bf16[128,128]{1,0:T(8,128)(2,1)S(1)}, bf16[128,128]{1,0:T(8,128)(2,1)}, u32[]{:S(2)}) copy-start(bf16[128,128]{1,0:T(8,128)(2,1)} %param.12) | copy-start | bytes 98308
  3.9 5.2 %copy-start.20 = (bf16[128,128]{1,0:T(8,128)(2,1)S(1)}, bf16[128,128]{1,0:T(8,128)(2,1)}, u32[]{:S(2)}) copy-start(bf16[128,128]{1,0:T(8,128)(2,1)} %param.11) | copy-start | bytes 98308
  3.9 12.5 %copy-start = (bf16[1,128,4096]{2,1,0:T(8,128)(2,1)S(1)}, bf16[1,128,4096]{2,1,0:T(8,128)(2,1)}, u32[]{:S(2)}) copy-start(bf16[1,128,4096]{2,1,0:T(8,128)(2,1)} %param.8) | copy-start | bytes 3145732
  3.9 14.9 %all-to-all-start = ((bf16[4,128,1024]{2,1,0:T(8,128)(2,1)}), bf16[4,128,1024]{2,1,0:T(8,128)(2,1)S(1)}, u32[]{:S(2)}, u32[]{:S(2)}) async-start(bf16[4,128,1024]{2,1,0:T(8,128)(2,1)} %shard_map.95), calls=%async_computation | async-start | bytes 2097152 | tf_op jit(solution)/shard_map/all_to_all | solution.py:283
  9.1 9.3 %collective-permute-start.1 = (bf16[128,128]{1,0:T(8,128)(2,1)S(1)}, bf16[128,128]{1,0:T(8,128)(2,1)S(1)}, u32[]{:S(2)}, u32[]{:S(2)}) collective-permute-start(bf16[128,128]{1,0:T(8,128)(2,1)S(1)} %broadcast_select_fusion.2), channel_id=1, source_target_pairs={{0,16},{16,0},{32,48},{48,32},{64,80},{80,64},{96,112},{112,96},{1... | collective-permute-start | bytes 98312 | tf_op jit(solution)/shard_map/ppermute | solution.py:295
  16.5 27.1 %collective-permute-start = (bf16[128,4096]{1,0:T(8,128)(2,1)S(1)}, bf16[128,4096]{1,0:T(8,128)(2,1)S(1)}, u32[]{:S(2)}, u32[]{:S(2)}) collective-permute-start(bf16[128,4096]{1,0:T(8,128)(2,1)S(1)} %bitcast.10), channel_id=1, source_target_pairs={{0,16},{16,0},{32,48},{48,32},{64,80},{80,64},{96,112},{112,96},{1... | collective-permute-start | bytes 3145736 | tf_op jit(solution)/shard_map/ppermute | solution.py:295
  18.8 1.3 copy-start.1
  20.2 12.2 %copy-start.14 = (s32[1,64]{1,0:T(1,128)S(1)}, s32[1,64]{1,0:T(1,128)}, u32[]{:S(2)}) copy-start(s32[1,64]{1,0:T(1,128)} %order.1) | copy-start | bytes 772
  20.2 23.5 %all-to-all-start.1 = ((bf16[16,256,128]{2,1,0:T(8,128)(2,1)}), bf16[16,256,128]{2,1,0:T(8,128)(2,1)S(1)}, u32[]{:S(2)}, u32[]{:S(2)}) async-start(bf16[16,256,128]{2,1,0:T(8,128)(2,1)} %broadcast_in_dim.13), calls=%async_computation.1 | async-start | bytes 2097152 | tf_op jit(solution)/shard_map/all_to_all | solution.py:265
  25.1 25.8 %collective-permute-start.2 = (bf16[128,4096]{1,0:T(8,128)(2,1)}, bf16[128,4096]{1,0:T(8,128)(2,1)}, u32[]{:S(2)}, u32[]{:S(2)}) collective-permute-start(bf16[128,4096]{1,0:T(8,128)(2,1)} %bitcast.23), channel_id=1, source_target_pairs={{0,16},{16,0},{32,48},{48,32},{64,80},{80,64},{96,112},{112,96},{1... | collective-permute-start | bytes 3145736 | tf_op jit(solution)/shard_map/ppermute | solution.py:295
  32.6 19.8 %collective-permute-start.4 = (bf16[512,1024]{1,0:T(8,128)(2,1)}, bf16[512,1024]{1,0:T(8,128)(2,1)}, u32[]{:S(2)}, u32[]{:S(2)}) collective-permute-start(bf16[512,1024]{1,0:T(8,128)(2,1)} %bitcast.18), channel_id=1, source_target_pairs={{0,128},{16,48},{32,160},{48,80},{64,192},{80,112},{96,224},{112,1... | collective-permute-start | bytes 3145736 | tf_op jit(solution)/shard_map/ppermute | solution.py:276
  36.1 16.4 %collective-permute-start.5 = (bf16[512,1024]{1,0:T(8,128)(2,1)}, bf16[512,1024]{1,0:T(8,128)(2,1)}, u32[]{:S(2)}, u32[]{:S(2)}) collective-permute-start(bf16[512,1024]{1,0:T(8,128)(2,1)} %bitcast.19), channel_id=1, source_target_pairs={{0,384},{16,112},{32,416},{48,16},{64,448},{80,48},{96,480},{112,8... | collective-permute-start | bytes 3145736 | tf_op jit(solution)/shard_map/ppermute | solution.py:276
  39.8 3.8 %copy-start.16 = (f32[256,64]{1,0:T(8,128)}, f32[256,64]{1,0:T(8,128)S(1)}, u32[]{:S(2)}) copy-start(f32[256,64]{1,0:T(8,128)S(1)} %get-tuple-element.31) | copy-start | bytes 196612
  39.8 3.8 %copy-start.18 = (f32[256,64]{1,0:T(8,128)}, f32[256,64]{1,0:T(8,128)S(1)}, u32[]{:S(2)}) copy-start(f32[256,64]{1,0:T(8,128)S(1)} %get-tuple-element.32) | copy-start | bytes 196612
  39.8 30.0 %collective-permute-start.3 = (bf16[512,1024]{1,0:T(8,128)(2,1)}, bf16[512,1024]{1,0:T(8,128)(2,1)}, u32[]{:S(2)}, u32[]{:S(2)}) collective-permute-start(bf16[512,1024]{1,0:T(8,128)(2,1)} %bitcast.20), channel_id=1, source_target_pairs={{0,256},{16,80},{32,288},{48,112},{64,320},{80,16},{96,352},{112,4... | collective-permute-start | bytes 3145736 | tf_op jit(solution)/shard_map/ppermute | solution.py:276
  45.4 31.7 %all-to-all-start.2 = ((bf16[16,256,128]{2,1,0:T(8,128)(2,1)}), bf16[16,256,128]{2,1,0:T(8,128)(2,1)}, u32[]{:S(2)}, u32[]{:S(2)}) async-start(bf16[16,256,128]{2,1,0:T(8,128)(2,1)} %copy-done.4), calls=%async_computation.2 | async-start | bytes 2097152 | tf_op jit(solution)/shard_map/all_to_all | solution.py:265
  52.5 1.2 copy-start.2
  54.9 14.8 %copy-start.6 = (bf16[1,128,4096]{2,1,0:T(8,128)(2,1)S(1)}, bf16[1,128,4096]{2,1,0:T(8,128)(2,1)}, u32[]{:S(2)}) copy-start(bf16[1,128,4096]{2,1,0:T(8,128)(2,1)} %param.9) | copy-start | bytes 3145732
  69.8 11.7 %copy-start.17 = (f32[256,64]{1,0:T(8,128)S(1)}, f32[256,64]{1,0:T(8,128)}, u32[]{:S(2)}) copy-start(f32[256,64]{1,0:T(8,128)} %copy-done.16) | copy-start | bytes 196612
  69.8 13.6 %copy-start.15 = (s32[1,8]{1,0:T(1,128)S(1)}, s32[1,8]{1,0:T(1,128)}, u32[]{:S(2)}) copy-start(s32[1,8]{1,0:T(1,128)} %lengths.1) | copy-start | bytes 100
  77.2 6.2 %collective-permute-start.7 = (bf16[4096,128]{1,0:T(8,128)(2,1)}, bf16[4096,128]{1,0:T(8,128)(2,1)}, u32[]{:S(2)}, u32[]{:S(2)}) collective-permute-start(bf16[4096,128]{1,0:T(8,128)(2,1)} %bitcast.5.own_at), channel_id=1, source_target_pairs={{0,16},{16,0},{32,48},{48,32},{64,80},{80,64},{96,112},{112,96},{1... | collective-permute-start | bytes 3145736 | tf_op jit(solution)/shard_map/ppermute | solution.py:295
  79.1 4.3 %collective-permute-start.6 = (f32[128,1024]{1,0:T(8,128)}, f32[128,1024]{1,0:T(8,128)}, u32[]{:S(2)}, u32[]{:S(2)}) collective-permute-start(f32[128,1024]{1,0:T(8,128)} %copy-done.13), channel_id=1, source_target_pairs={{0,16},{16,0},{32,48},{48,32},{64,80},{80,64},{96,112},{112,96},{1... | collective-permute-start | bytes 1572872 | tf_op jit(solution)/shard_map/ppermute | solution.py:295
  90.4 4.6 %collective-permute-start.9 = (bf16[2048,256]{1,0:T(8,128)(2,1)S(1)}, bf16[2048,256]{1,0:T(8,128)(2,1)S(1)}, u32[]{:S(2)}, u32[]{:S(2)}) collective-permute-start(bf16[2048,256]{1,0:T(8,128)(2,1)S(1)} %get-tuple-element.25), channel_id=1, source_target_pairs={{0,16},{16,0},{32,48},{48,32},{64,80},{80,64},{96,112},{112,96},{1... | collective-permute-start | bytes 3145736 | tf_op jit(solution)/shard_map/ppermute | solution.py:295
  96.2 24.7 %all-to-all-start.3 = ((bf16[16,128,256]{2,1,0:T(8,128)(2,1)}), bf16[16,128,256]{2,1,0:T(8,128)(2,1)}, u32[]{:S(2)}, u32[]{:S(2)}) async-start(bf16[16,128,256]{2,1,0:T(8,128)(2,1)} %bitcast.26), calls=%async_computation.3 | async-start | bytes 2097152 | tf_op jit(solution)/shard_map/all_to_all | solution.py:265
  104.1 56.6 %collective-permute-start.11 = (bf16[4096,128]{1,0:T(8,128)(2,1)S(1)}, bf16[4096,128]{1,0:T(8,128)(2,1)}, u32[]{:S(2)}, u32[]{:S(2)}) collective-permute-start(bf16[4096,128]{1,0:T(8,128)(2,1)S(1)} %bitcast.16), channel_id=1, source_target_pairs={{0,16},{16,0},{32,48},{48,32},{64,80},{80,64},{96,112},{112,96},{1... | collective-permute-start | bytes 3145736 | tf_op jit(solution)/shard_map/ppermute | solution.py:295
  122.3 4.7 %collective-permute-start.10 = (bf16[128,256]{1,0:T(8,128)(2,1)S(1)}, bf16[128,256]{1,0:T(8,128)(2,1)S(1)}, u32[]{:S(2)}, u32[]{:S(2)}) collective-permute-start(bf16[128,256]{1,0:T(8,128)(2,1)S(1)} %shard_map.100.grads), channel_id=1, source_target_pairs={{0,16},{16,0},{32,48},{48,32},{64,80},{80,64},{96,112},{112,96},{1... | collective-permute-start | bytes 196616 | tf_op jit(solution)/shard_map/ppermute | solution.py:295
  127.5 33.2 %copy-start.3 = (bf16[4,128,1024]{2,1,0:T(8,128)(2,1)S(1)}, bf16[4,128,1024]{2,1,0:T(8,128)(2,1)}, u32[]{:S(2)}) copy-start(bf16[4,128,1024]{2,1,0:T(8,128)(2,1)} %copy-done.1) | copy-start | bytes 3145732
  141.2 15.5 %collective-permute-start.13 = (bf16[128,128]{1,0:T(8,128)(2,1)S(1)}, bf16[128,128]{1,0:T(8,128)(2,1)S(1)}, u32[]{:S(2)}, u32[]{:S(2)}) collective-permute-start(bf16[128,128]{1,0:T(8,128)(2,1)S(1)} %reduce_sum.21), channel_id=1, source_target_pairs={{0,8},{1,9},{2,10},{3,11},{4,12},{5,13},{6,14},{7,15},{8,0},{9,1},... | collective-permute-start | bytes 98312 | tf_op jit(solution)/shard_map/ppermute | solution.py:350
  152.7 8.0 %collective-permute-start.8 = (bf16[128,512]{1,0:T(8,128)(2,1)S(1)}, bf16[128,512]{1,0:T(8,128)(2,1)S(1)}, u32[]{:S(2)}, u32[]{:S(2)}) collective-permute-start(bf16[128,512]{1,0:T(8,128)(2,1)S(1)} %get-tuple-element.23.grad_query), channel_id=1, source_target_pairs={{0,16},{16,0},{32,48},{48,32},{64,80},{80,64},{96,112},{112,96},{1... | collective-permute-start | bytes 393224 | tf_op jit(solution)/shard_map/ppermute | solution.py:295
  156.7 13.3 %collective-permute-start.14 = (bf16[128,128]{1,0:T(8,128)(2,1)S(1)}, bf16[128,128]{1,0:T(8,128)(2,1)S(1)}, u32[]{:S(2)}, u32[]{:S(2)}) collective-permute-start(bf16[128,128]{1,0:T(8,128)(2,1)S(1)} %add_convert_fusion.2), channel_id=1, source_target_pairs={{0,4},{1,5},{2,6},{3,7},{4,0},{5,1},{6,2},{7,3},{8,12},{9,13},{10,... | collective-permute-start | bytes 98312 | tf_op jit(solution)/shard_map/ppermute | solution.py:350
  165.5 10.2 %collective-permute-start.12 = (bf16[128,2048]{1,0:T(8,128)(2,1)S(1)}, bf16[128,2048]{1,0:T(8,128)(2,1)S(1)}, u32[]{:S(2)}, u32[]{:S(2)}) collective-permute-start(bf16[128,2048]{1,0:T(8,128)(2,1)S(1)} %get-tuple-element.27), channel_id=1, source_target_pairs={{0,16},{16,0},{32,48},{48,32},{64,80},{80,64},{96,112},{112,96},{1... | collective-permute-start | bytes 1572872 | tf_op jit(solution)/shard_map/ppermute | solution.py:295
  170.7 9.9 %all-to-all-start.5 = ((bf16[4,128,128]{2,1,0:T(8,128)(2,1)}), bf16[4,128,128]{2,1,0:T(8,128)(2,1)S(1)}, u32[]{:S(2)}, u32[]{:S(2)}) async-start(bf16[4,128,128]{2,1,0:T(8,128)(2,1)} %broadcast_in_dim.30), calls=%async_computation.5 | async-start | bytes 262144 | tf_op jit(solution)/shard_map/all_to_all | solution.py:355
  (9 other events, 8.5 us)

commit v4 on v3

--- a/solution.py
+++ b/solution.py
@@ -1,4 +1,3 @@
-import functools
 import math
 
 import jax
@@ -12,7 +11,7 @@
 NEG = -1e30
 BLOCK = 64
 LONGEST = 1024
-RING = (0, -1, 1, 2)
+RING = (0, 2, -1, 1)
 BF16 = jnp.bfloat16
 F32 = jnp.float32
 NT = (((1,), (1,)), ((), ()))
@@ -23,13 +22,13 @@
 HBM = pl.BlockSpec(memory_space=pltpu.HBM)
 
 
-def call(body, outs, in_specs, args, flops, scratch=(), limit=24):
+def call(body, outs, in_specs, args, flops, scratch=(), limit=24, out_specs=None):
     moved = sum(math.prod(a.shape) * a.dtype.itemsize for a in list(args) + list(outs))
     return pl.pallas_call(
         body,
         out_shape=outs,
         in_specs=in_specs,
-        out_specs=[VMEM] * len(outs),
+        out_specs=out_specs or [VMEM] * len(outs),
         scratch_shapes=list(scratch),
         compiler_params=pltpu.CompilerParams(vmem_limit_bytes=limit << 20),
         cost_estimate=pl.CostEstimate(flops=flops, bytes_accessed=moved, transcendentals=0),
@@ -60,16 +59,30 @@
     return copies
 
 
-def pack_kernel(query_weight, out_weight, out, query, turned, arrived):
+def write_copies(source, out, done):
+    copies = [pltpu.make_async_copy(source, out.at[i], done.at[i]) for i in range(out.shape[0])]
+    for copy in copies:
+        copy.start()
+    for copy in copies:
+        copy.wait()
+
+
+def pack_kernel(query_weight, out_weight, out, packed, turned, arrived, done):
     width = query_weight.shape[1]
-    copies = fetch((query_weight, out_weight), (query, turned), arrived)
+    copies = fetch((query_weight, out_weight), (packed.at[:, :width], turned), arrived)
+    copies[1].wait()
+    packed[:, width:] = turned[...].T
     copies[0].wait()
-    for copy in range(out.shape[0]):
-        out[copy, :, :width] = query[...]
-    copies[1].wait()
-    columns = turned[...].T
-    for copy in range(out.shape[0]):
-        out[copy, :, width:] = columns
+    write_copies(packed, out, done)
+
+
+def spread_kernel(place, key_weight, value_weight, received, out, held, done):
+    rows = key_weight.shape[0]
+    core = place[0] % 2
+    held[pl.ds(pl.multiple_of(core * rows, rows), rows), :] = jnp.where(
+        core == 0, key_weight[...], value_weight[...])
+    held[pl.ds(pl.multiple_of((1 - core) * rows, rows), rows), :] = received[...]
+    write_copies(held, out, done)
 
 
 def shard_order(core, chip, side):
@@ -83,41 +96,51 @@
     return order
 
 
-def partial_kernel(place, tokens, other_tokens, upstream, other_upstream, *rest, begin):
-    pieces, (mine, theirs) = rest[:-2], rest[-2:]
-    added = pieces[-2:] if begin else ()
-    pieces = pieces[:-2] if begin else pieces
-    rows, features = tokens.shape
-    width = mine.shape[1] // 2
+def partial_sums(place, sources, pieces, added, outs, begin, finished=None):
+    rows, features = sources[0].shape
+    width = outs[0].shape[1] // 2
     side = math.isqrt(features // (2 * rows))
     shards = shard_order(place[0] % 2, place[0] // 2, side)
-    for source, start, which, out in ((other_tokens, 0, 1, theirs), (other_upstream, width, 1, theirs),
-                                      (tokens, 0, 0, mine), (upstream, width, 0, mine)):
-        total = added[which][:, start:start + width] if begin else jnp.zeros((rows, width), F32)
-        for n in range(0, side * len(pieces), 2):
-            piece, at = pieces[n // side], (n % side) * rows
-            columns = [pl.ds(pl.multiple_of(shards[begin * side + n + i] * rows, rows), rows) for i in range(2)]
-            t = jnp.concatenate([source[:, here] for here in columns], axis=1)
-            total += lax.dot_general(t, piece[at:at + 2 * rows, start:start + width], NN,
-                                     preferred_element_type=F32)
-        out[:, start:start + width] = total
-
-
-def project_kernel(place, tokens, other_tokens, weight, cosine, sine, out):
+    for which in (1, 0):
+        for source, start in zip(sources[2 * which:], (0, width)):
+            total = added[which][:, start:start + width] if begin else jnp.zeros((rows, width), F32)
+            for n in range(0, side * len(pieces), 2):
+                piece, at = pieces[n // side], (n % side) * rows
+                columns = [pl.ds(pl.multiple_of(shards[begin * side + n + i] * rows, rows), rows) for i in range(2)]
+                t = jnp.concatenate([source[:, here] for here in columns], axis=1)
+                total += lax.dot_general(t, piece[at:at + 2 * rows, start:start + width], NN,
+                                         preferred_element_type=F32)
+            outs[which][:, start:start + width] = total
+        if which and finished:
+            finished()
+
+
+def first_partial_kernel(place, tokens, upstream, other_tokens, other_upstream, w0, w1, w2, mine, theirs):
+    partial_sums(place, (tokens, upstream, other_tokens, other_upstream), (w0, w1, w2), None, (mine, theirs), 0)
+
+
+def last_partial_kernel(place, tokens, upstream, other_tokens, other_upstream, w3, mine_before, theirs_before,
+                        mine, theirs_out, theirs, done):
+    copy = pltpu.make_async_copy(theirs, theirs_out, done)
+    partial_sums(place, (tokens, upstream, other_tokens, other_upstream), (w3,), (mine_before, theirs_before),
+                 (mine, theirs), 3, copy.start)
+    copy.wait()
+
+
+def project_kernel(place, tokens, other_tokens, weight, cosine, sine, out, held, done):
     rows = tokens.shape[0]
     own_core = place[0] % 2
     for source, core in ((tokens, own_core), (other_tokens, 1 - own_core)):
         here = pl.ds(pl.multiple_of(core * rows, rows), rows)
         v = lax.dot_general(source[...], weight[...], NN, preferred_element_type=F32)
-        v = (v * cosine[here, :] + swap_halves(v) * sine[here, :]).astype(BF16)
-        for chip in range(out.shape[0]):
-            out[chip, here, :] = v
-
-
-def attention_kernel(place, order, lengths, mine_at, theirs_at, own_at, other_at, cosine, sine,
+        held[here, :] = (v * cosine[here, :] + swap_halves(v) * sine[here, :]).astype(BF16)
+    write_copies(held, out, done)
+
+
+def attention_kernel(place, order, lengths, mine, theirs_at, own_at, other_at, cosine, sine,
                      grad_query, kept, sent, q_ref, a_ref, key_window, value_window, total, stored_at,
-                     mine, theirs, own_part, other_part, arrived):
-    copies = fetch((mine_at, theirs_at, own_at, other_at), (mine, theirs, own_part, other_part), arrived)
+                     theirs, own_part, other_part, arrived):
+    copies = fetch((theirs_at, own_at, other_at), (theirs, own_part, other_part), arrived)
     rows = mine.shape[0]
     head = cosine.shape[1]
     heads = q_ref.shape[1] // head
@@ -134,6 +157,8 @@
 
     lax.fori_loop(0, blocks, invert, 0)
     width = heads * head
+    kept[...] = jnp.zeros_like(kept)
+    sent[...] = jnp.zeros_like(sent)
     total[...] = jnp.zeros_like(total)
     for copy in copies:
         copy.wait()
@@ -191,8 +216,22 @@
             u = u * c[r0:r0 + BLOCK] - swap_halves(u) * s[r0:r0 + BLOCK]
             grad_query[r0:r0 + BLOCK, h * head:(h + 1) * head] = u.astype(BF16)
     half = seq // 2
-    kept[...] = total[:half].astype(BF16)
-    sent[...] = total[half:].astype(BF16)
+    for j in range(rows // BLOCK):
+        first = order[0, own * (rows // BLOCK) + j] - (span - 1)
+        for w in range(span):
+            spot = stored_at[jnp.maximum(first + w, 0)]
+            device = spot // 2
+            at = pl.multiple_of((device // 2) * (2 * BLOCK) + (spot % 2) * BLOCK, BLOCK)
+            stays = device % 2 == own_core
+            block = total[pl.ds(pl.multiple_of(jnp.where(stays, at, half + at), BLOCK), BLOCK), :].astype(BF16)
+
+            @pl.when(stays)
+            def _():
+                kept[pl.ds(at, BLOCK), :] = block
+
+            @pl.when(jnp.logical_not(stays))
+            def _():
+                sent[pl.ds(at, BLOCK), :] = block
 
 
 def owner_kernel(pieces, cosine, sine, grad_key_value):
@@ -278,8 +317,9 @@
     rings = [[(row * side + i) * 2 for i in range(side)] for row in range(side)]
     rings += [[(i * side + column) * 2 + 1 for i in range(side)] for column in range(side)]
     (packed,) = call(pack_kernel, [shape((side, rows, 2 * width))], [HBM] * 2, (query_weight, out_weight), 0,
-                     scratch=[pltpu.VMEM((rows, width), BF16), pltpu.VMEM((width, rows), BF16),
-                              pltpu.SemaphoreType.DMA((2,))])
+                     scratch=[pltpu.VMEM((rows, 2 * width), BF16), pltpu.VMEM((width, rows), BF16),
+                              pltpu.SemaphoreType.DMA((2,)), pltpu.SemaphoreType.DMA((side,))],
+                     limit=60, out_specs=[HBM])
     line = lax.all_to_all(packed, "ctx", 0, 0, tiled=True, axis_index_groups=rings).reshape(side * rows, 2 * width)
     held = [line] + [moved(line, 1, -offset) for offset in RING[1:]]
 
@@ -294,24 +334,26 @@
     def swap(v):
         return lax.ppermute(v, "ctx", other)
 
-    mine = jnp.where(is_key, key_weight, value_weight)
-    theirs = swap(jnp.where(is_key, value_weight, key_weight))
-    chip_weight = jnp.concatenate([jnp.where(is_key, mine, theirs), jnp.where(is_key, theirs, mine)], axis=0)
-    copies, _ = lax.optimization_barrier(
-        (jnp.broadcast_to(chip_weight[None], (chips,) + chip_weight.shape), line))
+    (copies,) = call(
+        spread_kernel, [shape((chips, 2 * rows, head))], [SMEM] + [VMEM] * 3,
+        (place, key_weight, value_weight, swap(jnp.where(is_key, value_weight, key_weight))), 0,
+        scratch=[pltpu.VMEM((2 * rows, head), BF16), pltpu.SemaphoreType.DMA((chips,))], out_specs=[HBM])
+    copies, _ = lax.optimization_barrier((copies, line))
     own_weight = to_chips(copies).reshape(features, head)
     other_tokens = swap(tokens)
     (projected,) = call(
         project_kernel, [shape((chips, 2 * rows, head))], [SMEM] + [VMEM] * 5,
-        (place, tokens, other_tokens, own_weight, own_cosine, own_sine), 4 * rows * features * head)
-    sources = (place, tokens, other_tokens, upstream, swap(upstream))
+        (place, tokens, other_tokens, own_weight, own_cosine, own_sine), 4 * rows * features * head,
+        scratch=[pltpu.VMEM((2 * rows, head), BF16), pltpu.SemaphoreType.DMA((chips,))], out_specs=[HBM])
+    sources = (place, tokens, upstream, other_tokens, swap(upstream))
     halves = [shape((rows, 2 * width), F32)] * 2
     mine, theirs = call(
-        functools.partial(partial_kernel, begin=0), halves, [SMEM] + [VMEM] * 7,
+        first_partial_kernel, halves, [SMEM] + [VMEM] * 7,
         sources + tuple(held[:3]), 3 * rows * features * width)
     mine, theirs = call(
-        functools.partial(partial_kernel, begin=3), halves, [SMEM] + [VMEM] * 7,
-        sources + (held[3], mine, theirs), rows * features * width)
+        last_partial_kernel, halves, [SMEM] + [VMEM] * 7,
+        sources + (held[3], mine, theirs), rows * features * width,
+        scratch=[pltpu.VMEM((rows, 2 * width), F32), pltpu.SemaphoreType.DMA], out_specs=[VMEM, HBM])
     own_part = to_chips(projected).reshape(seq, head)
     own_part, mine, theirs = lax.optimization_barrier((own_part, mine, theirs))
     received = swap(theirs)
@@ -321,17 +363,18 @@
     grad_query, kept, sent = call(
         attention_kernel,
         [shape((rows, width)), shape((seq // 2, 2 * head)), shape((seq // 2, 2 * head))],
-        [SMEM] * 3 + [HBM] * 4 + [VMEM] * 2,
+        [SMEM] * 3 + [VMEM] + [HBM] * 3 + [VMEM] * 2,
         (place, block_order, doc_lengths, mine, received, own_part, other_part, cosine, sine),
         20 * rows * heads * window * head,
         scratch=[pltpu.VMEM((rows, width), BF16), pltpu.VMEM((rows, width), BF16),
                  pltpu.VMEM((window, head), BF16), pltpu.VMEM((window, head), BF16),
                  pltpu.VMEM((seq, 2 * head), F32), pltpu.SMEM((seq // BLOCK,), jnp.int32),
-                 pltpu.VMEM((rows, 2 * width), F32), pltpu.VMEM((rows, 2 * width), F32),
+                 pltpu.VMEM((rows, 2 * width), F32),
                  pltpu.VMEM((seq, head), BF16), pltpu.VMEM((seq, head), BF16), pltpu.SemaphoreType.DMA((4,))],
         limit=28)
     pairs = (kept.astype(F32) + swap(sent).astype(F32)).astype(BF16)
-    pieces = to_chips(pairs).reshape(chips, rows, 2 * head)
+    pieces, other_grad_query, other_weight = lax.optimization_barrier(
+        (to_chips(pairs).reshape(chips, rows, 2 * head), swap(grad_query), other_weight))
     (grads,) = call(owner_kernel, [shape((rows, 2 * head))], [VMEM] * 3, (pieces, cosine, sine), 0)
     other_grads = swap(grads)
     (parts,) = call(
@@ -339,12 +382,10 @@
         (place, tokens, other_tokens, grads, other_grads), 2 * rows * features * head)
     input_mine, input_theirs = call(
         input_kernel, [shape((rows, features // 2))] * 2, [SMEM] + [VMEM] * 10,
-        (place, grad_query, swap(grad_query), grads, other_grads, own_weight, other_weight, *held),
+        (place, grad_query, other_grad_query, grads, other_grads, own_weight, other_weight, *held),
         2 * rows * features * (width + 2 * head))
-    (grad_input,) = call(
-        merge_kernel, [shape((rows, features))], [SMEM] + [VMEM] * 2,
-        (place, input_mine, swap(input_theirs)), 0)
-    grad_weight = jnp.sum(to_chips(parts).reshape(chips, rows, head).astype(F32), axis=0)
+    gathered, input_theirs = lax.optimization_barrier((to_chips(parts), input_theirs))
+    grad_weight = jnp.sum(gathered.reshape(chips, rows, head).astype(F32), axis=0)
     group, step = dp, dp // 2
     while group > 4 and group % 2 == 0:
         sent_on = lax.ppermute(grad_weight.astype(BF16), "dp", [(i, i ^ step) for i in range(dp)])
@@ -354,6 +395,9 @@
     spread = jnp.broadcast_to(grad_weight.astype(BF16)[None], (group, rows, head))
     gathered = lax.all_to_all(spread, "dp", 0, 0, tiled=True, axis_index_groups=near)
     grad_weight = jnp.sum(gathered.reshape(group, rows, head).astype(F32), axis=0)
+    (grad_input,) = call(
+        merge_kernel, [shape((rows, features))], [SMEM] + [VMEM] * 2,
+        (place, input_mine, swap(input_theirs)), 0)
     return grad_input[None], grad_weight
 
 

time: 183 us -> 183 us (level)
  Pallas kernels: 20.4 us -> 25.3 us
  blocking collectives: 13.6 us -> 9.44 us
    all_to_all x1 -> x0, starting transfers between devices: 4.98 us -> none  [on_device(): lax.all_to_all(spread, 'dp', 0, 0, tiled=True, axis_index_groups=near)]
    pallas_call x9 -> x10, Pallas kernels: 20.4 us -> 25.3 us  [call(): pl.pallas_call(body, out_shape=outs, in_specs=in_specs, out_specs=out_spe...]
    all_to_all x1, blocking collectives: 13.6 us -> 9.44 us  [on_device(): lax.all_to_all(spread, 'dp', 0, 0, tiled=True, axis_index_groups=near)]
    all_to_all x1 -> x0, waiting for transfers between devices: 2.62 us -> none  [on_device(): lax.all_to_all(spread, 'dp', 0, 0, tiled=True, axis_index_groups=near)]
    all_to_all x3 -> x4, starting transfers between devices: 18.1 us -> 20.6 us  [to_chips(): lax.all_to_all(pieces, 'ctx', 0, 0, tiled=True, axis_index_groups=planes)]
    unnamed x42 -> x50, local copies, waits for them, and re-layouts: 9.75 us -> 12 us
    ppermute x2, waiting for transfers between devices: 0.01 us -> 2 us  [on_device(): lax.ppermute(grad_weight.astype(BF16), 'dp', [(i, i ^ step) for i in rang...]
    all_to_all x3 -> x4, waiting for transfers between devices: 18.2 us -> 18.7 us  [to_chips(): lax.all_to_all(pieces, 'ctx', 0, 0, tiled=True, axis_index_groups=planes)]
  transfers between devices with their start and end apart: 20 -> 20, of which waited for: 9 -> 11; matrix products, arithmetic and copies ran while one was open for 2% -> 2% of each run, Pallas kernels for 7% -> 7%
where the time goes in v4:
time: 183 us; the launch traced here: 182 us
  starting transfers between devices  90.3 us (49%)
  waiting for transfers between devices  38.6 us (21%)
  Pallas kernels  25.3 us (14%)
  local copies, waits for them, and re-layouts  12.1 us (7%)
  blocking collectives  9.44 us (5%)
  other arithmetic  5.04 us (3%)
    ppermute x10, starting transfers between devices, swap(): return lax.ppermute(v, 'ctx', other)  36.9 us
    pallas_call x10, Pallas kernels, call(): pl.pallas_call(body, out_shape=outs, in_specs=in_specs, out_specs=out_spe...  25.3 us
    all_to_all x4, starting transfers between devices, to_chips(): lax.all_to_all(pieces, 'ctx', 0, 0, tiled=True, axis_index_groups=planes)  20.6 us
    all_to_all x4, waiting for transfers between devices, to_chips(): lax.all_to_all(pieces, 'ctx', 0, 0, tiled=True, axis_index_groups=planes)  18.7 us
    ppermute x2, starting transfers between devices, on_device(): lax.ppermute(grad_weight.astype(BF16), 'dp', [(i, i ^ step) for i in rang...  16.2 us
    ppermute x3, waiting for transfers between devices, moved(): return lax.ppermute(v, 'ctx', pairs)  13.5 us
    unnamed x50, local copies, waits for them, and re-layouts  12 us
    ppermute x3, starting transfers between devices, moved(): return lax.ppermute(v, 'ctx', pairs)  11.4 us
  transfers between devices with their start and end apart: 20, of which 11 were waited for; matrix products, arithmetic and copies ran while one was open for 2% of the time, Pallas kernels for 7%

profile of v4, /device:TPU:1, one launch (start us, length us, event | category | flops | bytes accessed | tf_op | source)
XLA Modules:
  0.0 181.9 jit_solution(8288113076634409325)
XLA Ops:
  0.6 2.1 %shard_map.96 = bf16[4,128,1024]{2,1,0:T(8,128)(2,1)} custom-call(bf16[128,512]{1,0:T(8,128)(2,1)} %query_weight.1, bf16[512,128]{1,0:T(8,128)(2,1)} %out_weight.1), custom_call_target="tpu_custom_call" | custom-call | bytes 1310720 | tf_op jit(solution)/shard_map/pallas_call | solution.py:27
  2.7 5.2 %all-to-all-start = ((bf16[4,128,1024]{2,1,0:T(8,128)(2,1)}), bf16[4,128,1024]{2,1,0:T(8,128)(2,1)S(1)}, u32[]{:S(2)}, u32[]{:S(2)}) async-start(bf16[4,128,1024]{2,1,0:T(8,128)(2,1)} %shard_map.96), calls=%async_computation | async-start | bytes 2097152 | tf_op jit(solution)/shard_map/all_to_all | solution.py:323
  7.9 7.3 %collective-permute-start = (bf16[128,4096]{1,0:T(8,128)(2,1)S(1)}, bf16[128,4096]{1,0:T(8,128)(2,1)S(1)}, u32[]{:S(2)}, u32[]{:S(2)}) collective-permute-start(bf16[128,4096]{1,0:T(8,128)(2,1)S(1)} %bitcast.10), channel_id=1, source_target_pairs={{0,16},{16,0},{32,48},{48,32},{64,80},{80,64},{96,112},{112,96},{1... | collective-permute-start | bytes 3145736 | tf_op jit(solution)/shard_map/ppermute | solution.py:335
  15.3 1.9 %collective-permute-start.1 = (bf16[128,128]{1,0:T(8,128)(2,1)S(1)}, bf16[128,128]{1,0:T(8,128)(2,1)S(1)}, u32[]{:S(2)}, u32[]{:S(2)}) collective-permute-start(bf16[128,128]{1,0:T(8,128)(2,1)S(1)} %broadcast_select_fusion), channel_id=1, source_target_pairs={{0,16},{16,0},{32,48},{48,32},{64,80},{80,64},{96,112},{112,96},{1... | collective-permute-start | bytes 98312 | tf_op jit(solution)/shard_map/ppermute | solution.py:335
  21.9 4.6 %all-to-all-start.1 = ((bf16[16,256,128]{2,1,0:T(8,128)(2,1)}), bf16[16,256,128]{2,1,0:T(8,128)(2,1)S(1)}, u32[]{:S(2)}, u32[]{:S(2)}) async-start(bf16[16,256,128]{2,1,0:T(8,128)(2,1)} %copy-done.5), calls=%async_computation.1 | async-start | bytes 2097152 | tf_op jit(solution)/shard_map/all_to_all | solution.py:304
  26.4 4.3 %collective-permute-start.2 = (bf16[128,4096]{1,0:T(8,128)(2,1)}, bf16[128,4096]{1,0:T(8,128)(2,1)}, u32[]{:S(2)}, u32[]{:S(2)}) collective-permute-start(bf16[128,4096]{1,0:T(8,128)(2,1)} %bitcast.23), channel_id=1, source_target_pairs={{0,16},{16,0},{32,48},{48,32},{64,80},{80,64},{96,112},{112,96},{1... | collective-permute-start | bytes 3145736 | tf_op jit(solution)/shard_map/ppermute | solution.py:335
  31.0 4.9 %collective-permute-start.4 = (bf16[512,1024]{1,0:T(8,128)(2,1)}, bf16[512,1024]{1,0:T(8,128)(2,1)}, u32[]{:S(2)}, u32[]{:S(2)}) collective-permute-start(bf16[512,1024]{1,0:T(8,128)(2,1)} %bitcast.18), channel_id=1, source_target_pairs={{0,256},{16,80},{32,288},{48,112},{64,320},{80,16},{96,352},{112,4... | collective-permute-start | bytes 3145736 | tf_op jit(solution)/shard_map/ppermute | solution.py:315
  35.9 2.2 %collective-permute-start.5 = (bf16[512,1024]{1,0:T(8,128)(2,1)}, bf16[512,1024]{1,0:T(8,128)(2,1)}, u32[]{:S(2)}, u32[]{:S(2)}) collective-permute-start(bf16[512,1024]{1,0:T(8,128)(2,1)} %bitcast.19), channel_id=1, source_target_pairs={{0,128},{16,48},{32,160},{48,80},{64,192},{80,112},{96,224},{112,1... | collective-permute-start | bytes 3145736 | tf_op jit(solution)/shard_map/ppermute | solution.py:315
  38.7 4.3 %collective-permute-start.3 = (bf16[512,1024]{1,0:T(8,128)(2,1)}, bf16[512,1024]{1,0:T(8,128)(2,1)}, u32[]{:S(2)}, u32[]{:S(2)}) collective-permute-start(bf16[512,1024]{1,0:T(8,128)(2,1)} %bitcast.20), channel_id=1, source_target_pairs={{0,384},{16,112},{32,416},{48,16},{64,448},{80,48},{96,480},{112,8... | collective-permute-start | bytes 3145736 | tf_op jit(solution)/shard_map/ppermute | solution.py:315
  43.2 2.3 %shard_map.97 = bf16[16,256,128]{2,1,0:T(8,128)(2,1)S(1)} custom-call(s32[1]{0:T(128)} %bitcast.place, bf16[128,4096]{1,0:T(8,128)(2,1)S(1)} %bitcast.11, bf16[128,4096]{1,0:T(8,128)(2,1)S(1)} %collective-permute-done.other_tokens, bf16[4096,128]{1,0:T(8,128)(2,1)S(1)} %bitcast.15, f32[256,128]{1,0:T(8,128)S(1)} %get-tuple-element.41.cosine, ...), custom_call_target="tpu_custom_call" | custom-call | flops 268435456 | bytes 4456452 | tf_op jit(solution)/shard_map/pallas_call | solution.py:27
  46.5 4.3 %all-to-all-start.2 = ((bf16[16,256,128]{2,1,0:T(8,128)(2,1)}), bf16[16,256,128]{2,1,0:T(8,128)(2,1)}, u32[]{:S(2)}, u32[]{:S(2)}) async-start(bf16[16,256,128]{2,1,0:T(8,128)(2,1)} %copy-done.4), calls=%async_computation.2 | async-start | bytes 2097152 | tf_op jit(solution)/shard_map/all_to_all | solution.py:304
  50.8 2.6 %collective-permute-done.4.w1 = bf16[512,1024]{1,0:T(8,128)(2,1)} collective-permute-done((bf16[512,1024]{1,0:T(8,128)(2,1)}, bf16[512,1024]{1,0:T(8,128)(2,1)}, u32[]{:S(2)}, u32[]{:S(2)}) %collective-permute-start.4) | collective-permute-done | bytes 1048608 | tf_op jit(solution)/shard_map/ppermute | solution.py:315
  53.4 10.9 %collective-permute-done.5.w2 = bf16[512,1024]{1,0:T(8,128)(2,1)} collective-permute-done((bf16[512,1024]{1,0:T(8,128)(2,1)}, bf16[512,1024]{1,0:T(8,128)(2,1)}, u32[]{:S(2)}, u32[]{:S(2)}) %collective-permute-start.5) | collective-permute-done | bytes 1048608 | tf_op jit(solution)/shard_map/ppermute | solution.py:315
  66.7 3.0 %shard_map.98 = (f32[128,1024]{1,0:T(8,128)S(1)}, f32[128,1024]{1,0:T(8,128)S(1)}) custom-call(s32[1]{0:T(128)} %bitcast.place, bf16[128,4096]{1,0:T(8,128)(2,1)S(1)} %bitcast.12, bf16[128,4096]{1,0:T(8,128)(2,1)S(1)} %bitcast.24, bf16[128,4096]{1,0:T(8,128)(2,1)S(1)} %collective-permute-done.other_tokens, ...), custom_call_target="tpu_custom_call" | custom-call | flops 805306368 | bytes 8388612 | tf_op jit(solution)/shard_map/pallas_call | solution.py:27
  69.8 2.3 %shard_map.99 = (f32[128,1024]{1,0:T(8,128)S(1)}, f32[128,1024]{1,0:T(8,128)S(1)}) custom-call(s32[1]{0:T(128)} %bitcast.place, bf16[128,4096]{1,0:T(8,128)(2,1)S(1)} %bitcast.13, bf16[128,4096]{1,0:T(8,128)(2,1)S(1)} %bitcast.25, bf16[128,4096]{1,0:T(8,128)(2,1)S(1)} %collective-permute-done.other_tokens, ...), custom_call_target="tpu_custom_call" | custom-call | flops 268435456 | bytes 7340036 | tf_op jit(solution)/shard_map/pallas_call | solution.py:27
  75.3 5.4 %collective-permute-start.7 = (bf16[4096,128]{1,0:T(8,128)(2,1)}, bf16[4096,128]{1,0:T(8,128)(2,1)}, u32[]{:S(2)}, u32[]{:S(2)}) collective-permute-start(bf16[4096,128]{1,0:T(8,128)(2,1)} %bitcast.5.own_at), channel_id=1, source_target_pairs={{0,16},{16,0},{32,48},{48,32},{64,80},{80,64},{96,112},{112,96},{1... | collective-permute-start | bytes 3145736 | tf_op jit(solution)/shard_map/ppermute | solution.py:335
  80.7 1.9 %collective-permute-start.6 = (f32[128,1024]{1,0:T(8,128)}, f32[128,1024]{1,0:T(8,128)}, u32[]{:S(2)}, u32[]{:S(2)}) collective-permute-start(f32[128,1024]{1,0:T(8,128)} %copy-done.18), channel_id=1, source_target_pairs={{0,16},{16,0},{32,48},{48,32},{64,80},{80,64},{96,112},{112,96},{1... | collective-permute-start | bytes 1572872 | tf_op jit(solution)/shard_map/ppermute | solution.py:335
  85.9 7.0 %shard_map.100 = (bf16[128,512]{1,0:T(8,128)(2,1)S(1)}, bf16[2048,256]{1,0:T(8,128)(2,1)S(1)}, bf16[2048,256]{1,0:T(8,128)(2,1)S(1)}) custom-call(s32[1]{0:T(128)} %bitcast.place, s32[1,64]{1,0:T(1,128)S(1)} %copy-done.19, s32[1,8]{1,0:T(1,128)S(1)} %copy-done.20, f32[128,1024]{1,0:T(8,128)S(1)} %copy-done.17, f32[128,1024]{1,0:T(8,128)} %collective-permute-done.6.theirs_at, ...), custom_call_target="tpu_custom_call" | custom-call | flops 1509949440 | bytes 5505316 | tf_op jit(solution)/shard_map/pallas_call | solution.py:27
  92.9 2.0 %collective-permute-start.8 = (bf16[2048,256]{1,0:T(8,128)(2,1)S(1)}, bf16[2048,256]{1,0:T(8,128)(2,1)S(1)}, u32[]{:S(2)}, u32[]{:S(2)}) collective-permute-start(bf16[2048,256]{1,0:T(8,128)(2,1)S(1)} %get-tuple-element.30), channel_id=1, source_target_pairs={{0,16},{16,0},{32,48},{48,32},{64,80},{80,64},{96,112},{112,96},{1... | collective-permute-start | bytes 3145736 | tf_op jit(solution)/shard_map/ppermute | solution.py:335
  94.9 2.3 %collective-permute-start.10 = (bf16[4096,128]{1,0:T(8,128)(2,1)S(1)}, bf16[4096,128]{1,0:T(8,128)(2,1)}, u32[]{:S(2)}, u32[]{:S(2)}) collective-permute-start(bf16[4096,128]{1,0:T(8,128)(2,1)S(1)} %bitcast.16), channel_id=1, source_target_pairs={{0,16},{16,0},{32,48},{48,32},{64,80},{80,64},{96,112},{112,96},{1... | collective-permute-start | bytes 3145736 | tf_op jit(solution)/shard_map/ppermute | solution.py:335
  98.7 7.1 %all-to-all-start.3 = ((bf16[16,128,256]{2,1,0:T(8,128)(2,1)}), bf16[16,128,256]{2,1,0:T(8,128)(2,1)}, u32[]{:S(2)}, u32[]{:S(2)}) async-start(bf16[16,128,256]{2,1,0:T(8,128)(2,1)} %bitcast.26), calls=%async_computation.3 | async-start | bytes 2097152 | tf_op jit(solution)/shard_map/all_to_all | solution.py:304
  105.9 2.3 %collective-permute-start.9 = (bf16[128,512]{1,0:T(8,128)(2,1)S(1)}, bf16[128,512]{1,0:T(8,128)(2,1)S(1)}, u32[]{:S(2)}, u32[]{:S(2)}) collective-permute-start(bf16[128,512]{1,0:T(8,128)(2,1)S(1)} %get-tuple-element.28.grad_query), channel_id=1, source_target_pairs={{0,16},{16,0},{32,48},{48,32},{64,80},{80,64},{96,112},{112,96},{1... | collective-permute-start | bytes 393224 | tf_op jit(solution)/shard_map/ppermute | solution.py:335
  109.8 12.8 %all-to-all-done.3.pieces = bf16[16,128,256]{2,1,0:T(8,128)(2,1)} async-done(((bf16[16,128,256]{2,1,0:T(8,128)(2,1)}), bf16[16,128,256]{2,1,0:T(8,128)(2,1)}, u32[]{:S(2)}, u32[]{:S(2)}) %all-to-all-start.3) | async-done | bytes 1048608 | tf_op jit(solution)/shard_map/all_to_all | solution.py:304
  124.1 3.8 %collective-permute-start.11 = (bf16[128,256]{1,0:T(8,128)(2,1)S(1)}, bf16[128,256]{1,0:T(8,128)(2,1)S(1)}, u32[]{:S(2)}, u32[]{:S(2)}) collective-permute-start(bf16[128,256]{1,0:T(8,128)(2,1)S(1)} %shard_map.101.grads), channel_id=1, source_target_pairs={{0,16},{16,0},{32,48},{48,32},{64,80},{80,64},{96,112},{112,96},{1... | collective-permute-start | bytes 196616 | tf_op jit(solution)/shard_map/ppermute | solution.py:335
  130.1 4.6 %all-to-all-start.4 = ((bf16[16,128,128]{2,1,0:T(8,128)(2,1)}), bf16[16,128,128]{2,1,0:T(8,128)(2,1)}, u32[]{:S(2)}, u32[]{:S(2)}) async-start(bf16[16,128,128]{2,1,0:T(8,128)(2,1)} %copy-done.8), calls=%async_computation.4 | async-start | bytes 1048576 | tf_op jit(solution)/shard_map/all_to_all | solution.py:304
  135.6 4.0 %shard_map.102 = (bf16[128,2048]{1,0:T(8,128)(2,1)S(1)}, bf16[128,2048]{1,0:T(8,128)(2,1)S(1)}) custom-call(s32[1]{0:T(128)} %bitcast.place, bf16[128,512]{1,0:T(8,128)(2,1)S(1)} %get-tuple-element.28.grad_query, bf16[128,512]{1,0:T(8,128)(2,1)S(1)} %copy-done.12, bf16[128,256]{1,0:T(8,128)(2,1)S(1)} %shard_map.101.grads, ...), custom_call_target="tpu_custom_call" | custom-call | flops 805306368 | bytes 7733252 | tf_op jit(solution)/shard_map/pallas_call | solution.py:27
  141.1 4.3 %all-to-all-done.4 = bf16[16,128,128]{2,1,0:T(8,128)(2,1)} async-done(((bf16[16,128,128]{2,1,0:T(8,128)(2,1)}), bf16[16,128,128]{2,1,0:T(8,128)(2,1)}, u32[]{:S(2)}, u32[]{:S(2)}) %all-to-all-start.4) | async-done | bytes 524320 | tf_op jit(solution)/shard_map/all_to_all | solution.py:304
  146.7 11.5 %collective-permute-start.13 = (bf16[128,128]{1,0:T(8,128)(2,1)S(1)}, bf16[128,128]{1,0:T(8,128)(2,1)S(1)}, u32[]{:S(2)}, u32[]{:S(2)}) collective-permute-start(bf16[128,128]{1,0:T(8,128)(2,1)S(1)} %reduce_sum.21), channel_id=1, source_target_pairs={{0,8},{1,9},{2,10},{3,11},{4,12},{5,13},{6,14},{7,15},{8,0},{9,1},... | collective-permute-start | bytes 98312 | tf_op jit(solution)/shard_map/ppermute | solution.py:391
  158.2 2.0 %collective-permute-done.13 = bf16[128,128]{1,0:T(8,128)(2,1)S(1)} collective-permute-done((bf16[128,128]{1,0:T(8,128)(2,1)S(1)}, bf16[128,128]{1,0:T(8,128)(2,1)S(1)}, u32[]{:S(2)}, u32[]{:S(2)}) %collective-permute-start.13) | collective-permute-done | bytes 32800 | tf_op jit(solution)/shard_map/ppermute | solution.py:391
  160.2 4.8 %collective-permute-start.14 = (bf16[128,128]{1,0:T(8,128)(2,1)S(1)}, bf16[128,128]{1,0:T(8,128)(2,1)S(1)}, u32[]{:S(2)}, u32[]{:S(2)}) collective-permute-start(bf16[128,128]{1,0:T(8,128)(2,1)S(1)} %add_convert_fusion.2), channel_id=1, source_target_pairs={{0,4},{1,5},{2,6},{3,7},{4,0},{5,1},{6,2},{7,3},{8,12},{9,13},{10,... | collective-permute-start | bytes 98312 | tf_op jit(solution)/shard_map/ppermute | solution.py:391
  164.9 5.6 %collective-permute-start.12 = (bf16[128,2048]{1,0:T(8,128)(2,1)}, bf16[128,2048]{1,0:T(8,128)(2,1)S(1)}, u32[]{:S(2)}, u32[]{:S(2)}) collective-permute-start(bf16[128,2048]{1,0:T(8,128)(2,1)} %copy-done.15), channel_id=1, source_target_pairs={{0,16},{16,0},{32,48},{48,32},{64,80},{80,64},{96,112},{112,96},{1... | collective-permute-start | bytes 1572872 | tf_op jit(solution)/shard_map/ppermute | solution.py:335
  170.6 9.4 %all_to_all.34 = bf16[4,128,128]{2,1,0:T(8,128)(2,1)S(1)} all-to-all(bf16[4,128,128]{2,1,0:T(8,128)(2,1)S(1)} %broadcast_in_dim.23), channel_id=1, replica_groups={{0,1,2,3},{4,5,6,7},{8,9,10,11},{12,13,14,15},{16,17,18,19},{20,21,22,2..., dimensions={0} | all-to-all | bytes 262144 | tf_op jit(solution)/shard_map/all_to_all | solution.py:396
  (83 shorter events, 27.8 us)
Async XLA Ops:
  2.7 5.2 %copy-start = (bf16[1,128,4096]{2,1,0:T(8,128)(2,1)S(1)}, bf16[1,128,4096]{2,1,0:T(8,128)(2,1)}, u32[]{:S(2)}) copy-start(bf16[1,128,4096]{2,1,0:T(8,128)(2,1)} %param.8) | copy-start | bytes 3145732
  2.7 12.5 %copy-start.13 = (bf16[128,128]{1,0:T(8,128)(2,1)S(1)}, bf16[128,128]{1,0:T(8,128)(2,1)}, u32[]{:S(2)}) copy-start(bf16[128,128]{1,0:T(8,128)(2,1)} %key_weight.1) | copy-start | bytes 98308
  2.7 12.5 %copy-start.14 = (bf16[128,128]{1,0:T(8,128)(2,1)S(1)}, bf16[128,128]{1,0:T(8,128)(2,1)}, u32[]{:S(2)}) copy-start(bf16[128,128]{1,0:T(8,128)(2,1)} %value_weight.1) | copy-start | bytes 98308
  2.7 18.1 %all-to-all-start = ((bf16[4,128,1024]{2,1,0:T(8,128)(2,1)}), bf16[4,128,1024]{2,1,0:T(8,128)(2,1)S(1)}, u32[]{:S(2)}, u32[]{:S(2)}) async-start(bf16[4,128,1024]{2,1,0:T(8,128)(2,1)} %shard_map.96), calls=%async_computation | async-start | bytes 2097152 | tf_op jit(solution)/shard_map/all_to_all | solution.py:323
  7.9 35.3 %collective-permute-start = (bf16[128,4096]{1,0:T(8,128)(2,1)S(1)}, bf16[128,4096]{1,0:T(8,128)(2,1)S(1)}, u32[]{:S(2)}, u32[]{:S(2)}) collective-permute-start(bf16[128,4096]{1,0:T(8,128)(2,1)S(1)} %bitcast.10), channel_id=1, source_target_pairs={{0,16},{16,0},{32,48},{48,32},{64,80},{80,64},{96,112},{112,96},{1... | collective-permute-start | bytes 3145736 | tf_op jit(solution)/shard_map/ppermute | solution.py:335
  15.3 3.1 %collective-permute-start.1 = (bf16[128,128]{1,0:T(8,128)(2,1)S(1)}, bf16[128,128]{1,0:T(8,128)(2,1)S(1)}, u32[]{:S(2)}, u32[]{:S(2)}) collective-permute-start(bf16[128,128]{1,0:T(8,128)(2,1)S(1)} %broadcast_select_fusion), channel_id=1, source_target_pairs={{0,16},{16,0},{32,48},{48,32},{64,80},{80,64},{96,112},{112,96},{1... | collective-permute-start | bytes 98312 | tf_op jit(solution)/shard_map/ppermute | solution.py:335
  20.9 9.8 %copy-start.19 = (s32[1,64]{1,0:T(1,128)S(1)}, s32[1,64]{1,0:T(1,128)}, u32[]{:S(2)}) copy-start(s32[1,64]{1,0:T(1,128)} %order.1) | copy-start | bytes 772
  21.9 21.3 %all-to-all-start.1 = ((bf16[16,256,128]{2,1,0:T(8,128)(2,1)}), bf16[16,256,128]{2,1,0:T(8,128)(2,1)S(1)}, u32[]{:S(2)}, u32[]{:S(2)}) async-start(bf16[16,256,128]{2,1,0:T(8,128)(2,1)} %copy-done.5), calls=%async_computation.1 | async-start | bytes 2097152 | tf_op jit(solution)/shard_map/all_to_all | solution.py:304
  26.4 24.4 %collective-permute-start.2 = (bf16[128,4096]{1,0:T(8,128)(2,1)}, bf16[128,4096]{1,0:T(8,128)(2,1)}, u32[]{:S(2)}, u32[]{:S(2)}) collective-permute-start(bf16[128,4096]{1,0:T(8,128)(2,1)} %bitcast.23), channel_id=1, source_target_pairs={{0,16},{16,0},{32,48},{48,32},{64,80},{80,64},{96,112},{112,96},{1... | collective-permute-start | bytes 3145736 | tf_op jit(solution)/shard_map/ppermute | solution.py:335
  31.0 22.4 %collective-permute-start.4 = (bf16[512,1024]{1,0:T(8,128)(2,1)}, bf16[512,1024]{1,0:T(8,128)(2,1)}, u32[]{:S(2)}, u32[]{:S(2)}) collective-permute-start(bf16[512,1024]{1,0:T(8,128)(2,1)} %bitcast.18), channel_id=1, source_target_pairs={{0,256},{16,80},{32,288},{48,112},{64,320},{80,16},{96,352},{112,4... | collective-permute-start | bytes 3145736 | tf_op jit(solution)/shard_map/ppermute | solution.py:315
  35.9 28.4 %collective-permute-start.5 = (bf16[512,1024]{1,0:T(8,128)(2,1)}, bf16[512,1024]{1,0:T(8,128)(2,1)}, u32[]{:S(2)}, u32[]{:S(2)}) collective-permute-start(bf16[512,1024]{1,0:T(8,128)(2,1)} %bitcast.19), channel_id=1, source_target_pairs={{0,128},{16,48},{32,160},{48,80},{64,192},{80,112},{96,224},{112,1... | collective-permute-start | bytes 3145736 | tf_op jit(solution)/shard_map/ppermute | solution.py:315
  38.7 4.5 %copy-start.21 = (f32[256,64]{1,0:T(8,128)}, f32[256,64]{1,0:T(8,128)S(1)}, u32[]{:S(2)}) copy-start(f32[256,64]{1,0:T(8,128)S(1)} %get-tuple-element.38) | copy-start | bytes 196612
  38.7 4.5 %copy-start.23 = (f32[256,64]{1,0:T(8,128)}, f32[256,64]{1,0:T(8,128)S(1)}, u32[]{:S(2)}) copy-start(f32[256,64]{1,0:T(8,128)S(1)} %get-tuple-element.39) | copy-start | bytes 196612
  38.7 4.5 %copy-start.24 = (f32[256,64]{1,0:T(8,128)}, f32[256,64]{1,0:T(8,128)S(1)}, u32[]{:S(2)}) copy-start(f32[256,64]{1,0:T(8,128)S(1)} %get-tuple-element.40) | copy-start | bytes 196612
  38.7 31.1 %collective-permute-start.3 = (bf16[512,1024]{1,0:T(8,128)(2,1)}, bf16[512,1024]{1,0:T(8,128)(2,1)}, u32[]{:S(2)}, u32[]{:S(2)}) collective-permute-start(bf16[512,1024]{1,0:T(8,128)(2,1)} %bitcast.20), channel_id=1, source_target_pairs={{0,384},{16,112},{32,416},{48,16},{64,448},{80,48},{96,480},{112,8... | collective-permute-start | bytes 3145736 | tf_op jit(solution)/shard_map/ppermute | solution.py:315
  46.5 28.8 %all-to-all-start.2 = ((bf16[16,256,128]{2,1,0:T(8,128)(2,1)}), bf16[16,256,128]{2,1,0:T(8,128)(2,1)}, u32[]{:S(2)}, u32[]{:S(2)}) async-start(bf16[16,256,128]{2,1,0:T(8,128)(2,1)} %copy-done.4), calls=%async_computation.2 | async-start | bytes 2097152 | tf_op jit(solution)/shard_map/all_to_all | solution.py:304
  66.7 3.0 %copy-start.7 = (bf16[1,128,4096]{2,1,0:T(8,128)(2,1)S(1)}, bf16[1,128,4096]{2,1,0:T(8,128)(2,1)}, u32[]{:S(2)}) copy-start(bf16[1,128,4096]{2,1,0:T(8,128)(2,1)} %param.9) | copy-start | bytes 3145732
  69.8 12.9 %copy-start.22 = (f32[256,64]{1,0:T(8,128)S(1)}, f32[256,64]{1,0:T(8,128)}, u32[]{:S(2)}) copy-start(f32[256,64]{1,0:T(8,128)} %copy-done.21) | copy-start | bytes 196612
  69.8 15.1 %copy-start.20 = (s32[1,8]{1,0:T(1,128)S(1)}, s32[1,8]{1,0:T(1,128)}, u32[]{:S(2)}) copy-start(s32[1,8]{1,0:T(1,128)} %lengths.1) | copy-start | bytes 100
  75.3 9.6 %collective-permute-start.7 = (bf16[4096,128]{1,0:T(8,128)(2,1)}, bf16[4096,128]{1,0:T(8,128)(2,1)}, u32[]{:S(2)}, u32[]{:S(2)}) collective-permute-start(bf16[4096,128]{1,0:T(8,128)(2,1)} %bitcast.5.own_at), channel_id=1, source_target_pairs={{0,16},{16,0},{32,48},{48,32},{64,80},{80,64},{96,112},{112,96},{1... | collective-permute-start | bytes 3145736 | tf_op jit(solution)/shard_map/ppermute | solution.py:335
  80.7 4.1 %collective-permute-start.6 = (f32[128,1024]{1,0:T(8,128)}, f32[128,1024]{1,0:T(8,128)}, u32[]{:S(2)}, u32[]{:S(2)}) collective-permute-start(f32[128,1024]{1,0:T(8,128)} %copy-done.18), channel_id=1, source_target_pairs={{0,16},{16,0},{32,48},{48,32},{64,80},{80,64},{96,112},{112,96},{1... | collective-permute-start | bytes 1572872 | tf_op jit(solution)/shard_map/ppermute | solution.py:335
  92.9 4.6 %collective-permute-start.8 = (bf16[2048,256]{1,0:T(8,128)(2,1)S(1)}, bf16[2048,256]{1,0:T(8,128)(2,1)S(1)}, u32[]{:S(2)}, u32[]{:S(2)}) collective-permute-start(bf16[2048,256]{1,0:T(8,128)(2,1)S(1)} %get-tuple-element.30), channel_id=1, source_target_pairs={{0,16},{16,0},{32,48},{48,32},{64,80},{80,64},{96,112},{112,96},{1... | collective-permute-start | bytes 3145736 | tf_op jit(solution)/shard_map/ppermute | solution.py:335
  94.9 13.3 %collective-permute-start.10 = (bf16[4096,128]{1,0:T(8,128)(2,1)S(1)}, bf16[4096,128]{1,0:T(8,128)(2,1)}, u32[]{:S(2)}, u32[]{:S(2)}) collective-permute-start(bf16[4096,128]{1,0:T(8,128)(2,1)S(1)} %bitcast.16), channel_id=1, source_target_pairs={{0,16},{16,0},{32,48},{48,32},{64,80},{80,64},{96,112},{112,96},{1... | collective-permute-start | bytes 3145736 | tf_op jit(solution)/shard_map/ppermute | solution.py:335
  98.7 23.9 %all-to-all-start.3 = ((bf16[16,128,256]{2,1,0:T(8,128)(2,1)}), bf16[16,128,256]{2,1,0:T(8,128)(2,1)}, u32[]{:S(2)}, u32[]{:S(2)}) async-start(bf16[16,128,256]{2,1,0:T(8,128)(2,1)} %bitcast.26), calls=%async_computation.3 | async-start | bytes 2097152 | tf_op jit(solution)/shard_map/all_to_all | solution.py:304
  105.9 3.3 %collective-permute-start.9 = (bf16[128,512]{1,0:T(8,128)(2,1)S(1)}, bf16[128,512]{1,0:T(8,128)(2,1)S(1)}, u32[]{:S(2)}, u32[]{:S(2)}) collective-permute-start(bf16[128,512]{1,0:T(8,128)(2,1)S(1)} %get-tuple-element.28.grad_query), channel_id=1, source_target_pairs={{0,16},{16,0},{32,48},{48,32},{64,80},{80,64},{96,112},{112,96},{1... | collective-permute-start | bytes 393224 | tf_op jit(solution)/shard_map/ppermute | solution.py:335
  124.1 4.7 %collective-permute-start.11 = (bf16[128,256]{1,0:T(8,128)(2,1)S(1)}, bf16[128,256]{1,0:T(8,128)(2,1)S(1)}, u32[]{:S(2)}, u32[]{:S(2)}) collective-permute-start(bf16[128,256]{1,0:T(8,128)(2,1)S(1)} %shard_map.101.grads), channel_id=1, source_target_pairs={{0,16},{16,0},{32,48},{48,32},{64,80},{80,64},{96,112},{112,96},{1... | collective-permute-start | bytes 196616 | tf_op jit(solution)/shard_map/ppermute | solution.py:335
  130.1 4.6 %copy-start.3 = (bf16[4,128,1024]{2,1,0:T(8,128)(2,1)S(1)}, bf16[4,128,1024]{2,1,0:T(8,128)(2,1)}, u32[]{:S(2)}) copy-start(bf16[4,128,1024]{2,1,0:T(8,128)(2,1)} %copy-done.1) | copy-start | bytes 3145732
  130.1 15.4 %all-to-all-start.4 = ((bf16[16,128,128]{2,1,0:T(8,128)(2,1)}), bf16[16,128,128]{2,1,0:T(8,128)(2,1)}, u32[]{:S(2)}, u32[]{:S(2)}) async-start(bf16[16,128,128]{2,1,0:T(8,128)(2,1)} %copy-done.8), calls=%async_computation.4 | async-start | bytes 1048576 | tf_op jit(solution)/shard_map/all_to_all | solution.py:304
  145.5 35.2 %copy-start.10 = (bf16[128,2048]{1,0:T(8,128)(2,1)S(1)}, bf16[128,2048]{1,0:T(8,128)(2,1)}, u32[]{:S(2)}) copy-start(bf16[128,2048]{1,0:T(8,128)(2,1)} %copy-done.9) | copy-start | bytes 1572868
  146.7 13.5 %collective-permute-start.13 = (bf16[128,128]{1,0:T(8,128)(2,1)S(1)}, bf16[128,128]{1,0:T(8,128)(2,1)S(1)}, u32[]{:S(2)}, u32[]{:S(2)}) collective-permute-start(bf16[128,128]{1,0:T(8,128)(2,1)S(1)} %reduce_sum.21), channel_id=1, source_target_pairs={{0,8},{1,9},{2,10},{3,11},{4,12},{5,13},{6,14},{7,15},{8,0},{9,1},... | collective-permute-start | bytes 98312 | tf_op jit(solution)/shard_map/ppermute | solution.py:391
  160.2 10.4 %collective-permute-start.14 = (bf16[128,128]{1,0:T(8,128)(2,1)S(1)}, bf16[128,128]{1,0:T(8,128)(2,1)S(1)}, u32[]{:S(2)}, u32[]{:S(2)}) collective-permute-start(bf16[128,128]{1,0:T(8,128)(2,1)S(1)} %add_convert_fusion.2), channel_id=1, source_target_pairs={{0,4},{1,5},{2,6},{3,7},{4,0},{5,1},{6,2},{7,3},{8,12},{9,13},{10,... | collective-permute-start | bytes 98312 | tf_op jit(solution)/shard_map/ppermute | solution.py:391
  164.9 15.8 %collective-permute-start.12 = (bf16[128,2048]{1,0:T(8,128)(2,1)}, bf16[128,2048]{1,0:T(8,128)(2,1)S(1)}, u32[]{:S(2)}, u32[]{:S(2)}) collective-permute-start(bf16[128,2048]{1,0:T(8,128)(2,1)} %copy-done.15), channel_id=1, source_target_pairs={{0,16},{16,0},{32,48},{48,32},{64,80},{80,64},{96,112},{112,96},{1... | collective-permute-start | bytes 1572872 | tf_op jit(solution)/shard_map/ppermute | solution.py:335
  (13 other events, 12.0 us)

commit v5 on v4

--- a/solution.py
+++ b/solution.py
@@ -67,31 +67,38 @@
         copy.wait()
 
 
-def pack_kernel(query_weight, out_weight, out, packed, turned, arrived, done):
-    width = query_weight.shape[1]
-    copies = fetch((query_weight, out_weight), (packed.at[:, :width], turned), arrived)
+def pack_kernel(query_weight, out_weight, key_weight, value_weight, out, packed, turned, arrived, done):
+    width, head = query_weight.shape[1], key_weight.shape[1]
+    copies = fetch(
+        (query_weight, out_weight, key_weight, value_weight),
+        (packed.at[:, :width], turned, packed.at[:, 2 * width:2 * width + head], packed.at[:, 2 * width + head:]),
+        arrived)
     copies[1].wait()
-    packed[:, width:] = turned[...].T
-    copies[0].wait()
+    packed[:, width:2 * width] = turned[...].T
+    for copy in (copies[0], copies[2], copies[3]):
+        copy.wait()
     write_copies(packed, out, done)
 
 
-def spread_kernel(place, key_weight, value_weight, received, out, held, done):
-    rows = key_weight.shape[0]
-    core = place[0] % 2
-    held[pl.ds(pl.multiple_of(core * rows, rows), rows), :] = jnp.where(
-        core == 0, key_weight[...], value_weight[...])
-    held[pl.ds(pl.multiple_of((1 - core) * rows, rows), rows), :] = received[...]
-    write_copies(held, out, done)
-
-
-def shard_order(core, chip, side):
+def split_kernel(line, big, small, copies, done):
+    width = big.shape[1]
+    small[...] = line[:, width:]
+    started = [pltpu.make_async_copy(small, copies.at[i], done.at[i]) for i in range(copies.shape[0])]
+    for copy in started:
+        copy.start()
+    big[...] = line[:, :width]
+    for copy in started:
+        copy.wait()
+
+
+def shard_order(core, chip, side, natural=False):
     row, column = chip // side, chip % side
     order = []
-    for offset in RING:
+    for second in range(side):
         for first in range(side):
-            down = jnp.where(core == 0, (row + offset + side) % side, first)
-            along = jnp.where(core == 0, first, (column + offset + side) % side)
+            offset = RING[second]
+            down = jnp.where(core == 0, second if natural else (row + offset + side) % side, first)
+            along = jnp.where(core == 0, first, second if natural else (column + offset + side) % side)
             order.append((down * side + along) * 2 + core)
     return order
 
@@ -127,14 +134,28 @@
     copy.wait()
 
 
-def project_kernel(place, tokens, other_tokens, weight, cosine, sine, out, held, done):
-    rows = tokens.shape[0]
-    own_core = place[0] % 2
-    for source, core in ((tokens, own_core), (other_tokens, 1 - own_core)):
-        here = pl.ds(pl.multiple_of(core * rows, rows), rows)
-        v = lax.dot_general(source[...], weight[...], NN, preferred_element_type=F32)
-        held[here, :] = (v * cosine[here, :] + swap_halves(v) * sine[here, :]).astype(BF16)
-    write_copies(held, out, done)
+def project_kernel(place, tokens, other_tokens, weights, mine, theirs):
+    rows, features = tokens.shape
+    side = math.isqrt(features // (2 * rows))
+    shards = shard_order(place[0] % 2, place[0] // 2, side, natural=True)
+    for source, out in ((other_tokens, theirs), (tokens, mine)):
+        total = jnp.zeros(out.shape, F32)
+        for n in range(0, side * side, 2):
+            columns = [pl.ds(pl.multiple_of(shards[n + i] * rows, rows), rows) for i in range(2)]
+            t = jnp.concatenate([source[:, here] for here in columns], axis=1)
+            total += lax.dot_general(t, weights[n * rows:(n + 2) * rows, :], NN, preferred_element_type=F32)
+        out[...] = total
+
+
+def rotate_kernel(mine, received, cosine, sine, out):
+    head = cosine.shape[1]
+    both = mine[...] + received[...]
+    key = both[:, :head]
+    key = (key * cosine[...] + swap_halves(key) * sine[...]).astype(BF16)
+    value = both[:, head:].astype(BF16)
+    for chip in range(out.shape[0]):
+        out[chip, :, :head] = key
+        out[chip, :, head:] = value
 
 
 def attention_kernel(place, order, lengths, mine, theirs_at, own_at, other_at, cosine, sine,
@@ -144,7 +165,7 @@
     rows = mine.shape[0]
     head = cosine.shape[1]
     heads = q_ref.shape[1] // head
-    seq = own_part.shape[0]
+    seq = 2 * own_part.shape[0]
     blocks = seq // BLOCK
     span = key_window.shape[0] // BLOCK
     scaling = head ** (-0.5)
@@ -180,10 +201,13 @@
         block = order[0, own * (rows // BLOCK) + j]
         first = block - (span - 1)
         for w in range(span):
-            source = pl.multiple_of(stored_at[jnp.maximum(first + w, 0)] * BLOCK, BLOCK)
-            first_half, second_half = own_part[pl.ds(source, BLOCK), :], other_part[pl.ds(source, BLOCK), :]
-            key_window[w * BLOCK:(w + 1) * BLOCK, :] = jnp.where(own_core == 0, first_half, second_half)
-            value_window[w * BLOCK:(w + 1) * BLOCK, :] = jnp.where(own_core == 0, second_half, first_half)
+            spot = stored_at[jnp.maximum(first + w, 0)]
+            device = spot // 2
+            source = pl.multiple_of((device // 2) * (2 * BLOCK) + (spot % 2) * BLOCK, BLOCK)
+            block_here = jnp.where(
+                device % 2 == own_core, own_part[pl.ds(source, BLOCK), :], other_part[pl.ds(source, BLOCK), :])
+            key_window[w * BLOCK:(w + 1) * BLOCK, :] = block_here[:, :head]
+            value_window[w * BLOCK:(w + 1) * BLOCK, :] = block_here[:, head:]
         q = jnp.concatenate([q_ref[r0:r0 + BLOCK, h * head:(h + 1) * head] for h in range(heads)], 0)
         a = jnp.concatenate([a_ref[r0:r0 + BLOCK, h * head:(h + 1) * head] for h in range(heads)], 0)
         lane = lax.broadcasted_iota(jnp.int32, (1, heads * BLOCK), 1)
@@ -253,25 +277,22 @@
         out[chip] = lax.dot_general(t, both, TN, preferred_element_type=F32).astype(BF16)
 
 
-def input_kernel(place, grad_query, other_grad_query, grads, other_grads, own_weight, other_weight,
-                 w0, w1, w2, w3, mine, theirs):
+def input_kernel(place, grad_query, other_grad_query, grads, other_grads, weights, w0, w1, w2, w3, mine, theirs):
     rows, width = grad_query.shape
-    head = own_weight.shape[1]
-    core = place[0] % 2
-    side = math.isqrt(own_weight.shape[0] // (2 * rows))
+    core, chip = place[0] % 2, place[0] // 2
+    side = math.isqrt(weights.shape[0] // rows)
     queries = jnp.concatenate([grad_query[...], other_grad_query[...]], axis=0)
     both = jnp.concatenate([grads[...], other_grads[...]], axis=0)
-    own_grad = jnp.where(core == 0, both[:, :head], both[:, head:])
-    other_grad = jnp.where(core == 0, both[:, head:], both[:, :head])
-    for n, shard in enumerate(shard_order(core, place[0] // 2, side)):
+    own_place = jnp.where(core == 0, chip // side, chip % side)
+    for n, shard in enumerate(shard_order(core, chip, side)):
         at = (n % side) * rows
-        here = pl.ds(pl.multiple_of(shard * rows, rows), rows)
+        held_at = ((own_place + RING[n // side] + side) % side) * side + n % side
+        small = weights[pl.ds(pl.multiple_of(held_at * rows, rows), rows), :]
         to = pl.ds(pl.multiple_of((shard // 2) * rows, rows), rows)
         part = (
             lax.dot_general(queries, (w0, w1, w2, w3)[n // side][at:at + rows, :width], NT,
                             preferred_element_type=F32)
-            + lax.dot_general(own_grad, own_weight[here, :], NT, preferred_element_type=F32)
-            + lax.dot_general(other_grad, other_weight[here, :], NT, preferred_element_type=F32)
+            + lax.dot_general(both, small, NT, preferred_element_type=F32)
         ).astype(BF16)
         mine[:, to] = part[:rows]
         theirs[:, to] = part[rows:]
@@ -292,7 +313,6 @@
     chips = ctx // 2
     seq = rows * ctx
     me = lax.axis_index("ctx")
-    core = me % 2
     head = key_weight.shape[1]
     width = query_weight.shape[1]
     heads = width // head
@@ -316,35 +336,35 @@
 
     rings = [[(row * side + i) * 2 for i in range(side)] for row in range(side)]
     rings += [[(i * side + column) * 2 + 1 for i in range(side)] for column in range(side)]
-    (packed,) = call(pack_kernel, [shape((side, rows, 2 * width))], [HBM] * 2, (query_weight, out_weight), 0,
-                     scratch=[pltpu.VMEM((rows, 2 * width), BF16), pltpu.VMEM((width, rows), BF16),
-                              pltpu.SemaphoreType.DMA((2,)), pltpu.SemaphoreType.DMA((side,))],
-                     limit=60, out_specs=[HBM])
-    line = lax.all_to_all(packed, "ctx", 0, 0, tiled=True, axis_index_groups=rings).reshape(side * rows, 2 * width)
+    crossing = [[(i * side + column) * 2 for i in range(side)] for column in range(side)]
+    crossing += [[(row * side + i) * 2 + 1 for i in range(side)] for row in range(side)]
+    (packed,) = call(
+        pack_kernel, [shape((side, rows, 2 * width + 2 * head))], [HBM] * 4,
+        (query_weight, out_weight, key_weight, value_weight), 0,
+        scratch=[pltpu.VMEM((rows, 2 * width + 2 * head), BF16), pltpu.VMEM((width, rows), BF16),
+                 pltpu.SemaphoreType.DMA((4,)), pltpu.SemaphoreType.DMA((side,))],
+        limit=60, out_specs=[HBM])
+    line = lax.all_to_all(packed, "ctx", 0, 0, tiled=True, axis_index_groups=rings)
+    line = line.reshape(side * rows, 2 * width + 2 * head)
+    line, small, copies = call(
+        split_kernel,
+        [shape((side * rows, 2 * width)), shape((side * rows, 2 * head)), shape((side, side * rows, 2 * head))],
+        [VMEM], (line,), 0, scratch=[pltpu.SemaphoreType.DMA((side,))], out_specs=[VMEM, VMEM, HBM])
+    small_weights = lax.all_to_all(
+        copies, "ctx", 0, 0, tiled=True, axis_index_groups=crossing).reshape(features // 2, 2 * head)
     held = [line] + [moved(line, 1, -offset) for offset in RING[1:]]
 
-    chip_blocks = lax.dynamic_slice_in_dim(block_order[0], (me // 2) * 4, 4)
-    chip_cosine, chip_sine = tables(chip_blocks, head)
-    cosine = lax.dynamic_slice_in_dim(chip_cosine, core * rows, rows)
-    sine = lax.dynamic_slice_in_dim(chip_sine, core * rows, rows)
-    is_key = core == 0
-    own_cosine = jnp.where(is_key, chip_cosine, 1.0)
-    own_sine = jnp.where(is_key, chip_sine, 0.0)
+    cosine, sine = tables(lax.dynamic_slice_in_dim(block_order[0], me * 2, 2), head)
 
     def swap(v):
         return lax.ppermute(v, "ctx", other)
 
-    (copies,) = call(
-        spread_kernel, [shape((chips, 2 * rows, head))], [SMEM] + [VMEM] * 3,
-        (place, key_weight, value_weight, swap(jnp.where(is_key, value_weight, key_weight))), 0,
-        scratch=[pltpu.VMEM((2 * rows, head), BF16), pltpu.SemaphoreType.DMA((chips,))], out_specs=[HBM])
-    copies, _ = lax.optimization_barrier((copies, line))
-    own_weight = to_chips(copies).reshape(features, head)
     other_tokens = swap(tokens)
+    kv_mine, kv_theirs = call(
+        project_kernel, [shape((rows, 2 * head), F32)] * 2, [SMEM] + [VMEM] * 3,
+        (place, tokens, other_tokens, small_weights), 4 * rows * features * head)
     (projected,) = call(
-        project_kernel, [shape((chips, 2 * rows, head))], [SMEM] + [VMEM] * 5,
-        (place, tokens, other_tokens, own_weight, own_cosine, own_sine), 4 * rows * features * head,
-        scratch=[pltpu.VMEM((2 * rows, head), BF16), pltpu.SemaphoreType.DMA((chips,))], out_specs=[HBM])
+        rotate_kernel, [shape((chips, rows, 2 * head))], [VMEM] * 4, (kv_mine, swap(kv_theirs), cosine, sine), 0)
     sources = (place, tokens, upstream, other_tokens, swap(upstream))
     halves = [shape((rows, 2 * width), F32)] * 2
     mine, theirs = call(
@@ -354,12 +374,11 @@
         last_partial_kernel, halves, [SMEM] + [VMEM] * 7,
         sources + (held[3], mine, theirs), rows * features * width,
         scratch=[pltpu.VMEM((rows, 2 * width), F32), pltpu.SemaphoreType.DMA], out_specs=[VMEM, HBM])
-    own_part = to_chips(projected).reshape(seq, head)
-    own_part, mine, theirs = lax.optimization_barrier((own_part, mine, theirs))
+    own_part = to_chips(projected).reshape(seq // 2, 2 * head)
+    own_part, theirs = lax.optimization_barrier((own_part, theirs))
     received = swap(theirs)
     other_part = swap(own_part)
-    other_weight = swap(own_weight)
-    window = LONGEST + 2 * BLOCK
+    window = LONGEST + BLOCK
     grad_query, kept, sent = call(
         attention_kernel,
         [shape((rows, width)), shape((seq // 2, 2 * head)), shape((seq // 2, 2 * head))],
@@ -370,19 +389,20 @@
                  pltpu.VMEM((window, head), BF16), pltpu.VMEM((window, head), BF16),
                  pltpu.VMEM((seq, 2 * head), F32), pltpu.SMEM((seq // BLOCK,), jnp.int32),
                  pltpu.VMEM((rows, 2 * width), F32),
-                 pltpu.VMEM((seq, head), BF16), pltpu.VMEM((seq, head), BF16), pltpu.SemaphoreType.DMA((4,))],
+                 pltpu.VMEM((seq // 2, 2 * head), BF16), pltpu.VMEM((seq // 2, 2 * head), BF16),
+                 pltpu.SemaphoreType.DMA((4,))],
         limit=28)
     pairs = (kept.astype(F32) + swap(sent).astype(F32)).astype(BF16)
-    pieces, other_grad_query, other_weight = lax.optimization_barrier(
-        (to_chips(pairs).reshape(chips, rows, 2 * head), swap(grad_query), other_weight))
+    pieces, other_grad_query = lax.optimization_barrier(
+        (to_chips(pairs).reshape(chips, rows, 2 * head), swap(grad_query)))
     (grads,) = call(owner_kernel, [shape((rows, 2 * head))], [VMEM] * 3, (pieces, cosine, sine), 0)
     other_grads = swap(grads)
     (parts,) = call(
         weight_kernel, [shape((chips, rows, head))], [SMEM] + [VMEM] * 4,
         (place, tokens, other_tokens, grads, other_grads), 2 * rows * features * head)
     input_mine, input_theirs = call(
-        input_kernel, [shape((rows, features // 2))] * 2, [SMEM] + [VMEM] * 10,
-        (place, grad_query, other_grad_query, grads, other_grads, own_weight, other_weight, *held),
+        input_kernel, [shape((rows, features // 2))] * 2, [SMEM] + [VMEM] * 9,
+        (place, grad_query, other_grad_query, grads, other_grads, small_weights, *held),
         2 * rows * features * (width + 2 * head))
     gathered, input_theirs = lax.optimization_barrier((to_chips(parts), input_theirs))
     grad_weight = jnp.sum(gathered.reshape(chips, rows, head).astype(F32), axis=0)
@@ -394,10 +414,11 @@
     near = [[first + i for i in range(group)] for first in range(0, dp, group)]
     spread = jnp.broadcast_to(grad_weight.astype(BF16)[None], (group, rows, head))
     gathered = lax.all_to_all(spread, "dp", 0, 0, tiled=True, axis_index_groups=near)
-    grad_weight = jnp.sum(gathered.reshape(group, rows, head).astype(F32), axis=0)
     (grad_input,) = call(
         merge_kernel, [shape((rows, features))], [SMEM] + [VMEM] * 2,
         (place, input_mine, swap(input_theirs)), 0)
+    gathered, grad_input = lax.optimization_barrier((gathered, grad_input))
+    grad_weight = jnp.sum(gathered.reshape(group, rows, head).astype(F32), axis=0)
     return grad_input[None], grad_weight
 
 

time: 183 us -> 179 us (0.978)
  waiting for transfers between devices: 38.6 us -> 52 us
  blocking collectives: 9.44 us -> 0 us
  local copies, waits for them, and re-layouts: 12.1 us -> 8.95 us
  other arithmetic: 5.04 us -> 2.65 us
  Pallas kernels: 25.3 us -> 23.2 us
    all_to_all x0 -> x2, starting transfers between devices: none -> 9.68 us  [the longest x1 5.53 us: on_device(): lax.all_to_all(spread, 'dp', 0, 0, tiled=True, axis_index_groups=near)]
    all_to_all x1 -> x0, blocking collectives: 9.44 us -> none  [on_device(): lax.all_to_all(spread, 'dp', 0, 0, tiled=True, axis_index_groups=near)]
    all_to_all x4 -> x3, starting transfers between devices: 20.6 us -> 12.2 us  [to_chips(): lax.all_to_all(pieces, 'ctx', 0, 0, tiled=True, axis_index_groups=planes)]
    all_to_all x4 -> x3, waiting for transfers between devices: 18.7 us -> 23.4 us  [to_chips(): lax.all_to_all(pieces, 'ctx', 0, 0, tiled=True, axis_index_groups=planes)]
    unnamed x50 -> x24, local copies, waits for them, and re-layouts: 12 us -> 8.19 us
    all_to_all x1, waiting for transfers between devices: 0.01 us -> 3.81 us  [on_device(): lax.all_to_all(packed, 'ctx', 0, 0, tiled=True, axis_index_groups=rings)]
    all_to_all x0 -> x2, waiting for transfers between devices: none -> 3.59 us  [the longest x1 3.59 us: on_device(): lax.all_to_all(spread, 'dp', 0, 0, tiled=True, axis_index_groups=near)]
    ppermute x3, starting transfers between devices: 11.4 us -> 8.68 us  [moved(): return lax.ppermute(v, 'ctx', pairs)]
  transfers between devices with their start and end apart: 20 -> 20, of which waited for: 11 -> 12; matrix products, arithmetic and copies ran while one was open for 2% -> 1% of each run, Pallas kernels for 7% -> 7%
where the time goes in v5:
time: 179 us; the launch traced here: 178 us
  starting transfers between devices  90.1 us (50%)
  waiting for transfers between devices  52 us (29%)
  Pallas kernels  23.2 us (13%)
  local copies, waits for them, and re-layouts  8.95 us (5%)
  other arithmetic  2.65 us (1%)
    ppermute x9, starting transfers between devices, swap(): return lax.ppermute(v, 'ctx', other)  38.6 us
    all_to_all x3, waiting for transfers between devices, to_chips(): lax.all_to_all(pieces, 'ctx', 0, 0, tiled=True, axis_index_groups=planes)  23.4 us
    pallas_call x11, Pallas kernels, call(): pl.pallas_call(body, out_shape=outs, in_specs=in_specs, out_specs=out_spe...  23.2 us
    ppermute x2, starting transfers between devices, on_device(): lax.ppermute(grad_weight.astype(BF16), 'dp', [(i, i ^ step) for i in rang...  15.8 us
    ppermute x3, waiting for transfers between devices, moved(): return lax.ppermute(v, 'ctx', pairs)  12.3 us
    all_to_all x3, starting transfers between devices, to_chips(): lax.all_to_all(pieces, 'ctx', 0, 0, tiled=True, axis_index_groups=planes)  12.2 us
    ppermute x3, starting transfers between devices, moved(): return lax.ppermute(v, 'ctx', pairs)  8.68 us
    unnamed x24, local copies, waits for them, and re-layouts  8.19 us
  transfers between devices with their start and end apart: 20, of which 12 were waited for; matrix products, arithmetic and copies ran while one was open for 1% of the time, Pallas kernels for 7%

profile of v5, /device:TPU:1, one launch (start us, length us, event | category | flops | bytes accessed | tf_op | source)
XLA Modules:
  0.0 177.9 jit_solution(12473617024273758632)
XLA Ops:
  0.6 2.2 %shard_map.95 = bf16[4,128,1280]{2,1,0:T(8,128)(2,1)} custom-call(bf16[128,512]{1,0:T(8,128)(2,1)} %query_weight.1, bf16[512,128]{1,0:T(8,128)(2,1)} %out_weight.1, bf16[128,128]{1,0:T(8,128)(2,1)} %key_weight.1, bf16[128,128]{1,0:T(8,128)(2,1)} %value_weight.1), custom_call_target="tpu_custom_call" | custom-call | bytes 1638400 | tf_op jit(solution)/shard_map/pallas_call | solution.py:27
  2.9 5.2 %all-to-all-start = ((bf16[4,128,1280]{2,1,0:T(8,128)(2,1)}), bf16[4,128,1280]{2,1,0:T(8,128)(2,1)S(1)}, u32[]{:S(2)}, u32[]{:S(2)}) async-start(bf16[4,128,1280]{2,1,0:T(8,128)(2,1)} %shard_map.95), calls=%async_computation | async-start | bytes 2621440 | tf_op jit(solution)/shard_map/all_to_all | solution.py:347
  8.0 7.3 %collective-permute-start = (bf16[128,4096]{1,0:T(8,128)(2,1)S(1)}, bf16[128,4096]{1,0:T(8,128)(2,1)S(1)}, u32[]{:S(2)}, u32[]{:S(2)}) collective-permute-start(bf16[128,4096]{1,0:T(8,128)(2,1)S(1)} %bitcast.10), channel_id=1, source_target_pairs={{0,16},{16,0},{32,48},{48,32},{64,80},{80,64},{96,112},{112,96},{1... | collective-permute-start | bytes 3145736 | tf_op jit(solution)/shard_map/ppermute | solution.py:360
  15.4 3.8 %all-to-all-done = bf16[4,128,1280]{2,1,0:T(8,128)(2,1)S(1)} async-done(((bf16[4,128,1280]{2,1,0:T(8,128)(2,1)}), bf16[4,128,1280]{2,1,0:T(8,128)(2,1)S(1)}, u32[]{:S(2)}, u32[]{:S(2)}) %all-to-all-start) | async-done | bytes 1310752 | tf_op jit(solution)/shard_map/all_to_all | solution.py:347
  21.4 4.1 %all-to-all-start.1 = ((bf16[4,512,256]{2,1,0:T(8,128)(2,1)}), bf16[4,512,256]{2,1,0:T(8,128)(2,1)S(1)}, u32[]{:S(2)}, u32[]{:S(2)}) async-start(bf16[4,512,256]{2,1,0:T(8,128)(2,1)} %copy-done.4), calls=%async_computation.1 | async-start | bytes 2097152 | tf_op jit(solution)/shard_map/all_to_all | solution.py:353
  25.5 7.9 %collective-permute-start.1 = (bf16[128,4096]{1,0:T(8,128)(2,1)}, bf16[128,4096]{1,0:T(8,128)(2,1)}, u32[]{:S(2)}, u32[]{:S(2)}) collective-permute-start(bf16[128,4096]{1,0:T(8,128)(2,1)} %bitcast.18), channel_id=1, source_target_pairs={{0,16},{16,0},{32,48},{48,32},{64,80},{80,64},{96,112},{112,96},{1... | collective-permute-start | bytes 3145736 | tf_op jit(solution)/shard_map/ppermute | solution.py:360
  33.8 2.2 %collective-permute-start.4 = (bf16[512,1024]{1,0:T(8,128)(2,1)}, bf16[512,1024]{1,0:T(8,128)(2,1)}, u32[]{:S(2)}, u32[]{:S(2)}) collective-permute-start(bf16[512,1024]{1,0:T(8,128)(2,1)} %get-tuple-element.23.w0), channel_id=1, source_target_pairs={{0,128},{16,48},{32,160},{48,80},{64,192},{80,112},{96,224},{112,1... | collective-permute-start | bytes 3145736 | tf_op jit(solution)/shard_map/ppermute | solution.py:335
  36.0 3.7 %collective-permute-start.3 = (bf16[512,1024]{1,0:T(8,128)(2,1)}, bf16[512,1024]{1,0:T(8,128)(2,1)}, u32[]{:S(2)}, u32[]{:S(2)}) collective-permute-start(bf16[512,1024]{1,0:T(8,128)(2,1)} %get-tuple-element.23.w0), channel_id=1, source_target_pairs={{0,256},{16,80},{32,288},{48,112},{64,320},{80,16},{96,352},{112,4... | collective-permute-start | bytes 3145736 | tf_op jit(solution)/shard_map/ppermute | solution.py:335
  40.2 4.7 %collective-permute-start.5 = (f32[128,256]{1,0:T(8,128)S(1)}, f32[128,256]{1,0:T(8,128)S(1)}, u32[]{:S(2)}, u32[]{:S(2)}) collective-permute-start(f32[128,256]{1,0:T(8,128)S(1)} %get-tuple-element.29), channel_id=1, source_target_pairs={{0,16},{16,0},{32,48},{48,32},{64,80},{80,64},{96,112},{112,96},{1... | collective-permute-start | bytes 393224 | tf_op jit(solution)/shard_map/ppermute | solution.py:360
  45.2 2.8 %collective-permute-start.2 = (bf16[512,1024]{1,0:T(8,128)(2,1)}, bf16[512,1024]{1,0:T(8,128)(2,1)}, u32[]{:S(2)}, u32[]{:S(2)}) collective-permute-start(bf16[512,1024]{1,0:T(8,128)(2,1)} %get-tuple-element.23.w0), channel_id=1, source_target_pairs={{0,384},{16,112},{32,416},{48,16},{64,448},{80,48},{96,480},{112,8... | collective-permute-start | bytes 3145736 | tf_op jit(solution)/shard_map/ppermute | solution.py:335
  49.4 4.3 %all-to-all-start.2 = ((bf16[16,128,256]{2,1,0:T(8,128)(2,1)}), bf16[16,128,256]{2,1,0:T(8,128)(2,1)}, u32[]{:S(2)}, u32[]{:S(2)}) async-start(bf16[16,128,256]{2,1,0:T(8,128)(2,1)} %copy-done.1), calls=%async_computation.2 | async-start | bytes 2097152 | tf_op jit(solution)/shard_map/all_to_all | solution.py:324
  53.7 11.3 %collective-permute-done.4.w2 = bf16[512,1024]{1,0:T(8,128)(2,1)} collective-permute-done((bf16[512,1024]{1,0:T(8,128)(2,1)}, bf16[512,1024]{1,0:T(8,128)(2,1)}, u32[]{:S(2)}, u32[]{:S(2)}) %collective-permute-start.4) | collective-permute-done | bytes 1048608 | tf_op jit(solution)/shard_map/ppermute | solution.py:335
  66.2 3.2 %shard_map.97 = (f32[128,1024]{1,0:T(8,128)S(1)}, f32[128,1024]{1,0:T(8,128)S(1)}) custom-call(s32[1]{0:T(128)} %bitcast.place, bf16[128,4096]{1,0:T(8,128)(2,1)S(1)} %bitcast.12, bf16[128,4096]{1,0:T(8,128)(2,1)S(1)} %bitcast.19, bf16[128,4096]{1,0:T(8,128)(2,1)S(1)} %collective-permute-done.other_tokens, ...), custom_call_target="tpu_custom_call" | custom-call | flops 805306368 | bytes 8388612 | tf_op jit(solution)/shard_map/pallas_call | solution.py:27
  70.5 2.3 %shard_map.98 = (f32[128,1024]{1,0:T(8,128)S(1)}, f32[128,1024]{1,0:T(8,128)S(1)}) custom-call(s32[1]{0:T(128)} %bitcast.place, bf16[128,4096]{1,0:T(8,128)(2,1)S(1)} %bitcast.13, bf16[128,4096]{1,0:T(8,128)(2,1)S(1)} %bitcast.20, bf16[128,4096]{1,0:T(8,128)(2,1)S(1)} %collective-permute-done.other_tokens, ...), custom_call_target="tpu_custom_call" | custom-call | flops 268435456 | bytes 7340036 | tf_op jit(solution)/shard_map/pallas_call | solution.py:27
  74.4 2.8 %all-to-all-done.2 = bf16[16,128,256]{2,1,0:T(8,128)(2,1)} async-done(((bf16[16,128,256]{2,1,0:T(8,128)(2,1)}), bf16[16,128,256]{2,1,0:T(8,128)(2,1)}, u32[]{:S(2)}, u32[]{:S(2)}) %all-to-all-start.2) | async-done | bytes 1048608 | tf_op jit(solution)/shard_map/all_to_all | solution.py:324
  77.2 4.8 %collective-permute-start.7 = (bf16[2048,256]{1,0:T(8,128)(2,1)}, bf16[2048,256]{1,0:T(8,128)(2,1)S(1)}, u32[]{:S(2)}, u32[]{:S(2)}) collective-permute-start(bf16[2048,256]{1,0:T(8,128)(2,1)} %bitcast.6.own_at), channel_id=1, source_target_pairs={{0,16},{16,0},{32,48},{48,32},{64,80},{80,64},{96,112},{112,96},{1... | collective-permute-start | bytes 3145736 | tf_op jit(solution)/shard_map/ppermute | solution.py:360
  83.9 2.1 %collective-permute-done.6.theirs_at = f32[128,1024]{1,0:T(8,128)S(1)} collective-permute-done((f32[128,1024]{1,0:T(8,128)}, f32[128,1024]{1,0:T(8,128)S(1)}, u32[]{:S(2)}, u32[]{:S(2)}) %collective-permute-start.6) | collective-permute-done | bytes 524320 | tf_op jit(solution)/shard_map/ppermute | solution.py:360
  87.0 6.4 %shard_map.101 = (bf16[128,512]{1,0:T(8,128)(2,1)S(1)}, bf16[2048,256]{1,0:T(8,128)(2,1)S(1)}, bf16[2048,256]{1,0:T(8,128)(2,1)S(1)}) custom-call(s32[1]{0:T(128)} %bitcast.place, s32[1,64]{1,0:T(1,128)S(1)} %copy-done.10, s32[1,8]{1,0:T(1,128)S(1)} %copy-done.11, f32[128,1024]{1,0:T(8,128)S(1)} %copy-done.8, ...), custom_call_target="tpu_custom_call" | custom-call | flops 1426063360 | bytes 5505316 | tf_op jit(solution)/shard_map/pallas_call | solution.py:27
  93.5 2.0 %collective-permute-start.8 = (bf16[2048,256]{1,0:T(8,128)(2,1)S(1)}, bf16[2048,256]{1,0:T(8,128)(2,1)S(1)}, u32[]{:S(2)}, u32[]{:S(2)}) collective-permute-start(bf16[2048,256]{1,0:T(8,128)(2,1)S(1)} %get-tuple-element.34), channel_id=1, source_target_pairs={{0,16},{16,0},{32,48},{48,32},{64,80},{80,64},{96,112},{112,96},{1... | collective-permute-start | bytes 3145736 | tf_op jit(solution)/shard_map/ppermute | solution.py:360
  95.5 2.5 %collective-permute-done.8 = bf16[2048,256]{1,0:T(8,128)(2,1)S(1)} collective-permute-done((bf16[2048,256]{1,0:T(8,128)(2,1)S(1)}, bf16[2048,256]{1,0:T(8,128)(2,1)S(1)}, u32[]{:S(2)}, u32[]{:S(2)}) %collective-permute-start.8) | collective-permute-done | bytes 1048608 | tf_op jit(solution)/shard_map/ppermute | solution.py:360
  99.3 4.3 %all-to-all-start.3 = ((bf16[16,128,256]{2,1,0:T(8,128)(2,1)}), bf16[16,128,256]{2,1,0:T(8,128)(2,1)}, u32[]{:S(2)}, u32[]{:S(2)}) async-start(bf16[16,128,256]{2,1,0:T(8,128)(2,1)} %bitcast.21), calls=%async_computation.3 | async-start | bytes 2097152 | tf_op jit(solution)/shard_map/all_to_all | solution.py:324
  107.6 14.6 %all-to-all-done.3.pieces = bf16[16,128,256]{2,1,0:T(8,128)(2,1)} async-done(((bf16[16,128,256]{2,1,0:T(8,128)(2,1)}), bf16[16,128,256]{2,1,0:T(8,128)(2,1)}, u32[]{:S(2)}, u32[]{:S(2)}) %all-to-all-start.3) | async-done | bytes 1048608 | tf_op jit(solution)/shard_map/all_to_all | solution.py:324
  123.6 2.9 %collective-permute-start.10 = (bf16[128,256]{1,0:T(8,128)(2,1)S(1)}, bf16[128,256]{1,0:T(8,128)(2,1)S(1)}, u32[]{:S(2)}, u32[]{:S(2)}) collective-permute-start(bf16[128,256]{1,0:T(8,128)(2,1)S(1)} %shard_map.102.grads), channel_id=1, source_target_pairs={{0,16},{16,0},{32,48},{48,32},{64,80},{80,64},{96,112},{112,96},{1... | collective-permute-start | bytes 196616 | tf_op jit(solution)/shard_map/ppermute | solution.py:360
  128.6 3.6 %all-to-all-start.4 = ((bf16[16,128,128]{2,1,0:T(8,128)(2,1)}), bf16[16,128,128]{2,1,0:T(8,128)(2,1)S(1)}, u32[]{:S(2)}, u32[]{:S(2)}) async-start(bf16[16,128,128]{2,1,0:T(8,128)(2,1)} %copy-done.3), calls=%async_computation.4 | async-start | bytes 1048576 | tf_op jit(solution)/shard_map/all_to_all | solution.py:324
  133.1 4.0 %shard_map.104 = (bf16[128,2048]{1,0:T(8,128)(2,1)S(1)}, bf16[128,2048]{1,0:T(8,128)(2,1)S(1)}) custom-call(s32[1]{0:T(128)} %bitcast.place, bf16[128,512]{1,0:T(8,128)(2,1)S(1)} %get-tuple-element.35.grad_query, bf16[128,512]{1,0:T(8,128)(2,1)S(1)} %copy-done.6, bf16[128,256]{1,0:T(8,128)(2,1)S(1)} %shard_map.102.grads, ...), custom_call_target="tpu_custom_call" | custom-call | flops 805306368 | bytes 6684676 | tf_op jit(solution)/shard_map/pallas_call | solution.py:27
  137.1 6.1 %all-to-all-done.4 = bf16[16,128,128]{2,1,0:T(8,128)(2,1)S(1)} async-done(((bf16[16,128,128]{2,1,0:T(8,128)(2,1)}), bf16[16,128,128]{2,1,0:T(8,128)(2,1)S(1)}, u32[]{:S(2)}, u32[]{:S(2)}) %all-to-all-start.4) | async-done | bytes 524320 | tf_op jit(solution)/shard_map/all_to_all | solution.py:324
  143.3 11.3 %collective-permute-start.11 = (bf16[128,128]{1,0:T(8,128)(2,1)S(1)}, bf16[128,128]{1,0:T(8,128)(2,1)S(1)}, u32[]{:S(2)}, u32[]{:S(2)}) collective-permute-start(bf16[128,128]{1,0:T(8,128)(2,1)S(1)} %reduce_sum.21), channel_id=1, source_target_pairs={{0,8},{1,9},{2,10},{3,11},{4,12},{5,13},{6,14},{7,15},{8,0},{9,1},... | collective-permute-start | bytes 98312 | tf_op jit(solution)/shard_map/ppermute | solution.py:411
  154.5 2.2 %collective-permute-done.11 = bf16[128,128]{1,0:T(8,128)(2,1)S(1)} collective-permute-done((bf16[128,128]{1,0:T(8,128)(2,1)S(1)}, bf16[128,128]{1,0:T(8,128)(2,1)S(1)}, u32[]{:S(2)}, u32[]{:S(2)}) %collective-permute-start.11) | collective-permute-done | bytes 32800 | tf_op jit(solution)/shard_map/ppermute | solution.py:411
  156.8 4.5 %collective-permute-start.12 = (bf16[128,128]{1,0:T(8,128)(2,1)S(1)}, bf16[128,128]{1,0:T(8,128)(2,1)S(1)}, u32[]{:S(2)}, u32[]{:S(2)}) collective-permute-start(bf16[128,128]{1,0:T(8,128)(2,1)S(1)} %add_convert_fusion.2), channel_id=1, source_target_pairs={{0,4},{1,5},{2,6},{3,7},{4,0},{5,1},{6,2},{7,3},{8,12},{9,13},{10,... | collective-permute-start | bytes 98312 | tf_op jit(solution)/shard_map/ppermute | solution.py:411
  161.3 4.9 %collective-permute-start.13 = (bf16[128,2048]{1,0:T(8,128)(2,1)S(1)}, bf16[128,2048]{1,0:T(8,128)(2,1)S(1)}, u32[]{:S(2)}, u32[]{:S(2)}) collective-permute-start(bf16[128,2048]{1,0:T(8,128)(2,1)S(1)} %get-tuple-element.41), channel_id=1, source_target_pairs={{0,16},{16,0},{32,48},{48,32},{64,80},{80,64},{96,112},{112,96},{1... | collective-permute-start | bytes 1572872 | tf_op jit(solution)/shard_map/ppermute | solution.py:360
  166.9 5.5 %all-to-all-start.5 = ((bf16[4,128,128]{2,1,0:T(8,128)(2,1)}), bf16[4,128,128]{2,1,0:T(8,128)(2,1)S(1)}, u32[]{:S(2)}, u32[]{:S(2)}) async-start(bf16[4,128,128]{2,1,0:T(8,128)(2,1)} %broadcast_in_dim.4), calls=%async_computation.5 | async-start | bytes 262144 | tf_op jit(solution)/shard_map/all_to_all | solution.py:416
  173.7 3.6 %all-to-all-done.5 = bf16[4,128,128]{2,1,0:T(8,128)(2,1)S(1)} async-done(((bf16[4,128,128]{2,1,0:T(8,128)(2,1)}), bf16[4,128,128]{2,1,0:T(8,128)(2,1)S(1)}, u32[]{:S(2)}, u32[]{:S(2)}) %all-to-all-start.5) | async-done | bytes 131104 | tf_op jit(solution)/shard_map/all_to_all | solution.py:416
  (55 shorter events, 23.8 us)
Async XLA Ops:
  2.8 5.2 %copy-start = (bf16[1,128,4096]{2,1,0:T(8,128)(2,1)S(1)}, bf16[1,128,4096]{2,1,0:T(8,128)(2,1)}, u32[]{:S(2)}) copy-start(bf16[1,128,4096]{2,1,0:T(8,128)(2,1)} %param.8) | copy-start | bytes 3145732
  2.9 16.3 %all-to-all-start = ((bf16[4,128,1280]{2,1,0:T(8,128)(2,1)}), bf16[4,128,1280]{2,1,0:T(8,128)(2,1)S(1)}, u32[]{:S(2)}, u32[]{:S(2)}) async-start(bf16[4,128,1280]{2,1,0:T(8,128)(2,1)} %shard_map.95), calls=%async_computation | async-start | bytes 2621440 | tf_op jit(solution)/shard_map/all_to_all | solution.py:347
  8.0 31.6 %collective-permute-start = (bf16[128,4096]{1,0:T(8,128)(2,1)S(1)}, bf16[128,4096]{1,0:T(8,128)(2,1)S(1)}, u32[]{:S(2)}, u32[]{:S(2)}) collective-permute-start(bf16[128,4096]{1,0:T(8,128)(2,1)S(1)} %bitcast.10), channel_id=1, source_target_pairs={{0,16},{16,0},{32,48},{48,32},{64,80},{80,64},{96,112},{112,96},{1... | collective-permute-start | bytes 3145736 | tf_op jit(solution)/shard_map/ppermute | solution.py:360
  20.4 1.0 copy-start.4
  21.4 12.1 %copy-start.10 = (s32[1,64]{1,0:T(1,128)S(1)}, s32[1,64]{1,0:T(1,128)}, u32[]{:S(2)}) copy-start(s32[1,64]{1,0:T(1,128)} %order.1) | copy-start | bytes 772
  21.4 18.3 %all-to-all-start.1 = ((bf16[4,512,256]{2,1,0:T(8,128)(2,1)}), bf16[4,512,256]{2,1,0:T(8,128)(2,1)S(1)}, u32[]{:S(2)}, u32[]{:S(2)}) async-start(bf16[4,512,256]{2,1,0:T(8,128)(2,1)} %copy-done.4), calls=%async_computation.1 | async-start | bytes 2097152 | tf_op jit(solution)/shard_map/all_to_all | solution.py:353
  25.5 28.2 %collective-permute-start.1 = (bf16[128,4096]{1,0:T(8,128)(2,1)}, bf16[128,4096]{1,0:T(8,128)(2,1)}, u32[]{:S(2)}, u32[]{:S(2)}) collective-permute-start(bf16[128,4096]{1,0:T(8,128)(2,1)} %bitcast.18), channel_id=1, source_target_pairs={{0,16},{16,0},{32,48},{48,32},{64,80},{80,64},{96,112},{112,96},{1... | collective-permute-start | bytes 3145736 | tf_op jit(solution)/shard_map/ppermute | solution.py:360
  33.8 31.2 %collective-permute-start.4 = (bf16[512,1024]{1,0:T(8,128)(2,1)}, bf16[512,1024]{1,0:T(8,128)(2,1)}, u32[]{:S(2)}, u32[]{:S(2)}) collective-permute-start(bf16[512,1024]{1,0:T(8,128)(2,1)} %get-tuple-element.23.w0), channel_id=1, source_target_pairs={{0,128},{16,48},{32,160},{48,80},{64,192},{80,112},{96,224},{112,1... | collective-permute-start | bytes 3145736 | tf_op jit(solution)/shard_map/ppermute | solution.py:335
  36.0 29.0 %collective-permute-start.3 = (bf16[512,1024]{1,0:T(8,128)(2,1)}, bf16[512,1024]{1,0:T(8,128)(2,1)}, u32[]{:S(2)}, u32[]{:S(2)}) collective-permute-start(bf16[512,1024]{1,0:T(8,128)(2,1)} %get-tuple-element.23.w0), channel_id=1, source_target_pairs={{0,256},{16,80},{32,288},{48,112},{64,320},{80,16},{96,352},{112,4... | collective-permute-start | bytes 3145736 | tf_op jit(solution)/shard_map/ppermute | solution.py:335
  40.2 8.0 %collective-permute-start.5 = (f32[128,256]{1,0:T(8,128)S(1)}, f32[128,256]{1,0:T(8,128)S(1)}, u32[]{:S(2)}, u32[]{:S(2)}) collective-permute-start(f32[128,256]{1,0:T(8,128)S(1)} %get-tuple-element.29), channel_id=1, source_target_pairs={{0,16},{16,0},{32,48},{48,32},{64,80},{80,64},{96,112},{112,96},{1... | collective-permute-start | bytes 393224 | tf_op jit(solution)/shard_map/ppermute | solution.py:360
  45.2 25.3 %collective-permute-start.2 = (bf16[512,1024]{1,0:T(8,128)(2,1)}, bf16[512,1024]{1,0:T(8,128)(2,1)}, u32[]{:S(2)}, u32[]{:S(2)}) collective-permute-start(bf16[512,1024]{1,0:T(8,128)(2,1)} %get-tuple-element.23.w0), channel_id=1, source_target_pairs={{0,384},{16,112},{32,416},{48,16},{64,448},{80,48},{96,480},{112,8... | collective-permute-start | bytes 3145736 | tf_op jit(solution)/shard_map/ppermute | solution.py:335
  48.4 1.0 copy-start.1
  49.4 27.8 %all-to-all-start.2 = ((bf16[16,128,256]{2,1,0:T(8,128)(2,1)}), bf16[16,128,256]{2,1,0:T(8,128)(2,1)}, u32[]{:S(2)}, u32[]{:S(2)}) async-start(bf16[16,128,256]{2,1,0:T(8,128)(2,1)} %copy-done.1), calls=%async_computation.2 | async-start | bytes 2097152 | tf_op jit(solution)/shard_map/all_to_all | solution.py:324
  65.0 1.2 copy-start.2
  70.5 15.5 %copy-start.11 = (s32[1,8]{1,0:T(1,128)S(1)}, s32[1,8]{1,0:T(1,128)}, u32[]{:S(2)}) copy-start(s32[1,8]{1,0:T(1,128)} %lengths.1) | copy-start | bytes 100
  72.8 0.8 copy-start.7
  73.6 0.8 copy-start.9
  77.2 8.8 %collective-permute-start.7 = (bf16[2048,256]{1,0:T(8,128)(2,1)}, bf16[2048,256]{1,0:T(8,128)(2,1)S(1)}, u32[]{:S(2)}, u32[]{:S(2)}) collective-permute-start(bf16[2048,256]{1,0:T(8,128)(2,1)} %bitcast.6.own_at), channel_id=1, source_target_pairs={{0,16},{16,0},{32,48},{48,32},{64,80},{80,64},{96,112},{112,96},{1... | collective-permute-start | bytes 3145736 | tf_op jit(solution)/shard_map/ppermute | solution.py:360
  82.0 4.0 %collective-permute-start.6 = (f32[128,1024]{1,0:T(8,128)}, f32[128,1024]{1,0:T(8,128)S(1)}, u32[]{:S(2)}, u32[]{:S(2)}) collective-permute-start(f32[128,1024]{1,0:T(8,128)} %copy-done.9), channel_id=1, source_target_pairs={{0,16},{16,0},{32,48},{48,32},{64,80},{80,64},{96,112},{112,96},{1... | collective-permute-start | bytes 1572872 | tf_op jit(solution)/shard_map/ppermute | solution.py:360
  86.0 1.0 copy-start.8
  93.5 4.6 %collective-permute-start.8 = (bf16[2048,256]{1,0:T(8,128)(2,1)S(1)}, bf16[2048,256]{1,0:T(8,128)(2,1)S(1)}, u32[]{:S(2)}, u32[]{:S(2)}) collective-permute-start(bf16[2048,256]{1,0:T(8,128)(2,1)S(1)} %get-tuple-element.34), channel_id=1, source_target_pairs={{0,16},{16,0},{32,48},{48,32},{64,80},{80,64},{96,112},{112,96},{1... | collective-permute-start | bytes 3145736 | tf_op jit(solution)/shard_map/ppermute | solution.py:360
  99.3 22.8 %all-to-all-start.3 = ((bf16[16,128,256]{2,1,0:T(8,128)(2,1)}), bf16[16,128,256]{2,1,0:T(8,128)(2,1)}, u32[]{:S(2)}, u32[]{:S(2)}) async-start(bf16[16,128,256]{2,1,0:T(8,128)(2,1)} %bitcast.21), calls=%async_computation.3 | async-start | bytes 2097152 | tf_op jit(solution)/shard_map/all_to_all | solution.py:324
  103.7 3.2 %collective-permute-start.9 = (bf16[128,512]{1,0:T(8,128)(2,1)S(1)}, bf16[128,512]{1,0:T(8,128)(2,1)S(1)}, u32[]{:S(2)}, u32[]{:S(2)}) collective-permute-start(bf16[128,512]{1,0:T(8,128)(2,1)S(1)} %get-tuple-element.35.grad_query), channel_id=1, source_target_pairs={{0,16},{16,0},{32,48},{48,32},{64,80},{80,64},{96,112},{112,96},{1... | collective-permute-start | bytes 393224 | tf_op jit(solution)/shard_map/ppermute | solution.py:360
  106.9 0.7 copy-start.5
  123.6 3.7 %collective-permute-start.10 = (bf16[128,256]{1,0:T(8,128)(2,1)S(1)}, bf16[128,256]{1,0:T(8,128)(2,1)S(1)}, u32[]{:S(2)}, u32[]{:S(2)}) collective-permute-start(bf16[128,256]{1,0:T(8,128)(2,1)S(1)} %shard_map.102.grads), channel_id=1, source_target_pairs={{0,16},{16,0},{32,48},{48,32},{64,80},{80,64},{96,112},{112,96},{1... | collective-permute-start | bytes 196616 | tf_op jit(solution)/shard_map/ppermute | solution.py:360
  127.8 0.8 copy-start.3
  128.6 14.6 %all-to-all-start.4 = ((bf16[16,128,128]{2,1,0:T(8,128)(2,1)}), bf16[16,128,128]{2,1,0:T(8,128)(2,1)S(1)}, u32[]{:S(2)}, u32[]{:S(2)}) async-start(bf16[16,128,128]{2,1,0:T(8,128)(2,1)} %copy-done.3), calls=%async_computation.4 | async-start | bytes 1048576 | tf_op jit(solution)/shard_map/all_to_all | solution.py:324
  132.2 0.9 copy-start.6
  143.3 13.5 %collective-permute-start.11 = (bf16[128,128]{1,0:T(8,128)(2,1)S(1)}, bf16[128,128]{1,0:T(8,128)(2,1)S(1)}, u32[]{:S(2)}, u32[]{:S(2)}) collective-permute-start(bf16[128,128]{1,0:T(8,128)(2,1)S(1)} %reduce_sum.21), channel_id=1, source_target_pairs={{0,8},{1,9},{2,10},{3,11},{4,12},{5,13},{6,14},{7,15},{8,0},{9,1},... | collective-permute-start | bytes 98312 | tf_op jit(solution)/shard_map/ppermute | solution.py:411
  156.8 9.5 %collective-permute-start.12 = (bf16[128,128]{1,0:T(8,128)(2,1)S(1)}, bf16[128,128]{1,0:T(8,128)(2,1)S(1)}, u32[]{:S(2)}, u32[]{:S(2)}) collective-permute-start(bf16[128,128]{1,0:T(8,128)(2,1)S(1)} %add_convert_fusion.2), channel_id=1, source_target_pairs={{0,4},{1,5},{2,6},{3,7},{4,0},{5,1},{6,2},{7,3},{8,12},{9,13},{10,... | collective-permute-start | bytes 98312 | tf_op jit(solution)/shard_map/ppermute | solution.py:411
  161.3 11.2 %collective-permute-start.13 = (bf16[128,2048]{1,0:T(8,128)(2,1)S(1)}, bf16[128,2048]{1,0:T(8,128)(2,1)S(1)}, u32[]{:S(2)}, u32[]{:S(2)}) collective-permute-start(bf16[128,2048]{1,0:T(8,128)(2,1)S(1)} %get-tuple-element.41), channel_id=1, source_target_pairs={{0,16},{16,0},{32,48},{48,32},{64,80},{80,64},{96,112},{112,96},{1... | collective-permute-start | bytes 1572872 | tf_op jit(solution)/shard_map/ppermute | solution.py:360
  166.9 10.3 %all-to-all-start.5 = ((bf16[4,128,128]{2,1,0:T(8,128)(2,1)}), bf16[4,128,128]{2,1,0:T(8,128)(2,1)S(1)}, u32[]{:S(2)}, u32[]{:S(2)}) async-start(bf16[4,128,128]{2,1,0:T(8,128)(2,1)} %broadcast_in_dim.4), calls=%async_computation.5 | async-start | bytes 262144 | tf_op jit(solution)/shard_map/all_to_all | solution.py:416

commit v6 on v5

--- a/solution.py
+++ b/solution.py
@@ -406,19 +406,22 @@
         2 * rows * features * (width + 2 * head))
     gathered, input_theirs = lax.optimization_barrier((to_chips(parts), input_theirs))
     grad_weight = jnp.sum(gathered.reshape(chips, rows, head).astype(F32), axis=0)
-    group, step = dp, dp // 2
+    group = dp
     while group > 4 and group % 2 == 0:
-        sent_on = lax.ppermute(grad_weight.astype(BF16), "dp", [(i, i ^ step) for i in range(dp)])
-        grad_weight = grad_weight.astype(BF16).astype(F32) + sent_on.astype(F32)
-        group, step = group // 2, step // 2
+        group //= 2
     near = [[first + i for i in range(group)] for first in range(0, dp, group)]
     spread = jnp.broadcast_to(grad_weight.astype(BF16)[None], (group, rows, head))
     gathered = lax.all_to_all(spread, "dp", 0, 0, tiled=True, axis_index_groups=near)
     (grad_input,) = call(
         merge_kernel, [shape((rows, features))], [SMEM] + [VMEM] * 2,
         (place, input_mine, swap(input_theirs)), 0)
-    gathered, grad_input = lax.optimization_barrier((gathered, grad_input))
     grad_weight = jnp.sum(gathered.reshape(group, rows, head).astype(F32), axis=0)
+    step = group
+    while step < dp:
+        received = lax.ppermute(grad_weight.astype(BF16), "dp", [(i, i ^ step) for i in range(dp)])
+        received, grad_input = lax.optimization_barrier((received, grad_input))
+        grad_weight = grad_weight.astype(BF16).astype(F32) + received.astype(F32)
+        step *= 2
     return grad_input[None], grad_weight
 
 

time: 179 us -> 181 us (1.011)
  the two profiles are of different devices: /device:TPU:1 before, /device:TPU:2 now
where the time goes in v6:
time: 181 us; the launch traced here: 180 us
  starting transfers between devices  80.3 us (44%)
  waiting for transfers between devices  55.8 us (31%)
  Pallas kernels  23.2 us (13%)
  blocking collectives  8.88 us (5%)
  local copies, waits for them, and re-layouts  8.3 us (5%)
  other arithmetic  2.6 us (1%)
    pallas_call x11, Pallas kernels, call(): pl.pallas_call(body, out_shape=outs, in_specs=in_specs, out_specs=out_spe...  23.2 us
    ppermute x2, starting transfers between devices, on_device(): lax.ppermute(grad_weight.astype(BF16), 'dp', [(i, i ^ step) for i in rang...  19.2 us
    all_to_all x3, waiting for transfers between devices, to_chips(): lax.all_to_all(pieces, 'ctx', 0, 0, tiled=True, axis_index_groups=planes)  19 us
    ppermute x9, starting transfers between devices, swap(): return lax.ppermute(v, 'ctx', other)  17.9 us
    all_to_all x3, starting transfers between devices, to_chips(): lax.all_to_all(pieces, 'ctx', 0, 0, tiled=True, axis_index_groups=planes)  17.9 us
    ppermute x3, waiting for transfers between devices, moved(): return lax.ppermute(v, 'ctx', pairs)  14.8 us
    ppermute x3, starting transfers between devices, moved(): return lax.ppermute(v, 'ctx', pairs)  12.1 us
    all_to_all x1, starting transfers between devices, on_device(): lax.all_to_all(packed, 'ctx', 0, 0, tiled=True, axis_index_groups=rings)  9.56 us
  transfers between devices with their start and end apart: 19, of which 12 were waited for; matrix products, arithmetic and copies ran while one was open for 0% of the time, Pallas kernels for 7%

profile of v6, /device:TPU:2, one launch (start us, length us, event | category | flops | bytes accessed | tf_op | source)
XLA Modules:
  0.0 180.1 jit_solution(11387940585922943280)
XLA Ops:
  0.6 2.2 %shard_map.95 = bf16[4,128,1280]{2,1,0:T(8,128)(2,1)} custom-call(bf16[128,512]{1,0:T(8,128)(2,1)} %query_weight.1, bf16[512,128]{1,0:T(8,128)(2,1)} %out_weight.1, bf16[128,128]{1,0:T(8,128)(2,1)} %key_weight.1, bf16[128,128]{1,0:T(8,128)(2,1)} %value_weight.1), custom_call_target="tpu_custom_call" | custom-call | bytes 1638400 | tf_op jit(solution)/shard_map/pallas_call | solution.py:27
  2.9 9.6 %all-to-all-start = ((bf16[4,128,1280]{2,1,0:T(8,128)(2,1)}), bf16[4,128,1280]{2,1,0:T(8,128)(2,1)S(1)}, u32[]{:S(2)}, u32[]{:S(2)}) async-start(bf16[4,128,1280]{2,1,0:T(8,128)(2,1)} %shard_map.95), calls=%async_computation | async-start | bytes 2621440 | tf_op jit(solution)/shard_map/all_to_all | solution.py:347
  12.4 1.9 %collective-permute-start = (bf16[128,4096]{1,0:T(8,128)(2,1)S(1)}, bf16[128,4096]{1,0:T(8,128)(2,1)S(1)}, u32[]{:S(2)}, u32[]{:S(2)}) collective-permute-start(bf16[128,4096]{1,0:T(8,128)(2,1)S(1)} %bitcast.10), channel_id=1, source_target_pairs={{0,16},{16,0},{32,48},{48,32},{64,80},{80,64},{96,112},{112,96},{1... | collective-permute-start | bytes 3145736 | tf_op jit(solution)/shard_map/ppermute | solution.py:360
  14.3 8.9 %all-to-all-done = bf16[4,128,1280]{2,1,0:T(8,128)(2,1)S(1)} async-done(((bf16[4,128,1280]{2,1,0:T(8,128)(2,1)}), bf16[4,128,1280]{2,1,0:T(8,128)(2,1)S(1)}, u32[]{:S(2)}, u32[]{:S(2)}) %all-to-all-start) | async-done | bytes 1310752 | tf_op jit(solution)/shard_map/all_to_all | solution.py:347
  25.5 3.6 %all-to-all-start.1 = ((bf16[4,512,256]{2,1,0:T(8,128)(2,1)}), bf16[4,512,256]{2,1,0:T(8,128)(2,1)S(1)}, u32[]{:S(2)}, u32[]{:S(2)}) async-start(bf16[4,512,256]{2,1,0:T(8,128)(2,1)} %copy-done.5), calls=%async_computation.1 | async-start | bytes 2097152 | tf_op jit(solution)/shard_map/all_to_all | solution.py:353
  29.2 1.9 %collective-permute-start.1 = (bf16[128,4096]{1,0:T(8,128)(2,1)}, bf16[128,4096]{1,0:T(8,128)(2,1)}, u32[]{:S(2)}, u32[]{:S(2)}) collective-permute-start(bf16[128,4096]{1,0:T(8,128)(2,1)} %bitcast.18), channel_id=1, source_target_pairs={{0,16},{16,0},{32,48},{48,32},{64,80},{80,64},{96,112},{112,96},{1... | collective-permute-start | bytes 3145736 | tf_op jit(solution)/shard_map/ppermute | solution.py:360
  31.3 3.9 %collective-permute-start.4 = (bf16[512,1024]{1,0:T(8,128)(2,1)}, bf16[512,1024]{1,0:T(8,128)(2,1)}, u32[]{:S(2)}, u32[]{:S(2)}) collective-permute-start(bf16[512,1024]{1,0:T(8,128)(2,1)} %get-tuple-element.25.w0), channel_id=1, source_target_pairs={{0,128},{16,48},{32,160},{48,80},{64,192},{80,112},{96,224},{112,1... | collective-permute-start | bytes 3145736 | tf_op jit(solution)/shard_map/ppermute | solution.py:335
  35.2 4.6 %collective-permute-start.3 = (bf16[512,1024]{1,0:T(8,128)(2,1)}, bf16[512,1024]{1,0:T(8,128)(2,1)}, u32[]{:S(2)}, u32[]{:S(2)}) collective-permute-start(bf16[512,1024]{1,0:T(8,128)(2,1)} %get-tuple-element.25.w0), channel_id=1, source_target_pairs={{0,256},{16,80},{32,288},{48,112},{64,320},{80,16},{96,352},{112,4... | collective-permute-start | bytes 3145736 | tf_op jit(solution)/shard_map/ppermute | solution.py:335
  40.6 1.9 %collective-permute-start.5 = (f32[128,256]{1,0:T(8,128)S(1)}, f32[128,256]{1,0:T(8,128)S(1)}, u32[]{:S(2)}, u32[]{:S(2)}) collective-permute-start(f32[128,256]{1,0:T(8,128)S(1)} %get-tuple-element.31), channel_id=1, source_target_pairs={{0,16},{16,0},{32,48},{48,32},{64,80},{80,64},{96,112},{112,96},{1... | collective-permute-start | bytes 393224 | tf_op jit(solution)/shard_map/ppermute | solution.py:360
  42.8 3.7 %collective-permute-start.2 = (bf16[512,1024]{1,0:T(8,128)(2,1)}, bf16[512,1024]{1,0:T(8,128)(2,1)}, u32[]{:S(2)}, u32[]{:S(2)}) collective-permute-start(bf16[512,1024]{1,0:T(8,128)(2,1)} %get-tuple-element.25.w0), channel_id=1, source_target_pairs={{0,384},{16,112},{32,416},{48,16},{64,448},{80,48},{96,480},{112,8... | collective-permute-start | bytes 3145736 | tf_op jit(solution)/shard_map/ppermute | solution.py:335
  47.8 5.0 %all-to-all-start.2 = ((bf16[16,128,256]{2,1,0:T(8,128)(2,1)}), bf16[16,128,256]{2,1,0:T(8,128)(2,1)}, u32[]{:S(2)}, u32[]{:S(2)}) async-start(bf16[16,128,256]{2,1,0:T(8,128)(2,1)} %copy-done.1), calls=%async_computation.2 | async-start | bytes 2097152 | tf_op jit(solution)/shard_map/all_to_all | solution.py:324
  52.8 14.8 %collective-permute-done.3.w1 = bf16[512,1024]{1,0:T(8,128)(2,1)} collective-permute-done((bf16[512,1024]{1,0:T(8,128)(2,1)}, bf16[512,1024]{1,0:T(8,128)(2,1)}, u32[]{:S(2)}, u32[]{:S(2)}) %collective-permute-start.3) | collective-permute-done | bytes 1048608 | tf_op jit(solution)/shard_map/ppermute | solution.py:335
  68.8 3.3 %shard_map.97 = (f32[128,1024]{1,0:T(8,128)S(1)}, f32[128,1024]{1,0:T(8,128)S(1)}) custom-call(s32[1]{0:T(128)} %bitcast.place, bf16[128,4096]{1,0:T(8,128)(2,1)S(1)} %bitcast.12, bf16[128,4096]{1,0:T(8,128)(2,1)S(1)} %bitcast.19, bf16[128,4096]{1,0:T(8,128)(2,1)S(1)} %collective-permute-done.other_tokens, ...), custom_call_target="tpu_custom_call" | custom-call | flops 805306368 | bytes 8388612 | tf_op jit(solution)/shard_map/pallas_call | solution.py:27
  72.2 2.2 %shard_map.98 = (f32[128,1024]{1,0:T(8,128)S(1)}, f32[128,1024]{1,0:T(8,128)S(1)}) custom-call(s32[1]{0:T(128)} %bitcast.place, bf16[128,4096]{1,0:T(8,128)(2,1)S(1)} %bitcast.13, bf16[128,4096]{1,0:T(8,128)(2,1)S(1)} %bitcast.20, bf16[128,4096]{1,0:T(8,128)(2,1)S(1)} %collective-permute-done.other_tokens, ...), custom_call_target="tpu_custom_call" | custom-call | flops 268435456 | bytes 7340036 | tf_op jit(solution)/shard_map/pallas_call | solution.py:27
  76.1 2.4 %collective-permute-start.7 = (bf16[2048,256]{1,0:T(8,128)(2,1)}, bf16[2048,256]{1,0:T(8,128)(2,1)S(1)}, u32[]{:S(2)}, u32[]{:S(2)}) collective-permute-start(bf16[2048,256]{1,0:T(8,128)(2,1)} %bitcast.6.own_at), channel_id=1, source_target_pairs={{0,16},{16,0},{32,48},{48,32},{64,80},{80,64},{96,112},{112,96},{1... | collective-permute-start | bytes 3145736 | tf_op jit(solution)/shard_map/ppermute | solution.py:360
  78.5 1.9 %collective-permute-start.6 = (f32[128,1024]{1,0:T(8,128)}, f32[128,1024]{1,0:T(8,128)S(1)}, u32[]{:S(2)}, u32[]{:S(2)}) collective-permute-start(f32[128,1024]{1,0:T(8,128)} %copy-done.10), channel_id=1, source_target_pairs={{0,16},{16,0},{32,48},{48,32},{64,80},{80,64},{96,112},{112,96},{1... | collective-permute-start | bytes 1572872 | tf_op jit(solution)/shard_map/ppermute | solution.py:360
  80.4 2.1 %collective-permute-done.6.theirs_at = f32[128,1024]{1,0:T(8,128)S(1)} collective-permute-done((f32[128,1024]{1,0:T(8,128)}, f32[128,1024]{1,0:T(8,128)S(1)}, u32[]{:S(2)}, u32[]{:S(2)}) %collective-permute-start.6) | collective-permute-done | bytes 524320 | tf_op jit(solution)/shard_map/ppermute | solution.py:360
  83.6 6.4 %shard_map.101 = (bf16[128,512]{1,0:T(8,128)(2,1)S(1)}, bf16[2048,256]{1,0:T(8,128)(2,1)S(1)}, bf16[2048,256]{1,0:T(8,128)(2,1)S(1)}) custom-call(s32[1]{0:T(128)} %bitcast.place, s32[1,64]{1,0:T(1,128)S(1)} %copy-done.11, s32[1,8]{1,0:T(1,128)S(1)} %copy-done.12, f32[128,1024]{1,0:T(8,128)S(1)} %copy-done.9, ...), custom_call_target="tpu_custom_call" | custom-call | flops 1426063360 | bytes 5505316 | tf_op jit(solution)/shard_map/pallas_call | solution.py:27
  90.0 2.0 %collective-permute-start.8 = (bf16[2048,256]{1,0:T(8,128)(2,1)S(1)}, bf16[2048,256]{1,0:T(8,128)(2,1)S(1)}, u32[]{:S(2)}, u32[]{:S(2)}) collective-permute-start(bf16[2048,256]{1,0:T(8,128)(2,1)S(1)} %get-tuple-element.36), channel_id=1, source_target_pairs={{0,16},{16,0},{32,48},{48,32},{64,80},{80,64},{96,112},{112,96},{1... | collective-permute-start | bytes 3145736 | tf_op jit(solution)/shard_map/ppermute | solution.py:360
  92.0 2.5 %collective-permute-done.8 = bf16[2048,256]{1,0:T(8,128)(2,1)S(1)} collective-permute-done((bf16[2048,256]{1,0:T(8,128)(2,1)S(1)}, bf16[2048,256]{1,0:T(8,128)(2,1)S(1)}, u32[]{:S(2)}, u32[]{:S(2)}) %collective-permute-start.8) | collective-permute-done | bytes 1048608 | tf_op jit(solution)/shard_map/ppermute | solution.py:360
  95.8 6.8 %all-to-all-start.3 = ((bf16[16,128,256]{2,1,0:T(8,128)(2,1)}), bf16[16,128,256]{2,1,0:T(8,128)(2,1)}, u32[]{:S(2)}, u32[]{:S(2)}) async-start(bf16[16,128,256]{2,1,0:T(8,128)(2,1)} %bitcast.21), calls=%async_computation.3 | async-start | bytes 2097152 | tf_op jit(solution)/shard_map/all_to_all | solution.py:324
  102.6 2.0 %collective-permute-start.9 = (bf16[128,512]{1,0:T(8,128)(2,1)S(1)}, bf16[128,512]{1,0:T(8,128)(2,1)S(1)}, u32[]{:S(2)}, u32[]{:S(2)}) collective-permute-start(bf16[128,512]{1,0:T(8,128)(2,1)S(1)} %get-tuple-element.37.grad_query), channel_id=1, source_target_pairs={{0,16},{16,0},{32,48},{48,32},{64,80},{80,64},{96,112},{112,96},{1... | collective-permute-start | bytes 393224 | tf_op jit(solution)/shard_map/ppermute | solution.py:360
  106.5 13.0 %all-to-all-done.3.pieces = bf16[16,128,256]{2,1,0:T(8,128)(2,1)} async-done(((bf16[16,128,256]{2,1,0:T(8,128)(2,1)}), bf16[16,128,256]{2,1,0:T(8,128)(2,1)}, u32[]{:S(2)}, u32[]{:S(2)}) %all-to-all-start.3) | async-done | bytes 1048608 | tf_op jit(solution)/shard_map/all_to_all | solution.py:324
  125.3 6.1 %all-to-all-start.4 = ((bf16[16,128,128]{2,1,0:T(8,128)(2,1)}), bf16[16,128,128]{2,1,0:T(8,128)(2,1)S(1)}, u32[]{:S(2)}, u32[]{:S(2)}) async-start(bf16[16,128,128]{2,1,0:T(8,128)(2,1)} %copy-done.4), calls=%async_computation.4 | async-start | bytes 1048576 | tf_op jit(solution)/shard_map/all_to_all | solution.py:324
  132.3 4.0 %shard_map.104 = (bf16[128,2048]{1,0:T(8,128)(2,1)S(1)}, bf16[128,2048]{1,0:T(8,128)(2,1)S(1)}) custom-call(s32[1]{0:T(128)} %bitcast.place, bf16[128,512]{1,0:T(8,128)(2,1)S(1)} %get-tuple-element.37.grad_query, bf16[128,512]{1,0:T(8,128)(2,1)S(1)} %copy-done.7, bf16[128,256]{1,0:T(8,128)(2,1)S(1)} %shard_map.102.grads, ...), custom_call_target="tpu_custom_call" | custom-call | flops 805306368 | bytes 6684676 | tf_op jit(solution)/shard_map/pallas_call | solution.py:27
  136.3 5.9 %all-to-all-done.4 = bf16[16,128,128]{2,1,0:T(8,128)(2,1)S(1)} async-done(((bf16[16,128,128]{2,1,0:T(8,128)(2,1)}), bf16[16,128,128]{2,1,0:T(8,128)(2,1)S(1)}, u32[]{:S(2)}, u32[]{:S(2)}) %all-to-all-start.4) | async-done | bytes 524320 | tf_op jit(solution)/shard_map/all_to_all | solution.py:324
  142.2 1.9 %collective-permute-start.12 = (bf16[128,2048]{1,0:T(8,128)(2,1)S(1)}, bf16[128,2048]{1,0:T(8,128)(2,1)S(1)}, u32[]{:S(2)}, u32[]{:S(2)}) collective-permute-start(bf16[128,2048]{1,0:T(8,128)(2,1)S(1)} %get-tuple-element.43), channel_id=1, source_target_pairs={{0,16},{16,0},{32,48},{48,32},{64,80},{80,64},{96,112},{112,96},{1... | collective-permute-start | bytes 1572872 | tf_op jit(solution)/shard_map/ppermute | solution.py:360
  144.3 8.9 %all_to_all.34 = bf16[4,128,128]{2,1,0:T(8,128)(2,1)S(1)} all-to-all(bf16[4,128,128]{2,1,0:T(8,128)(2,1)S(1)} %broadcast_in_dim.4), channel_id=1, replica_groups={{0,1,2,3},{4,5,6,7},{8,9,10,11},{12,13,14,15},{16,17,18,19},{20,21,22,2..., dimensions={0} | all-to-all | bytes 262144 | tf_op jit(solution)/shard_map/all_to_all | solution.py:414
  153.2 8.1 %collective-permute-start.11 = (bf16[128,128]{1,0:T(8,128)(2,1)S(1)}, bf16[128,128]{1,0:T(8,128)(2,1)S(1)}, u32[]{:S(2)}, u32[]{:S(2)}) collective-permute-start(bf16[128,128]{1,0:T(8,128)(2,1)S(1)} %reduce_sum.25), channel_id=1, source_target_pairs={{0,4},{1,5},{2,6},{3,7},{4,0},{5,1},{6,2},{7,3},{8,12},{9,13},{10,... | collective-permute-start | bytes 98312 | tf_op jit(solution)/shard_map/ppermute | solution.py:421
  162.5 2.1 %collective-permute-done.11 = bf16[128,128]{1,0:T(8,128)(2,1)S(1)} collective-permute-done((bf16[128,128]{1,0:T(8,128)(2,1)S(1)}, bf16[128,128]{1,0:T(8,128)(2,1)S(1)}, u32[]{:S(2)}, u32[]{:S(2)}) %collective-permute-start.11) | collective-permute-done | bytes 32800 | tf_op jit(solution)/shard_map/ppermute | solution.py:421
  164.6 11.1 %collective-permute-start.13 = (bf16[128,128]{1,0:T(8,128)(2,1)S(1)}, bf16[128,128]{1,0:T(8,128)(2,1)S(1)}, u32[]{:S(2)}, u32[]{:S(2)}) collective-permute-start(bf16[128,128]{1,0:T(8,128)(2,1)S(1)} %add_convert_fusion.1), channel_id=1, source_target_pairs={{0,8},{1,9},{2,10},{3,11},{4,12},{5,13},{6,14},{7,15},{8,0},{9,1},... | collective-permute-start | bytes 98312 | tf_op jit(solution)/shard_map/ppermute | solution.py:421
  175.7 3.8 %collective-permute-done.13 = bf16[128,128]{1,0:T(8,128)(2,1)S(1)} collective-permute-done((bf16[128,128]{1,0:T(8,128)(2,1)S(1)}, bf16[128,128]{1,0:T(8,128)(2,1)S(1)}, u32[]{:S(2)}, u32[]{:S(2)}) %collective-permute-start.13) | collective-permute-done | bytes 32800 | tf_op jit(solution)/shard_map/ppermute | solution.py:421
  (56 shorter events, 20.7 us)
Async XLA Ops:
  2.9 9.6 %copy-start = (bf16[1,128,4096]{2,1,0:T(8,128)(2,1)S(1)}, bf16[1,128,4096]{2,1,0:T(8,128)(2,1)}, u32[]{:S(2)}) copy-start(bf16[1,128,4096]{2,1,0:T(8,128)(2,1)} %param.8) | copy-start | bytes 3145732
  2.9 20.4 %all-to-all-start = ((bf16[4,128,1280]{2,1,0:T(8,128)(2,1)}), bf16[4,128,1280]{2,1,0:T(8,128)(2,1)S(1)}, u32[]{:S(2)}, u32[]{:S(2)}) async-start(bf16[4,128,1280]{2,1,0:T(8,128)(2,1)} %shard_map.95), calls=%async_computation | async-start | bytes 2621440 | tf_op jit(solution)/shard_map/all_to_all | solution.py:347
  12.4 27.4 %collective-permute-start = (bf16[128,4096]{1,0:T(8,128)(2,1)S(1)}, bf16[128,4096]{1,0:T(8,128)(2,1)S(1)}, u32[]{:S(2)}, u32[]{:S(2)}) collective-permute-start(bf16[128,4096]{1,0:T(8,128)(2,1)S(1)} %bitcast.10), channel_id=1, source_target_pairs={{0,16},{16,0},{32,48},{48,32},{64,80},{80,64},{96,112},{112,96},{1... | collective-permute-start | bytes 3145736 | tf_op jit(solution)/shard_map/ppermute | solution.py:360
  24.5 1.0 copy-start.5
  25.5 5.6 %copy-start.11 = (s32[1,64]{1,0:T(1,128)S(1)}, s32[1,64]{1,0:T(1,128)}, u32[]{:S(2)}) copy-start(s32[1,64]{1,0:T(1,128)} %order.1) | copy-start | bytes 772
  25.5 14.6 %all-to-all-start.1 = ((bf16[4,512,256]{2,1,0:T(8,128)(2,1)}), bf16[4,512,256]{2,1,0:T(8,128)(2,1)S(1)}, u32[]{:S(2)}, u32[]{:S(2)}) async-start(bf16[4,512,256]{2,1,0:T(8,128)(2,1)} %copy-done.5), calls=%async_computation.1 | async-start | bytes 2097152 | tf_op jit(solution)/shard_map/all_to_all | solution.py:353
  29.2 23.6 %collective-permute-start.1 = (bf16[128,4096]{1,0:T(8,128)(2,1)}, bf16[128,4096]{1,0:T(8,128)(2,1)}, u32[]{:S(2)}, u32[]{:S(2)}) collective-permute-start(bf16[128,4096]{1,0:T(8,128)(2,1)} %bitcast.18), channel_id=1, source_target_pairs={{0,16},{16,0},{32,48},{48,32},{64,80},{80,64},{96,112},{112,96},{1... | collective-permute-start | bytes 3145736 | tf_op jit(solution)/shard_map/ppermute | solution.py:360
  31.3 21.5 %collective-permute-start.4 = (bf16[512,1024]{1,0:T(8,128)(2,1)}, bf16[512,1024]{1,0:T(8,128)(2,1)}, u32[]{:S(2)}, u32[]{:S(2)}) collective-permute-start(bf16[512,1024]{1,0:T(8,128)(2,1)} %get-tuple-element.25.w0), channel_id=1, source_target_pairs={{0,128},{16,48},{32,160},{48,80},{64,192},{80,112},{96,224},{112,1... | collective-permute-start | bytes 3145736 | tf_op jit(solution)/shard_map/ppermute | solution.py:335
  35.2 32.4 %collective-permute-start.3 = (bf16[512,1024]{1,0:T(8,128)(2,1)}, bf16[512,1024]{1,0:T(8,128)(2,1)}, u32[]{:S(2)}, u32[]{:S(2)}) collective-permute-start(bf16[512,1024]{1,0:T(8,128)(2,1)} %get-tuple-element.25.w0), channel_id=1, source_target_pairs={{0,256},{16,80},{32,288},{48,112},{64,320},{80,16},{96,352},{112,4... | collective-permute-start | bytes 3145736 | tf_op jit(solution)/shard_map/ppermute | solution.py:335
  40.6 6.0 %collective-permute-start.5 = (f32[128,256]{1,0:T(8,128)S(1)}, f32[128,256]{1,0:T(8,128)S(1)}, u32[]{:S(2)}, u32[]{:S(2)}) collective-permute-start(f32[128,256]{1,0:T(8,128)S(1)} %get-tuple-element.31), channel_id=1, source_target_pairs={{0,16},{16,0},{32,48},{48,32},{64,80},{80,64},{96,112},{112,96},{1... | collective-permute-start | bytes 393224 | tf_op jit(solution)/shard_map/ppermute | solution.py:360
  42.8 29.3 %collective-permute-start.2 = (bf16[512,1024]{1,0:T(8,128)(2,1)}, bf16[512,1024]{1,0:T(8,128)(2,1)}, u32[]{:S(2)}, u32[]{:S(2)}) collective-permute-start(bf16[512,1024]{1,0:T(8,128)(2,1)} %get-tuple-element.25.w0), channel_id=1, source_target_pairs={{0,384},{16,112},{32,416},{48,16},{64,448},{80,48},{96,480},{112,8... | collective-permute-start | bytes 3145736 | tf_op jit(solution)/shard_map/ppermute | solution.py:335
  46.8 1.0 copy-start.1
  47.8 28.3 %all-to-all-start.2 = ((bf16[16,128,256]{2,1,0:T(8,128)(2,1)}), bf16[16,128,256]{2,1,0:T(8,128)(2,1)}, u32[]{:S(2)}, u32[]{:S(2)}) async-start(bf16[16,128,256]{2,1,0:T(8,128)(2,1)} %copy-done.1), calls=%async_computation.2 | async-start | bytes 2097152 | tf_op jit(solution)/shard_map/all_to_all | solution.py:324
  67.6 1.2 copy-start.2
  68.8 3.3 %copy-start.3 = (bf16[1,128,4096]{2,1,0:T(8,128)(2,1)S(1)}, bf16[1,128,4096]{2,1,0:T(8,128)(2,1)}, u32[]{:S(2)}) copy-start(bf16[1,128,4096]{2,1,0:T(8,128)(2,1)} %param.9) | copy-start | bytes 3145732
  72.1 10.4 %copy-start.12 = (s32[1,8]{1,0:T(1,128)S(1)}, s32[1,8]{1,0:T(1,128)}, u32[]{:S(2)}) copy-start(s32[1,8]{1,0:T(1,128)} %lengths.1) | copy-start | bytes 100
  74.4 0.8 copy-start.8
  75.2 0.8 copy-start.10
  76.1 6.4 %collective-permute-start.7 = (bf16[2048,256]{1,0:T(8,128)(2,1)}, bf16[2048,256]{1,0:T(8,128)(2,1)S(1)}, u32[]{:S(2)}, u32[]{:S(2)}) collective-permute-start(bf16[2048,256]{1,0:T(8,128)(2,1)} %bitcast.6.own_at), channel_id=1, source_target_pairs={{0,16},{16,0},{32,48},{48,32},{64,80},{80,64},{96,112},{112,96},{1... | collective-permute-start | bytes 3145736 | tf_op jit(solution)/shard_map/ppermute | solution.py:360
  78.5 4.0 %collective-permute-start.6 = (f32[128,1024]{1,0:T(8,128)}, f32[128,1024]{1,0:T(8,128)S(1)}, u32[]{:S(2)}, u32[]{:S(2)}) collective-permute-start(f32[128,1024]{1,0:T(8,128)} %copy-done.10), channel_id=1, source_target_pairs={{0,16},{16,0},{32,48},{48,32},{64,80},{80,64},{96,112},{112,96},{1... | collective-permute-start | bytes 1572872 | tf_op jit(solution)/shard_map/ppermute | solution.py:360
  82.5 1.0 copy-start.9
  90.0 4.6 %collective-permute-start.8 = (bf16[2048,256]{1,0:T(8,128)(2,1)S(1)}, bf16[2048,256]{1,0:T(8,128)(2,1)S(1)}, u32[]{:S(2)}, u32[]{:S(2)}) collective-permute-start(bf16[2048,256]{1,0:T(8,128)(2,1)S(1)} %get-tuple-element.36), channel_id=1, source_target_pairs={{0,16},{16,0},{32,48},{48,32},{64,80},{80,64},{96,112},{112,96},{1... | collective-permute-start | bytes 3145736 | tf_op jit(solution)/shard_map/ppermute | solution.py:360
  95.8 23.6 %all-to-all-start.3 = ((bf16[16,128,256]{2,1,0:T(8,128)(2,1)}), bf16[16,128,256]{2,1,0:T(8,128)(2,1)}, u32[]{:S(2)}, u32[]{:S(2)}) async-start(bf16[16,128,256]{2,1,0:T(8,128)(2,1)} %bitcast.21), calls=%async_computation.3 | async-start | bytes 2097152 | tf_op jit(solution)/shard_map/all_to_all | solution.py:324
  102.6 3.2 %collective-permute-start.9 = (bf16[128,512]{1,0:T(8,128)(2,1)S(1)}, bf16[128,512]{1,0:T(8,128)(2,1)S(1)}, u32[]{:S(2)}, u32[]{:S(2)}) collective-permute-start(bf16[128,512]{1,0:T(8,128)(2,1)S(1)} %get-tuple-element.37.grad_query), channel_id=1, source_target_pairs={{0,16},{16,0},{32,48},{48,32},{64,80},{80,64},{96,112},{112,96},{1... | collective-permute-start | bytes 393224 | tf_op jit(solution)/shard_map/ppermute | solution.py:360
  105.8 0.7 copy-start.6
  120.9 3.1 %collective-permute-start.10 = (bf16[128,256]{1,0:T(8,128)(2,1)S(1)}, bf16[128,256]{1,0:T(8,128)(2,1)S(1)}, u32[]{:S(2)}, u32[]{:S(2)}) collective-permute-start(bf16[128,256]{1,0:T(8,128)(2,1)S(1)} %shard_map.102.grads), channel_id=1, source_target_pairs={{0,16},{16,0},{32,48},{48,32},{64,80},{80,64},{96,112},{112,96},{1... | collective-permute-start | bytes 196616 | tf_op jit(solution)/shard_map/ppermute | solution.py:360
  124.5 0.8 copy-start.4
  125.3 17.0 %all-to-all-start.4 = ((bf16[16,128,128]{2,1,0:T(8,128)(2,1)}), bf16[16,128,128]{2,1,0:T(8,128)(2,1)S(1)}, u32[]{:S(2)}, u32[]{:S(2)}) async-start(bf16[16,128,128]{2,1,0:T(8,128)(2,1)} %copy-done.4), calls=%async_computation.4 | async-start | bytes 1048576 | tf_op jit(solution)/shard_map/all_to_all | solution.py:324
  131.4 0.9 copy-start.7
  142.2 19.0 %collective-permute-start.12 = (bf16[128,2048]{1,0:T(8,128)(2,1)S(1)}, bf16[128,2048]{1,0:T(8,128)(2,1)S(1)}, u32[]{:S(2)}, u32[]{:S(2)}) collective-permute-start(bf16[128,2048]{1,0:T(8,128)(2,1)S(1)} %get-tuple-element.43), channel_id=1, source_target_pairs={{0,16},{16,0},{32,48},{48,32},{64,80},{80,64},{96,112},{112,96},{1... | collective-permute-start | bytes 1572872 | tf_op jit(solution)/shard_map/ppermute | solution.py:360
  153.2 11.4 %collective-permute-start.11 = (bf16[128,128]{1,0:T(8,128)(2,1)S(1)}, bf16[128,128]{1,0:T(8,128)(2,1)S(1)}, u32[]{:S(2)}, u32[]{:S(2)}) collective-permute-start(bf16[128,128]{1,0:T(8,128)(2,1)S(1)} %reduce_sum.25), channel_id=1, source_target_pairs={{0,4},{1,5},{2,6},{3,7},{4,0},{5,1},{6,2},{7,3},{8,12},{9,13},{10,... | collective-permute-start | bytes 98312 | tf_op jit(solution)/shard_map/ppermute | solution.py:421
  164.6 14.9 %collective-permute-start.13 = (bf16[128,128]{1,0:T(8,128)(2,1)S(1)}, bf16[128,128]{1,0:T(8,128)(2,1)S(1)}, u32[]{:S(2)}, u32[]{:S(2)}) collective-permute-start(bf16[128,128]{1,0:T(8,128)(2,1)S(1)} %add_convert_fusion.1), channel_id=1, source_target_pairs={{0,8},{1,9},{2,10},{3,11},{4,12},{5,13},{6,14},{7,15},{8,0},{9,1},... | collective-permute-start | bytes 98312 | tf_op jit(solution)/shard_map/ppermute | solution.py:421
